TPU v7x, 32 devices: a whole 2x2x4 slice. The times are simulated.
32 devices in a mesh: space: 16 (over z, y, x), members: 2 (over core).
Axes of the slice: x: 2, y: 2, z: 4, core: 2. Of those that a mesh axis runs over, the one named last changes fastest.
Arguments:
- log_field: float32 [128, 2048], P('members', 'space'), may hold values from -6 to 6
- obs_heads: float32 [512], P('space'), may hold values from -6 to 6
- obs_var: float32 [512], P('space'), may hold values from 0.05 to 0.5
- obs_noise: float32 [128, 512], P('members', 'space'), may hold values from -6 to 6
- obs_index: int32 [16, 32], P('space'), may hold values from 0 to 127
- obs_count: int32 [16], P('space'), may hold values from 1 to 32, 256 in all
- neighbours: int32 [128, 64], P('members'), may hold values from 0 to 127, all different within a row
- lift_gain: float32 [48], replicated, may hold values from -4 to 4
- lift_bias: float32 [48], replicated, may hold values from -3 to 3
- conv_first: bfloat16 [3, 48, 48], replicated, may hold values from -0.5 to 0.5
- bias_first: float32 [48], replicated, may hold values from -2 to 2
- conv_second: bfloat16 [3, 48, 96], replicated, may hold values from -0.375 to 0.375
- bias_second: float32 [48], replicated, may hold values from -2 to 2
- readout: bfloat16 [144], replicated, may hold values from -0.5 to 0.5
Outputs:
- updated_field: float32 [128, 2048], P('members', 'space')
- new_heads: float32 [128, 2048], P('members', 'space')
Inputs may be any that keep to these rules, and one draw needn't show every extreme that they name: `obs_index`: cells are counted within the tile that holds the slot. `obs_count`: the counts sum to 256 and the largest is exactly 32. `neighbours`: each row names 64 different members; every member is named by some row.
All inputs are finite; a program needn't handle non-finite values. No bound on the sum of `obs_count` on one device may be relied on, other than what follows from the above.
Results may differ from a plain program's by a relative error of at most 0.0051.
Values may be sent and summed in bfloat16 or wider, within the bound.
No kernel may reach another device: no remote copies, remote signals or barrier semaphores. Data moves between devices by JAX's collectives and lax.ppermute only.
A program may use at most 64 MiB of HBM per device.

v0:
```python
import jax
import jax.numpy as jnp
from jax import lax
from jax.sharding import PartitionSpec as P


def padded(block, sides, width):
    for axis, dim in sides:
        count = lax.axis_size(axis)
        forward = [(i, i + 1) for i in range(count - 1)]
        backward = [(target, source) for source, target in forward]
        low = lax.ppermute(
            lax.slice_in_dim(block, block.shape[dim] - width, None, axis=dim), axis, forward
        )
        high = lax.ppermute(lax.slice_in_dim(block, 0, width, axis=dim), axis, backward)
        block = jnp.concatenate([low, block, high], axis=dim)
    return block


def dilated_conv(padded_input, kernel_taps, kernel_bias, dilation, width_cells):
    total_sum = None
    for kernel_tap in range(3):
        window_cells = lax.slice_in_dim(
            padded_input, kernel_tap * dilation, kernel_tap * dilation + width_cells, axis=2
        )
        term_value = jnp.einsum(
            "oc,cmn->omn", kernel_taps[kernel_tap], window_cells, preferred_element_type=jnp.float32
        )
        total_sum = term_value if total_sum is None else total_sum + term_value
    return jax.nn.silu(total_sum + kernel_bias[:, None, None])


def read_heads(readout, first_layer, second_layer, third_layer):
    channels = first_layer.shape[0]
    result = jnp.einsum(
        "c,cmn->mn", readout[:channels], first_layer, preferred_element_type=jnp.float32
    )
    result = result + jnp.einsum(
        "c,cmn->mn",
        readout[channels : 2 * channels],
        second_layer,
        preferred_element_type=jnp.float32,
    )
    return result + jnp.einsum(
        "c,cmn->mn", readout[2 * channels :], third_layer, preferred_element_type=jnp.float32
    )


def local_surrogate(
    log_values, lift_gain, lift_bias, conv_first, bias_first, conv_second, bias_second, readout
):
    cells_here = log_values.shape[1]
    first_layer = jnp.tanh(
        lift_gain[:, None, None] * log_values[None] + lift_bias[:, None, None]
    ).astype(jnp.bfloat16)
    padded_first = padded(first_layer, (("space", 2),), 1)
    second_layer = dilated_conv(padded_first, conv_first, bias_first, 1, cells_here).astype(
        jnp.bfloat16
    )
    joined_layers = jnp.concatenate([first_layer, second_layer], axis=0)
    padded_joined = padded(joined_layers, (("space", 2),), 2)
    third_layer = dilated_conv(padded_joined, conv_second, bias_second, 2, cells_here).astype(
        jnp.bfloat16
    )
    return read_heads(readout, first_layer, second_layer, third_layer)


def gram_terms(neighbour_rows, innov_rows, obs_weight):
    anomaly = neighbour_rows - jnp.mean(neighbour_rows, axis=1, keepdims=True)
    scaled = anomaly * obs_weight
    gram = jnp.einsum("bko,blo->bkl", scaled, anomaly, precision=lax.Precision.HIGHEST)
    rhs = jnp.einsum("bko,bo->bk", scaled, innov_rows, precision=lax.Precision.HIGHEST)
    return (gram, rhs)


def solve_weights(gram, rhs):
    order = gram.shape[-1]
    system = gram + (order - 1.0) * jnp.eye(order, dtype=jnp.float32)
    factor = jnp.linalg.cholesky(system)
    half_solved = jax.scipy.linalg.solve_triangular(factor, rhs[..., None], lower=True)
    solved = jax.scipy.linalg.solve_triangular(factor, half_solved, lower=True, trans=1)[..., 0]
    return solved - jnp.mean(solved, axis=-1, keepdims=True)


def on_device(
    log_field,
    obs_heads,
    obs_var,
    obs_noise,
    obs_index,
    obs_count,
    neighbours,
    lift_gain,
    lift_bias,
    conv_first,
    bias_first,
    conv_second,
    bias_second,
    readout,
):
    heads = local_surrogate(
        log_field, lift_gain, lift_bias, conv_first, bias_first, conv_second, bias_second, readout
    )
    own_obs = jnp.take(heads, obs_index[0], axis=1)
    live_slots = jnp.arange(obs_var.shape[0], dtype=jnp.int32) < obs_count[0]
    obs_weight = jnp.where(live_slots, 1.0 / obs_var, 0.0)
    innovation = obs_heads[None, :] + jnp.sqrt(obs_var)[None, :] * obs_noise - own_obs
    panel = lax.all_gather(own_obs, "members", axis=0, tiled=True)
    local_members = log_field.shape[0]
    gram, rhs = gram_terms(jnp.take(panel, neighbours, axis=0), innovation, obs_weight)
    gram, rhs = lax.psum((gram, rhs), "space")
    coef = solve_weights(gram, rhs)
    row_ids = jnp.arange(local_members, dtype=jnp.int32)[:, None]
    mixing = (
        jnp.zeros((local_members, panel.shape[0]), jnp.float32).at[row_ids, neighbours].add(coef)
    )
    updated_field = log_field + jnp.dot(
        mixing,
        lax.all_gather(log_field, "members", axis=0, tiled=True),
        precision=lax.Precision.HIGHEST,
    )
    new_heads = local_surrogate(
        updated_field,
        lift_gain,
        lift_bias,
        conv_first,
        bias_first,
        conv_second,
        bias_second,
        readout,
    )
    return (updated_field, new_heads)


def solution(mesh):
    in_specs = (
        P("members", "space"),
        P("space"),
        P("space"),
        P("members", "space"),
        P("space", None),
        P("space"),
        P("members", None),
        P(),
        P(),
        P(),
        P(),
        P(),
        P(),
        P(),
    )
    out_specs = (P("members", "space"), P("members", "space"))
    return jax.shard_map(
        on_device, mesh=mesh, in_specs=in_specs, out_specs=out_specs, check_vma=False
    )
```

profile of v0, /device:TPU:0, one launch (start us, length us, event | category | flops | bytes accessed | tf_op | source)
XLA Modules:
  0.0 743.3 jit_solution(11877593431523016333)
XLA Ops:
  9.3 4.8 collective-permute-start
  23.8 2.7 fusion.27
  28.2 2.4 copy.58
  30.6 5.1 collective-permute-start.2
  47.4 2.7 fusion.49
  53.1 10.8 %gather_fusion.1 = f32[4096,32]{1,0:T(8,128)S(1)} fusion(f32[128,32]{1,0:T(8,128)S(1)} %bitcast.176, s32[4096]{0:T(1024)S(1)} %broadcast_clamp_fusion), kind=kCustom, calls=%fused_computation.1 | custom fusion | bytes 1064960 | tf_op jit(solution)/shard_map/jit(_take)/gather | solution.py:110
  64.8 5.3 fusion.33
  74.3 78.5 %psum.15 = f32[64,64]{1,0:T(8,128)S(1)} all-reduce(f32[64,64]{1,0:T(8,128)S(1)} %bitcast.183), channel_id=1, replica_groups=mesh['space'=16,'members'=2] {'space'}, use_global_device_ids=true, to_apply=%region_4.5 | all-reduce | flops 4096 | bytes 32768 | tf_op jit(solution)/shard_map/psum | solution.py:111
  152.8 47.3 %all-reduce.2.cloned.1.call-done = f32[64,64,64]{1,2,0:T(8,128)} async-done(((f32[64,64,64]{1,2,0:T(8,128)}), f32[64,64,64]{1,2,0:T(8,128)}) %all-reduce.2.cloned.1.call-update) | async-done | bytes 1048592 | tf_op jit(solution)/shard_map/psum | solution.py:111
  200.1 3.2 broadcast_add_fusion
  203.4 3.1 copy.67
  206.4 3.4 fusion
  209.8 376.8 %custom-call.11 = f32[64,64,64]{2,1,0:T(8,128)} custom-call(f32[64,64,64]{2,1,0:T(8,128)} %fusion), custom_call_target="Cholesky" | custom-call | tf_op jit(solution)/shard_map/jit(cholesky)/cholesky | solution.py:79
  586.6 2.4 copy.68
  591.4 68.4 %custom-call.12 = f32[64,1,64,64]{0,2,3,1:T(8,128)} custom-call(f32[64,1,64,64]{0,3,2,1:T(8,128)} %select_bitcast_fusion), custom_call_target="InvertDiagBlocksLowerTriangular" | custom-call | tf_op jit(solution)/shard_map/jit(_solve_triangular)/vmap()/triangular_solve | solution.py:81
  659.8 3.1 copy.87
  664.8 3.4 fusion.130
  668.5 28.8 %scatter_custom_fusion = f32[8192]{0:T(1024)S(1)} fusion(s32[4096]{0:T(1024)S(1)} %reshape.111, f32[4096]{0:T(1024)S(1)} %reshape.113, f32[]{:T(128)} %constant.90.clone.1), kind=kCustom, calls=%fused_computation.113 | custom fusion | flops 4096 | bytes 32772
  700.4 3.6 collective-permute-start.4
  707.6 3.1 collective-permute-done.5
  712.2 2.7 fusion.29
  718.4 4.3 collective-permute-start.6
  730.4 2.3 fusion.7
  732.8 2.7 fusion.47
  (133 shorter events, 56.8 us)
Async XLA Ops:
  7.2 193.0 %all-reduce.2.cloned.1.call-start = ((), (), s32[]{:S(2)}) async-start(), calls=%async_computation | async-start | bytes 4194304 | tf_op jit(solution)/shard_map/psum | solution.py:111
  8.6 7.6 %copy-start.19 = (s32[1,32]{1,0:T(1,128)S(1)}, s32[1,32]{1,0:T(1,128)}, u32[]{:S(2)}) copy-start(s32[1,32]{1,0:T(1,128)} %param.18) | copy-start | bytes 388
  8.6 8.2 %copy-start.3 = (s32[64,64]{1,0:T(8,128)S(1)}, s32[64,64]{1,0:T(8,128)}, u32[]{:S(2)}) copy-start(s32[64,64]{1,0:T(8,128)} %param.20) | copy-start | bytes 49156
  8.6 8.3 %copy-start.1 = (f32[64,128]{1,0:T(8,128)S(1)}, f32[64,128]{1,0:T(8,128)}, u32[]{:S(2)}) copy-start(f32[64,128]{1,0:T(8,128)} %param.14) | copy-start | bytes 98308
  8.6 8.2 %copy-start.4 = (bf16[3,48,48]{2,1,0:T(8,128)(2,1)S(1)}, bf16[3,48,48]{2,1,0:T(8,128)(2,1)}, u32[]{:S(2)}) copy-start(bf16[3,48,48]{2,1,0:T(8,128)(2,1)} %param.23) | copy-start | bytes 41476
  8.6 8.2 %copy-start.7 = (f32[48]{0:T(128)S(1)}, f32[48]{0:T(128)}, u32[]{:S(2)}) copy-start(f32[48]{0:T(128)} %param.22) | copy-start | bytes 580
  8.6 8.2 %copy-start.8 = (f32[48]{0:T(128)S(1)}, f32[48]{0:T(128)}, u32[]{:S(2)}) copy-start(f32[48]{0:T(128)} %param.21) | copy-start | bytes 580
  8.6 9.8 %copy-start.13 = (bf16[144]{0:T(256)(128)(2,1)S(1)}, bf16[144]{0:T(256)(128)(2,1)}, u32[]{:S(2)}) copy-start(bf16[144]{0:T(256)(128)(2,1)} %param.27) | copy-start | bytes 868
  9.3 11.7 %collective-permute-start = (bf16[48,64,1]{1,0,2:T(8,128)(2,1)S(1)}, bf16[48,64,1]{1,0,2:T(8,128)(2,1)S(1)}, u32[]{:S(2)}, u32[]{:S(2)}) collective-permute-start(bf16[48,64,1]{1,0,2:T(8,128)(2,1)S(1)} %copy.54), channel_id=1, source_target_pairs={{0,2},{2,4},{4,6},{6,8},{8,10},{10,12},{12,14},{14,16},{16,18},{18... | collective-permute-start | bytes 18440 | tf_op jit(solution)/shard_map/ppermute | solution.py:12
  14.9 7.4 collective-permute-start.1
  16.8 2.8 copy-start.18
  16.8 3.4 copy-start.17
  30.6 8.2 %collective-permute-start.2 = (bf16[96,64,2]{0,1,2:T(8,128)(2,1)}, bf16[96,64,2]{0,1,2:T(8,128)(2,1)}, u32[]{:S(2)}, u32[]{:S(2)}) collective-permute-start(bf16[96,64,2]{0,1,2:T(8,128)(2,1)} %copy.58), channel_id=1, source_target_pairs={{0,2},{2,4},{4,6},{6,8},{8,10},{10,12},{12,14},{14,16},{16,18},{18... | collective-permute-start | bytes 73736 | tf_op jit(solution)/shard_map/ppermute | solution.py:12
  36.0 4.4 copy-start.5
  37.4 6.1 collective-permute-start.3
  47.4 3.5 copy-start.9
  203.4 3.1 copy-start
  697.5 6.5 copy-start.2
  699.4 4.6 copy-start.14
  700.4 6.0 collective-permute-start.4
  705.1 5.6 collective-permute-start.5
  707.1 5.1 copy-start.21
  718.4 6.7 collective-permute-start.6
  723.7 5.8 collective-permute-start.7
  (8 other events, 16.8 us)
Sparse Core Ops, SparseCore 0:
  70.3 129.7 all-reduce.1
where the time goes:
time: 751 us; the launch traced here: 743 us
  other arithmetic  491 us (65%)
  blocking collectives  82.4 us (11%)
  waiting for transfers between devices  53.1 us (7%)
  local copies, waits for them, and re-layouts  41 us (5%)
  matrix products  36.9 us (5%)
  starting transfers between devices  23.1 us (3%)
  between operations  15.7 us (2%)
    another operation x4, other arithmetic, solve_weights(): factor = jnp.linalg.cholesky(system)  378 us
    psum x1, blocking collectives, on_device(): gram, rhs = lax.psum((gram, rhs), 'space')  78.5 us
    another operation x3, other arithmetic, solve_weights(): jax.scipy.linalg.solve_triangular(factor, half_solved, lower=True, trans=1)  70.1 us
    psum x1, waiting for transfers between devices, on_device(): gram, rhs = lax.psum((gram, rhs), 'space')  47.3 us
    unnamed x5, other arithmetic  29.1 us
    dot_general x10, matrix products, dilated_conv(): jnp.einsum('oc,cmn->omn', kernel_taps[kernel_tap], window_cells, preferre...  18.3 us
    ppermute x4, starting transfers between devices, padded(): lax.ppermute(lax.slice_in_dim(block, block.shape[dim] - width, None, axis...  17.9 us
  transfers between devices with their start and end apart: 9, of which 4 were waited for; matrix products, arithmetic and copies ran while one was open for 3% of the time, Pallas kernels for 0%

commit v1 on v0

v1 whole, which is shorter than its diff:
```python
import functools

import jax
import jax.numpy as jnp
from jax import lax
from jax.experimental import pallas as pl
from jax.experimental.pallas import tpu as pltpu
from jax.sharding import PartitionSpec as P

F32 = jnp.float32
BF16 = jnp.bfloat16
HALO = 3
EDGE = 8
PARTS = 4
VMEM = pl.BlockSpec(memory_space=pltpu.VMEM)
SMEM = pl.BlockSpec(memory_space=pltpu.SMEM)


def shape(dims, dtype=F32):
    return jax.ShapeDtypeStruct(dims, dtype)


def call(kernel, outs, args, in_specs=None, scratch=(), flops=0, limit=40):
    return pl.pallas_call(
        kernel,
        out_shape=outs,
        in_specs=in_specs or [VMEM] * len(args),
        out_specs=jax.tree.map(lambda _: VMEM, outs),
        scratch_shapes=list(scratch),
        cost_estimate=pl.CostEstimate(flops=flops, bytes_accessed=1 << 18, transcendentals=0),
        compiler_params=pltpu.CompilerParams(vmem_limit_bytes=limit << 20),
    )(*args)


def column(row):
    size = row.shape[1]
    same = lax.broadcasted_iota(jnp.int32, (size, size), 0) == lax.broadcasted_iota(
        jnp.int32, (size, size), 1
    )
    return jnp.sum(jnp.where(same, row, 0.0), axis=1, keepdims=True)


def pick(rows, group, width):
    own = rows[:, :width]
    for other in range(1, rows.shape[1] // width):
        own = jnp.where(group == other, rows[:, other * width : (other + 1) * width], own)
    return own


def edges_kernel(field, turned, low, high):
    value = field[...].T
    turned[...] = value
    low[...] = value[:EDGE]
    high[...] = value[value.shape[0] - EDGE :]


def weights_kernel(
    gain, bias, conv1, bias1, conv2, bias2, readout, neighbours,
    taps1, taps2, last, columns, near, near_turned, wide1, wide2,
):
    channels = gain.shape[0]
    for tap in range(3):
        wide1[:, tap * channels : (tap + 1) * channels] = 0.5 * conv1[tap].astype(F32)
    taps1[...] = wide1[...].astype(BF16)
    wide2[...] = jnp.zeros_like(wide2)
    both = 2 * channels
    for tap in range(3):
        wide2[0:channels, tap * both : (tap + 1) * both] = 0.5 * conv2[tap].astype(F32)
    row = readout[...].astype(F32).reshape(1, 3 * channels)
    wide2[channels : channels + 1, both : 2 * both] = row[:, :both]
    taps2[...] = wide2[...].astype(BF16)
    pad = jnp.zeros((last.shape[0] - 1, channels), F32)
    last[...] = jnp.concatenate([row[:, both:], pad], axis=0).astype(BF16)
    for spot, (source, factor) in enumerate(((gain, 1.0), (bias, 1.0), (bias1, 0.5), (bias2, 0.5))):
        col = column(source[...].astype(F32).reshape(1, channels)) * factor
        columns[spot] = jnp.broadcast_to(col, (channels, columns.shape[2]))
    ids = neighbours[...]
    pair = jnp.concatenate([ids, ids], axis=1)
    near[...] = jnp.concatenate([pair, pair], axis=0)
    near_turned[...] = pair.T


def surrogate(ext, space, taps1, taps2, last, columns, first, second, heads, turned):
    spaces = lax.axis_size("space")
    cells = ext.shape[0] - 2 * HALO
    members = ext.shape[1]
    run = cells // PARTS
    rows = run + 2 * HALO
    lanes = PARTS * members
    wide = jnp.concatenate([ext[q * run : q * run + rows] for q in range(PARTS)], axis=1)
    gain, bias, bias1, bias2 = [
        jnp.concatenate([columns[i]] * (lanes // columns.shape[2]), axis=1) for i in range(4)
    ]
    channels = gain.shape[0]
    lane = lax.broadcasted_iota(jnp.int32, (1, lanes), 1)
    left = jnp.where((lane < members) & (space == 0), 0.0, 1.0)
    right = jnp.where((lane >= lanes - members) & (space == spaces - 1), 0.0, 1.0)
    for r in range(rows):
        value = jnp.tanh(gain * wide[r : r + 1] + bias)
        if r < HALO:
            value = value * left
        if r >= rows - HALO:
            value = value * right
        first[r] = value.astype(BF16)
    for i in range(rows - 2):
        window = first[i : i + 3].reshape(3 * channels, lanes)
        half = jnp.dot(taps1[...], window, preferred_element_type=F32) + bias1
        value = half + half * jnp.tanh(half)
        if i < HALO - 1:
            value = value * left
        if i >= rows - 2 - (HALO - 1):
            value = value * right
        second[i] = value.astype(BF16)
    for n in range(run):
        window = jnp.concatenate(
            [first[n + 1], second[n], first[n + 3], second[n + 2], first[n + 5], second[n + 4]],
            axis=0,
        )
        total = jnp.dot(taps2[...], window, preferred_element_type=F32)
        half = total[:channels] + bias2
        third = (half + half * jnp.tanh(half)).astype(BF16)
        rest = jnp.dot(last[...], third, preferred_element_type=F32)
        heads[n : n + 1, :] = total[channels : channels + 1] + rest[0:1]
    for q in range(PARTS):
        turned[q * run : (q + 1) * run, :] = heads[:, q * members : (q + 1) * members]


def observe_kernel(
    field, from_left, from_right, taps1, taps2, last, columns,
    obs_heads, obs_var, obs_noise, obs_index, obs_count,
    sent, first, second, heads, turned, chosen,
):
    space = lax.axis_index("space")
    group = lax.axis_index("members")
    members = field.shape[0]
    own = field[...].T
    ext = jnp.concatenate(
        [
            pick(from_left[...], group, members)[EDGE - HALO :],
            own,
            pick(from_right[...], group, members)[:HALO],
        ],
        axis=0,
    )
    surrogate(ext, space, taps1, taps2, last, columns, first, second, heads, turned)
    slots = obs_var.shape[0]
    for k in range(slots):
        chosen[k : k + 1, :] = turned[pl.ds(obs_index[0, k], 1), :]
    own_obs = chosen[...]
    target = column(obs_heads[...].reshape(1, slots))
    variance = column(obs_var[...].reshape(1, slots))
    live = lax.broadcasted_iota(jnp.int32, (slots, 1), 0) < obs_count[0]
    root = jnp.where(live, lax.rsqrt(variance), 0.0)
    innovation = target + jnp.sqrt(variance) * obs_noise[...].T - own_obs
    payload = jnp.concatenate([root * own_obs, root * innovation], axis=1)
    for copy in range(sent.shape[0]):
        sent[copy] = payload


def split3(value):
    one = value.astype(BF16)
    rest = value - one.astype(F32)
    two = rest.astype(BF16)
    three = (rest - two.astype(F32)).astype(BF16)
    return jnp.concatenate([one, two, three], axis=1)


def lane_gather(table, index):
    low = index & 127
    high = index >> 7
    found = None
    for tile in range(table.shape[1] // 128):
        part = jnp.take_along_axis(
            table[:, tile * 128 : (tile + 1) * 128], low, axis=1, mode="promise_in_bounds"
        )
        found = part if found is None else jnp.where(high == tile, part, found)
    return found


def update_kernel(
    got, field, turned_all, from_left, from_right, taps1, taps2, last, columns, near, near_turned,
    updated, new_heads,
    system, inverse, first, second, heads, turned,
):
    space = lax.axis_index("space")
    group = lax.axis_index("members")
    groups, slots = got.shape[0], got.shape[1] * got.shape[2]
    members = got.shape[3] // 2
    everyone = groups * members
    order = near.shape[0] // 2
    half_lane = lax.broadcasted_iota(jnp.int32, (1, 128), 1) < 64

    panel = jnp.concatenate(
        [got[g].reshape(slots, 2 * members)[:, :members] for g in range(groups)], axis=1
    )
    panel = panel - jnp.mean(panel, axis=1, keepdims=True)
    innovation = got[group].reshape(slots, 2 * members)[:, members:]
    stacked = jnp.concatenate([panel, innovation], axis=1)
    product = lax.dot_general(
        stacked, panel, (((0,), (0,)), ((), ())),
        precision=lax.Precision.HIGHEST, preferred_element_type=F32,
    )
    gram = split3(product[:everyone])
    sides = product[everyone:]

    ids = near[...]
    second_half = (lax.broadcasted_iota(jnp.int32, (128, 128), 0) >= 64).astype(jnp.int32)
    lane_id = lax.broadcasted_iota(jnp.int32, (128, 128), 1)
    row_id = lax.broadcasted_iota(jnp.int32, (128, 128), 0)
    everyone_id = lax.broadcasted_iota(jnp.int32, (128, everyone), 1)

    def extract(quad, carry):
        found = []
        for b in range(2):
            column_id = 4 * quad + 2 * b + second_half
            member = jnp.take_along_axis(ids, column_id, axis=1, mode="promise_in_bounds")
            member = jnp.concatenate([member] * (everyone // 128), axis=1)
            chosen = jnp.where(member == everyone_id, 1.0, 0.0).astype(BF16)
            parts = jnp.dot(chosen, gram, preferred_element_type=F32)
            rows = (
                parts[:, :everyone]
                + parts[:, everyone : 2 * everyone]
                + parts[:, 2 * everyone :]
            )
            found.append(lane_gather(rows, ids))
        block = jnp.where(half_lane, found[0], found[1]).T
        own = 4 * quad + 2 * (row_id >= 64).astype(jnp.int32) + (lane_id >= 64).astype(jnp.int32)
        block = block + jnp.where((row_id & 63) == own, order - 1.0, 0.0)
        system[pl.ds(pl.multiple_of(quad * 128, 128), 128), :] = block
        return carry

    lax.fori_loop(0, order // 4, extract, 0)
    side = lane_gather(jnp.concatenate([sides, sides], axis=0), ids)
    side = jnp.where(row_id >= 64, 1.0, side).T[:order]
    system[order // 2 * order : (order // 2 + 1) * order, :] = side

    blocks = order // 2
    level = lax.broadcasted_iota(jnp.int32, (order, 128), 0)

    def both(value):
        turn = pltpu.roll(value, 64, 1)
        return jnp.where(half_lane, value, turn), jnp.where(half_lane, turn, value)

    chunk = 4

    def eliminate(start, pair):
        base = pl.multiple_of(pair * order, order)
        col0, col1 = both(system[pl.ds(base, order), :])
        pivot0 = 2 * pair
        d0, e0 = both(system[pl.ds(base + pivot0, 1), :])
        _, f0 = both(system[pl.ds(base + pivot0 + 1, 1), :])
        inv0 = 1.0 / d0
        ratio = e0 * inv0
        inv1 = 1.0 / (f0 - ratio * e0)
        inverse[pl.ds(pivot0, 1), :] = inv0
        inverse[pl.ds(pivot0 + 1, 1), :] = inv1
        fac0 = jnp.where(level == pivot0, 0.0, col0 * inv0)
        fac1 = jnp.where(level == pivot0 + 1, 0.0, (col1 - fac0 * e0) * inv1)

        for block in list(range(start, blocks)) + [blocks]:
            at = block * order
            row0 = system[pl.ds(at + pivot0, 1), :]
            row1 = system[pl.ds(at + pivot0 + 1, 1), :] - ratio * row0
            system[at : at + order, :] = system[at : at + order, :] - fac0 * row0 - fac1 * row1

    for start in range(0, blocks, chunk):
        def step(pair, carry, start=start):
            eliminate(start, pair)
            return carry

        lax.fori_loop(start, start + chunk, step, 0)

    solved = system[blocks * order : (blocks + 1) * order, :] * inverse[...]
    sums = jnp.sum(solved, axis=0, keepdims=True)
    share = sums / pltpu.roll(sums, 64, 1)
    coef = (solved - pltpu.roll(solved, 64, 1) * share)[:, :members]
    coef = coef - jnp.mean(coef, axis=0, keepdims=True)
    names = lax.broadcasted_iota(jnp.int32, (everyone, members), 0)
    mixing = jnp.zeros((everyone, members), F32)
    for i in range(order):
        mixing = jnp.where(names == near_turned[i : i + 1, :members], coef[i : i + 1], mixing)

    sources = jnp.concatenate(
        [from_left[EDGE - HALO :, :], turned_all[...], from_right[:HALO, :]], axis=0
    )
    own = jnp.concatenate(
        [
            pick(from_left[...], group, members)[EDGE - HALO :],
            field[...].T,
            pick(from_right[...], group, members)[:HALO],
        ],
        axis=0,
    )
    ext = own + jnp.dot(
        sources, mixing, precision=lax.Precision.HIGHEST, preferred_element_type=F32
    )
    cells = field.shape[1]
    updated[...] = ext[HALO : HALO + cells].T
    surrogate(ext, space, taps1, taps2, last, columns, first, second, heads, turned)
    new_heads[...] = turned[...].T


def on_device(
    log_field, obs_heads, obs_var, obs_noise, obs_index, obs_count, neighbours,
    lift_gain, lift_bias, conv_first, bias_first, conv_second, bias_second, readout,
):
    members, cells = log_field.shape
    spaces = lax.axis_size("space")
    channels = lift_gain.shape[0]
    slots = obs_var.shape[0]
    order = neighbours.shape[1]
    everyone = lax.all_gather(log_field, "members", axis=0, tiled=True)
    total = everyone.shape[0]
    turned_all, low, high = call(
        edges_kernel,
        (shape((cells, total)), shape((EDGE, total)), shape((EDGE, total))),
        (everyone,),
    )
    forward = [(i, i + 1) for i in range(spaces - 1)]
    backward = [(i + 1, i) for i in range(spaces - 1)]
    from_left = lax.ppermute(high, "space", forward)
    from_right = lax.ppermute(low, "space", backward)
    taps1, taps2, last, columns, near, near_turned = call(
        weights_kernel,
        (
            shape((channels, 3 * channels), BF16),
            shape((channels + 16, 6 * channels), BF16),
            shape((16, channels), BF16),
            shape((4, channels, 128)),
            shape((2 * members, 2 * order), jnp.int32),
            shape((2 * order, members), jnp.int32),
        ),
        (lift_gain, lift_bias, conv_first, bias_first, conv_second, bias_second, readout, neighbours),
        scratch=(
            pltpu.VMEM((channels, 3 * channels), F32),
            pltpu.VMEM((channels + 16, 6 * channels), F32),
        ),
        flops=1 << 22,
    )
    run = cells // PARTS
    rows = run + 2 * HALO
    lanes = PARTS * members
    work = (
        pltpu.VMEM((rows, channels, lanes), BF16),
        pltpu.VMEM((rows - 2, channels, lanes), BF16),
        pltpu.VMEM((run, lanes), F32),
        pltpu.VMEM((cells, members), F32),
    )
    sent = call(
        observe_kernel,
        shape((spaces, slots, 2 * members)),
        (
            log_field, from_left, from_right, taps1, taps2, last, columns,
            obs_heads, obs_var, obs_noise, obs_index, obs_count,
        ),
        in_specs=[VMEM] * 10 + [SMEM] * 2,
        scratch=work + (pltpu.VMEM((slots, members), F32),),
    )
    got = lax.all_to_all(sent, "space", 0, 0)
    got = lax.all_gather(got, "members", axis=0, tiled=False)
    return call(
        update_kernel,
        (shape((members, cells)), shape((members, cells))),
        (
            got, log_field, turned_all, from_left, from_right,
            taps1, taps2, last, columns, near, near_turned,
        ),
        scratch=(
            pltpu.VMEM(((order // 2 + 1) * order, 128), F32),
            pltpu.VMEM((order, 128), F32),
        )
        + work,
    )


def solution(mesh):
    in_specs = (
        P("members", "space"),
        P("space"),
        P("space"),
        P("members", "space"),
        P("space", None),
        P("space"),
        P("members", None),
        P(),
        P(),
        P(),
        P(),
        P(),
        P(),
        P(),
    )
    out_specs = (P("members", "space"), P("members", "space"))
    return jax.shard_map(
        on_device, mesh=mesh, in_specs=in_specs, out_specs=out_specs, check_vma=False
    )
```

time: 751 us -> 59.6 us (0.08)
  other arithmetic: 491 us -> 0 us
  blocking collectives: 82.4 us -> 20.3 us
  waiting for transfers between devices: 53.1 us -> 2.6 us
  local copies, waits for them, and re-layouts: 41 us -> 1.36 us
  matrix products: 36.9 us -> 0 us
  Pallas kernels: 0 us -> 27.5 us
  starting transfers between devices: 23.1 us -> 6.03 us
  between operations: 15.7 us -> 1.41 us
    another operation x7 -> x0, other arithmetic: 448 us -> none  [the longest x4 378 us: solve_weights(): factor = jnp.linalg.cholesky(system)]
    psum x1 -> x0, blocking collectives: 78.5 us -> none  [on_device(): gram, rhs = lax.psum((gram, rhs), 'space')]
    psum x1 -> x0, waiting for transfers between devices: 47.3 us -> none  [on_device(): gram, rhs = lax.psum((gram, rhs), 'space')]
    dot_general x19 -> x0, matrix products: 31.7 us -> none  [the longest x10 18.3 us: dilated_conv(): jnp.einsum('oc,cmn->omn', kernel_taps[kernel_tap], window_cells, preferre...]
    unnamed x5 -> x0, other arithmetic: 29.1 us -> none
    pallas_call x0 -> x4, Pallas kernels: none -> 27.5 us  [call(): pl.pallas_call(kernel, out_shape=outs, in_specs=in_specs or [VMEM] * len(...]
    ppermute x8 -> x2, starting transfers between devices: 23 us -> 6.03 us  [the longest x1 4.74 us: on_device(): from_left = lax.ppermute(high, 'space', forward)]
    all_to_all x0 -> x1, blocking collectives: none -> 16 us  [on_device(): got = lax.all_to_all(sent, 'space', 0, 0)]
  transfers between devices with their start and end apart: 9 -> 2, of which waited for: 4 -> 1; matrix products, arithmetic and copies ran while one was open for 3% -> 0% of each run, Pallas kernels for 0% -> 0%
where the time goes in v1:
time: 59.6 us; the launch traced here: 59.2 us
  Pallas kernels  27.5 us (46%)
  blocking collectives  20.3 us (34%)
  starting transfers between devices  6.03 us (10%)
  waiting for transfers between devices  2.6 us (4%)
  between operations  1.41 us (2%)
  local copies, waits for them, and re-layouts  1.36 us (2%)
    pallas_call x4, Pallas kernels, call(): pl.pallas_call(kernel, out_shape=outs, in_specs=in_specs or [VMEM] * len(...  27.5 us
    all_to_all x1, blocking collectives, on_device(): got = lax.all_to_all(sent, 'space', 0, 0)  16 us
    ppermute x1, starting transfers between devices, on_device(): from_left = lax.ppermute(high, 'space', forward)  4.74 us
    ppermute x1, waiting for transfers between devices, on_device(): from_right = lax.ppermute(low, 'space', backward)  2.6 us
    all_gather x1, blocking collectives, on_device(): everyone = lax.all_gather(log_field, 'members', axis=0, tiled=True)  2.17 us
    all_gather x1, blocking collectives, on_device(): got = lax.all_gather(got, 'members', axis=0, tiled=False)  2.17 us
    unnamed x27, local copies, waits for them, and re-layouts  1.36 us
    ppermute x1, starting transfers between devices, on_device(): from_right = lax.ppermute(low, 'space', backward)  1.29 us
  transfers between devices with their start and end apart: 2, of which 1 were waited for; matrix products, arithmetic and copies ran while one was open for 0% of the time, Pallas kernels for 0%

profile of v1, /device:TPU:0, one launch (start us, length us, event | category | flops | bytes accessed | tf_op | source)
XLA Modules:
  0.0 59.2 jit_solution(1339616007318330295)
XLA Ops:
  0.6 2.2 %all_gather.9.field = f32[128,128]{1,0:T(8,128)S(1)} all-gather(f32[64,128]{1,0:T(8,128)} %field.3), channel_id=1, replica_groups=mesh['space'=16,'members'=2] {'members'}, dimensions={0}, use_global_device_ids=true | all-gather | bytes 98304 | tf_op jit(solution)/shard_map/all_gather | solution.py:312
  2.8 0.1 shard_map.149
  2.9 0.0 copy-start.1
  2.9 4.7 %collective-permute-start = (f32[8,128]{1,0:T(8,128)S(1)}, f32[8,128]{1,0:T(8,128)S(1)}, u32[]{:S(2)}, u32[]{:S(2)}) collective-permute-start(f32[8,128]{1,0:T(8,128)S(1)} %get-tuple-element.11), channel_id=1, source_target_pairs={{0,2},{2,4},{4,6},{6,8},{8,10},{10,12},{12,14},{14,16},{16,18},{18... | collective-permute-start | bytes 12296 | tf_op jit(solution)/shard_map/ppermute | solution.py:321
  7.7 1.3 %collective-permute-start.1 = (f32[8,128]{1,0:T(8,128)S(1)}, f32[8,128]{1,0:T(8,128)S(1)}, u32[]{:S(2)}, u32[]{:S(2)}) collective-permute-start(f32[8,128]{1,0:T(8,128)S(1)} %get-tuple-element.12), channel_id=1, source_target_pairs={{2,0},{4,2},{6,4},{8,6},{10,8},{12,10},{14,12},{16,14},{18,16},{20... | collective-permute-start | bytes 12296 | tf_op jit(solution)/shard_map/ppermute | solution.py:322
  9.6 0.0 copy-start.4
  9.6 0.0 copy-start.5
  9.6 0.0 copy-start.6
  9.7 0.0 copy-start.7
  9.7 0.1 copy.17.obs_noise
  9.8 0.5 copy-done.4
  10.3 0.0 copy-done.5
  10.3 0.0 copy-done.6
  10.3 0.0 copy-done.7
  10.3 0.0 copy-done.8
  10.3 0.2 shard_map.150
  10.6 2.6 %collective-permute-done.1.from_right = f32[8,128]{1,0:T(8,128)S(1)} collective-permute-done((f32[8,128]{1,0:T(8,128)S(1)}, f32[8,128]{1,0:T(8,128)S(1)}, u32[]{:S(2)}, u32[]{:S(2)}) %collective-permute-start.1) | collective-permute-done | bytes 4128 | tf_op jit(solution)/shard_map/ppermute | solution.py:322
  13.2 0.6 %copy-done.9 = f32[32]{0:T(128)S(1)} copy-done((f32[32]{0:T(128)S(1)}, f32[32]{0:T(128)}, u32[]{:S(2)}) %copy-start.9) | copy-done | bytes 152
  13.8 0.0 copy-done.10
  13.8 0.0 copy-done.11
  13.9 4.8 %shard_map.151 = f32[16,32,128]{2,1,0:T(8,128)S(1)} custom-call(f32[64,128]{1,0:T(8,128)S(1)} %copy-done, f32[8,128]{1,0:T(8,128)S(1)} %collective-permute-done.from_left, f32[8,128]{1,0:T(8,128)S(1)} %collective-permute-done.1.from_right, bf16[48,144]{1,0:T(8,128)(2,1)S(1)} %get-tuple-element.13.taps1, bf16[64,288]{1,0:T(8,128)(2,1)S(1)} %get-tuple-element.14.taps2, ...), custom_call_target="tpu_custom_call" | custom-call | bytes 262144 | tf_op jit(solution)/shard_map/pallas_call | solution.py:24
  18.6 16.0 %all_to_all.5 = f32[16,32,128]{2,1,0:T(8,128)S(1)} all-to-all(f32[16,32,128]{2,1,0:T(8,128)S(1)} %shard_map.151), channel_id=1, replica_groups=mesh['space'=16,'members'=2] {'space'}, dimensions={0} | all-to-all | bytes 524288 | tf_op jit(solution)/shard_map/all_to_all | solution.py:359
  34.6 2.2 %all-gather = f32[32,32,128]{2,1,0:T(8,128)S(1)} all-gather(f32[16,32,128]{2,1,0:T(8,128)S(1)} %all_to_all.5), channel_id=2, replica_groups=mesh['space'=16,'members'=2] {'members'}, dimensions={0}, use_global_device_ids=true | all-gather | bytes 786432 | tf_op jit(solution)/shard_map/all_gather | solution.py:360
  36.8 22.4 %shard_map.152 = (f32[64,128]{1,0:T(8,128)}, f32[64,128]{1,0:T(8,128)}) custom-call(f32[2,16,32,128]{3,2,1,0:T(8,128)S(1)} %bitcast.1, f32[64,128]{1,0:T(8,128)S(1)} %copy-done, f32[128,128]{1,0:T(8,128)S(1)} %get-tuple-element.17.turned_all, f32[8,128]{1,0:T(8,128)S(1)} %collective-permute-done.from_left, f32[8,128]{1,0:T(8,128)S(1)} %collective-permute-done.1.from_right, ...), custom_call_target="tpu_custom_call" | custom-call | bytes 262144 | tf_op jit(solution)/shard_map/pallas_call | solution.py:24
  (14 shorter events, 0.0 us)
Async XLA Ops:
  0.6 9.0 %copy-start.12 = (f32[64,32]{0,1:T(8,128)S(1)}, f32[64,32]{0,1:T(8,128)}, u32[]{:S(2)}) copy-start(f32[64,32]{0,1:T(8,128)} %param.17) | copy-start | bytes 24580
  2.8 7.0 %copy-start.2 = (bf16[3,48,96]{2,1,0:T(8,128)(2,1)S(1)}, bf16[3,48,96]{2,1,0:T(8,128)(2,1)}, u32[]{:S(2)}) copy-start(bf16[3,48,96]{2,1,0:T(8,128)(2,1)} %conv2.1) | copy-start | bytes 82948
  2.8 7.0 %copy-start.3 = (s32[64,64]{1,0:T(8,128)S(1)}, s32[64,64]{1,0:T(8,128)}, u32[]{:S(2)}) copy-start(s32[64,64]{1,0:T(8,128)} %neighbours.1) | copy-start | bytes 49156
  2.9 6.9 %copy-start.1 = (bf16[3,48,48]{2,1,0:T(8,128)(2,1)S(1)}, bf16[3,48,48]{2,1,0:T(8,128)(2,1)}, u32[]{:S(2)}) copy-start(bf16[3,48,48]{2,1,0:T(8,128)(2,1)} %conv1.1) | copy-start | bytes 41476
  2.9 7.6 %collective-permute-start = (f32[8,128]{1,0:T(8,128)S(1)}, f32[8,128]{1,0:T(8,128)S(1)}, u32[]{:S(2)}, u32[]{:S(2)}) collective-permute-start(f32[8,128]{1,0:T(8,128)S(1)} %get-tuple-element.11), channel_id=1, source_target_pairs={{0,2},{2,4},{4,6},{6,8},{8,10},{10,12},{12,14},{14,16},{16,18},{18... | collective-permute-start | bytes 12296 | tf_op jit(solution)/shard_map/ppermute | solution.py:321
  7.7 5.5 %collective-permute-start.1 = (f32[8,128]{1,0:T(8,128)S(1)}, f32[8,128]{1,0:T(8,128)S(1)}, u32[]{:S(2)}, u32[]{:S(2)}) collective-permute-start(f32[8,128]{1,0:T(8,128)S(1)} %get-tuple-element.12), channel_id=1, source_target_pairs={{2,0},{4,2},{6,4},{8,6},{10,8},{12,10},{14,12},{16,14},{18,16},{20... | collective-permute-start | bytes 12296 | tf_op jit(solution)/shard_map/ppermute | solution.py:322
  9.6 0.7 %copy-start.4 = (f32[48]{0:T(128)S(1)}, f32[48]{0:T(128)}, u32[]{:S(2)}) copy-start(f32[48]{0:T(128)} %gain.1) | copy-start | bytes 580
  9.6 0.7 %copy-start.5 = (f32[48]{0:T(128)S(1)}, f32[48]{0:T(128)}, u32[]{:S(2)}) copy-start(f32[48]{0:T(128)} %bias.1) | copy-start | bytes 580
  9.6 0.7 %copy-start.6 = (f32[48]{0:T(128)S(1)}, f32[48]{0:T(128)}, u32[]{:S(2)}) copy-start(f32[48]{0:T(128)} %bias1.1) | copy-start | bytes 580
  9.7 0.7 %copy-start.7 = (f32[48]{0:T(128)S(1)}, f32[48]{0:T(128)}, u32[]{:S(2)}) copy-start(f32[48]{0:T(128)} %bias2.1) | copy-start | bytes 580
  9.7 0.7 %copy-start.8 = (bf16[144]{0:T(256)(128)(2,1)S(1)}, bf16[144]{0:T(256)(128)(2,1)}, u32[]{:S(2)}) copy-start(bf16[144]{0:T(256)(128)(2,1)} %readout.1) | copy-start | bytes 868
  10.3 2.8 %copy-start = (f32[64,128]{1,0:T(8,128)S(1)}, f32[64,128]{1,0:T(8,128)}, u32[]{:S(2)}) copy-start(f32[64,128]{1,0:T(8,128)} %field.3) | copy-start | bytes 98308
  13.2 0.7 %copy-start.9 = (f32[32]{0:T(128)S(1)}, f32[32]{0:T(128)}, u32[]{:S(2)}) copy-start(f32[32]{0:T(128)} %obs_heads.1) | copy-start | bytes 388
  13.2 0.7 %copy-start.10 = (f32[32]{0:T(128)S(1)}, f32[32]{0:T(128)}, u32[]{:S(2)}) copy-start(f32[32]{0:T(128)} %obs_var.1) | copy-start | bytes 388
  13.2 0.7 %copy-start.11 = (s32[1,32]{1,0:T(1,128)S(1)}, s32[1,32]{1,0:T(1,128)}, u32[]{:S(2)}) copy-start(s32[1,32]{1,0:T(1,128)} %obs_index.1) | copy-start | bytes 388

commit v2 on v1

v2 whole, which is shorter than its diff:
```python
import jax
import jax.numpy as jnp
from jax import lax
from jax.experimental import pallas as pl
from jax.experimental.pallas import tpu as pltpu
from jax.sharding import PartitionSpec as P

F32 = jnp.float32
BF16 = jnp.bfloat16
HALO = 3
EDGE = 8
PARTS = 4
VMEM = pl.BlockSpec(memory_space=pltpu.VMEM)
SMEM = pl.BlockSpec(memory_space=pltpu.SMEM)


def shape(dims, dtype=F32):
    return jax.ShapeDtypeStruct(dims, dtype)


def call(kernel, outs, args, in_specs=None, scratch=(), flops=0, limit=40):
    return pl.pallas_call(
        kernel,
        out_shape=outs,
        in_specs=in_specs or [VMEM] * len(args),
        out_specs=jax.tree.map(lambda _: VMEM, outs),
        scratch_shapes=list(scratch),
        cost_estimate=pl.CostEstimate(flops=flops, bytes_accessed=1 << 18, transcendentals=0),
        compiler_params=pltpu.CompilerParams(vmem_limit_bytes=limit << 20),
    )(*args)


def column(row):
    size = row.shape[1]
    same = lax.broadcasted_iota(jnp.int32, (size, size), 0) == lax.broadcasted_iota(
        jnp.int32, (size, size), 1
    )
    return jnp.sum(jnp.where(same, row, 0.0), axis=1, keepdims=True)


def edges_kernel(field, low, high):
    value = field[...].T
    low[...] = value[:EDGE]
    high[...] = value[value.shape[0] - EDGE :]


def layers(wide, run, left, right, taps1, taps2, columns, first, second, heads):
    lanes = wide.shape[1]
    rows = run + 2 * HALO
    gain, bias, bias1, bias2, last = [
        jnp.concatenate([columns[i]] * (lanes // columns.shape[2]), axis=1) for i in range(5)
    ]
    channels = gain.shape[0]
    for r in range(rows):
        value = jnp.tanh(gain * wide[r : r + 1] + bias)
        if left is not None and r < HALO:
            value = value * left
        if right is not None and r >= rows - HALO:
            value = value * right
        first[r] = value.astype(BF16)
    for i in range(rows - 2):
        window = first[i : i + 3].reshape(3 * channels, lanes)
        half = jnp.dot(taps1[...], window, preferred_element_type=F32) + bias1
        value = half + half * jnp.tanh(half)
        if left is not None and i < HALO - 1:
            value = value * left
        if right is not None and i >= rows - 2 - (HALO - 1):
            value = value * right
        second[i] = value.astype(BF16)
    split = 3 * channels
    for n in range(run):
        window1 = jnp.concatenate([first[n + 1], first[n + 3], first[n + 5]], axis=0)
        window2 = jnp.concatenate([second[n], second[n + 2], second[n + 4]], axis=0)
        total = jnp.dot(taps2[:, :split], window1, preferred_element_type=F32) + jnp.dot(
            taps2[:, split:], window2, preferred_element_type=F32
        )
        half = total[:channels] + bias2
        third = (half + half * jnp.tanh(half)).astype(BF16).astype(F32)
        rest = jnp.sum(third * last, axis=0, keepdims=True)
        heads[n : n + 1, :] = total[channels : channels + 1] + rest


def in_runs(ext):
    run = (ext.shape[0] - 2 * HALO) // PARTS
    return jnp.concatenate([ext[q * run : (q + 1) * run + 2 * HALO] for q in range(PARTS)], axis=1)


def prepare_kernel(
    field, gain, bias, conv1, bias1, conv2, bias2, readout, neighbours,
    taps1, taps2, columns, near, near_turned, own, inner,
    wide1, wide2, first, second, heads,
):
    channels = gain.shape[0]
    split = 3 * channels
    row = readout[...].astype(F32).reshape(1, split)
    wide2[...] = jnp.zeros_like(wide2)
    for tap in range(3):
        at = slice(tap * channels, (tap + 1) * channels)
        wide1[:, at] = 0.5 * conv1[tap].astype(F32)
        both = 0.5 * conv2[tap].astype(F32)
        wide2[0:channels, at] = both[:, :channels]
        wide2[0:channels, split + tap * channels : split + (tap + 1) * channels] = both[:, channels:]
    wide2[channels : channels + 1, channels : 2 * channels] = row[:, :channels]
    wide2[channels : channels + 1, split + channels : split + 2 * channels] = row[
        :, channels : 2 * channels
    ]
    taps1[...] = wide1[...].astype(BF16)
    taps2[...] = wide2[...].astype(BF16)
    rows = [
        gain[...].reshape(1, channels),
        bias[...].reshape(1, channels),
        0.5 * bias1[...].reshape(1, channels),
        0.5 * bias2[...].reshape(1, channels),
        row[:, 2 * channels :],
    ]
    for spot, value in enumerate(rows):
        columns[spot] = jnp.broadcast_to(column(value), (channels, columns.shape[2]))
    ids = neighbours[...]
    pair = jnp.concatenate([ids, ids], axis=1)
    near[...] = jnp.concatenate([pair, pair], axis=0)
    near_turned[...] = pair.T
    turned = field[...].T
    own[...] = turned
    members = turned.shape[1]
    zeros = jnp.zeros((HALO, members), F32)
    wide = in_runs(jnp.concatenate([zeros, turned, zeros], axis=0))
    run = turned.shape[0] // PARTS
    layers(wide, run, None, None, taps1, taps2, columns, first, second, heads)
    for q in range(PARTS):
        inner[q * run : (q + 1) * run, :] = heads[:, q * members : (q + 1) * members]


def observe_kernel(
    own, inner, from_left, from_right, taps1, taps2, columns,
    obs_heads, obs_var, obs_noise, obs_index, obs_count,
    sent, ext, first, second, heads, turned, chosen,
):
    space = lax.axis_index("space")
    spaces = lax.axis_size("space")
    cells, members = own.shape
    ext[0:EDGE, :] = from_left[...]
    ext[EDGE : EDGE + cells, :] = own[...]
    ext[EDGE + cells :, :] = from_right[...]
    ends = jnp.concatenate(
        [ext[EDGE - HALO : EDGE + 2 * HALO, :], ext[EDGE + cells - 2 * HALO : EDGE + cells + HALO, :]],
        axis=1,
    )
    lane = lax.broadcasted_iota(jnp.int32, (1, 2 * members), 1)
    left = jnp.where((lane < members) & (space == 0), 0.0, 1.0)
    right = jnp.where((lane >= members) & (space == spaces - 1), 0.0, 1.0)
    layers(ends, HALO, left, right, taps1, taps2, columns, first, second, heads)
    turned[...] = inner[...]
    turned[0:HALO, :] = heads[0:HALO, :members]
    turned[cells - HALO :, :] = heads[0:HALO, members:]
    slots = obs_var.shape[0]
    for k in range(slots):
        chosen[k : k + 1, :] = turned[pl.ds(obs_index[0, k], 1), :]
    own_obs = chosen[...]
    target = column(obs_heads[...].reshape(1, slots))
    variance = column(obs_var[...].reshape(1, slots))
    live = lax.broadcasted_iota(jnp.int32, (slots, 1), 0) < obs_count[0]
    root = jnp.where(live, lax.rsqrt(variance), 0.0)
    innovation = target + jnp.sqrt(variance) * obs_noise[...].T - own_obs
    payload = jnp.concatenate([root * own_obs, root * innovation], axis=1)
    for copy in range(sent.shape[0]):
        sent[copy] = payload


def split3(value):
    one = value.astype(BF16)
    rest = value - one.astype(F32)
    two = rest.astype(BF16)
    three = (rest - two.astype(F32)).astype(BF16)
    return jnp.concatenate([one, two, three], axis=1)


def lane_gather(table, index):
    low = index & 127
    high = index >> 7
    found = None
    for tile in range(table.shape[1] // 128):
        part = jnp.take_along_axis(
            table[:, tile * 128 : (tile + 1) * 128], low, axis=1, mode="promise_in_bounds"
        )
        found = part if found is None else jnp.where(high == tile, part, found)
    return found


def update_kernel(
    got, ext, taps1, taps2, columns, near, near_turned,
    updated, new_heads,
    system, first, second, heads, turned,
):
    space = lax.axis_index("space")
    spaces = lax.axis_size("space")
    group = lax.axis_index("members")
    groups, slots = got.shape[0], got.shape[1] * got.shape[2]
    members = got.shape[3] // 2
    everyone = groups * members
    order = near.shape[0] // 2
    half_lane = lax.broadcasted_iota(jnp.int32, (1, 128), 1) < 64

    panel = jnp.concatenate(
        [got[g].reshape(slots, 2 * members)[:, :members] for g in range(groups)], axis=1
    )
    panel = panel - jnp.mean(panel, axis=1, keepdims=True)
    innovation = got[group].reshape(slots, 2 * members)[:, members:]
    stacked = jnp.concatenate([panel, innovation], axis=1)
    product = lax.dot_general(
        stacked, panel, (((0,), (0,)), ((), ())),
        precision=lax.Precision.HIGHEST, preferred_element_type=F32,
    )
    gram = split3(product[:everyone])
    sides = product[everyone:]

    ids = near[...]
    second_half = (lax.broadcasted_iota(jnp.int32, (128, 128), 0) >= 64).astype(jnp.int32)
    lane_id = lax.broadcasted_iota(jnp.int32, (128, 128), 1)
    row_id = lax.broadcasted_iota(jnp.int32, (128, 128), 0)
    everyone_id = lax.broadcasted_iota(jnp.int32, (128, everyone), 1)

    def extract(quad, carry):
        found = []
        for b in range(2):
            column_id = 4 * quad + 2 * b + second_half
            member = jnp.take_along_axis(ids, column_id, axis=1, mode="promise_in_bounds")
            member = jnp.concatenate([member] * (everyone // 128), axis=1)
            chosen = jnp.where(member == everyone_id, 1.0, 0.0).astype(BF16)
            parts = jnp.dot(chosen, gram, preferred_element_type=F32)
            rows = (
                parts[:, :everyone]
                + parts[:, everyone : 2 * everyone]
                + parts[:, 2 * everyone :]
            )
            found.append(lane_gather(rows, ids))
        block = jnp.where(half_lane, found[0], found[1]).T
        own = 4 * quad + 2 * (row_id >= 64).astype(jnp.int32) + (lane_id >= 64).astype(jnp.int32)
        block = block + jnp.where((row_id & 63) == own, order - 1.0, 0.0)
        system[pl.ds(pl.multiple_of(quad * 128, 128), 128), :] = block
        return carry

    lax.fori_loop(0, order // 4, extract, 0, unroll=order // 4)
    side = lane_gather(jnp.concatenate([sides, sides], axis=0), ids)
    side = jnp.where(row_id >= 64, 1.0, side).T[:order]
    system[order // 2 * order : (order // 2 + 1) * order, :] = side

    blocks = order // 2
    level = lax.broadcasted_iota(jnp.int32, (order, 128), 0)

    def both(value):
        turn = pltpu.roll(value, 64, 1)
        return jnp.where(half_lane, value, turn), jnp.where(half_lane, turn, value)

    def factors(current, pair):
        one, two = 2 * pair, 2 * pair + 1
        col0, col1 = both(current)
        d0, e0 = col0[one:two], col1[one:two]
        inv0 = 1.0 / d0
        ratio = e0 * inv0
        inv1 = 1.0 / (col1[two : two + 1] - ratio * e0)
        fac0 = jnp.where(level == one, 0.0, col0 * inv0)
        fac1 = jnp.where(level == two, 0.0, (col1 - fac0 * e0) * inv1)
        return fac0, fac1, ratio, inv0, inv1

    def eliminated(block, pair, fac0, fac1, ratio):
        at = block * order
        row0 = system[at + 2 * pair : at + 2 * pair + 1, :]
        row1 = system[at + 2 * pair + 1 : at + 2 * pair + 2, :] - ratio * row0
        return system[at : at + order, :] - fac0 * row0 - fac1 * row1

    inverses = []
    fac0, fac1, ratio, inv0, inv1 = factors(system[0:order, :], 0)
    for pair in range(blocks):
        inverses += [inv0, inv1]
        ahead = eliminated(pair + 1, pair, fac0, fac1, ratio)
        if pair + 1 < blocks:
            later = factors(ahead, pair + 1)
        for block in range(pair + 2, blocks + 1):
            system[block * order : (block + 1) * order, :] = eliminated(
                block, pair, fac0, fac1, ratio
            )
        if pair + 1 < blocks:
            fac0, fac1, ratio, inv0, inv1 = later
    solved = ahead * jnp.concatenate(inverses, axis=0)
    sums = jnp.sum(solved, axis=0, keepdims=True)
    share = sums / pltpu.roll(sums, 64, 1)
    coef = (solved - pltpu.roll(solved, 64, 1) * share)[:, :members]
    coef = coef - jnp.mean(coef, axis=0, keepdims=True)
    names = lax.broadcasted_iota(jnp.int32, (everyone, members), 0)
    mixing = jnp.zeros((everyone, members), F32)
    for i in range(order):
        mixing = jnp.where(names == near_turned[i : i + 1, :members], coef[i : i + 1], mixing)

    cells = updated.shape[1]
    inside = slice(EDGE - HALO, EDGE + cells + HALO)
    sources = jnp.concatenate([ext[g][inside] for g in range(groups)], axis=1)
    field = ext[group][inside] + jnp.dot(
        sources, mixing, precision=lax.Precision.HIGHEST, preferred_element_type=F32
    )
    updated[...] = field[HALO : HALO + cells].T
    run = cells // PARTS
    lane = lax.broadcasted_iota(jnp.int32, (1, PARTS * members), 1)
    left = jnp.where((lane < members) & (space == 0), 0.0, 1.0)
    right = jnp.where((lane >= (PARTS - 1) * members) & (space == spaces - 1), 0.0, 1.0)
    layers(in_runs(field), run, left, right, taps1, taps2, columns, first, second, heads)
    for q in range(PARTS):
        turned[q * run : (q + 1) * run, :] = heads[:, q * members : (q + 1) * members]
    new_heads[...] = turned[...].T


def on_device(
    log_field, obs_heads, obs_var, obs_noise, obs_index, obs_count, neighbours,
    lift_gain, lift_bias, conv_first, bias_first, conv_second, bias_second, readout,
):
    members, cells = log_field.shape
    spaces = lax.axis_size("space")
    channels = lift_gain.shape[0]
    slots = obs_var.shape[0]
    order = neighbours.shape[1]
    low, high = call(
        edges_kernel, (shape((EDGE, members)), shape((EDGE, members))), (log_field,)
    )
    forward = [(i, i + 1) for i in range(spaces - 1)]
    backward = [(i + 1, i) for i in range(spaces - 1)]
    from_left = lax.ppermute(high, "space", forward)
    from_right = lax.ppermute(low, "space", backward)

    def work(run, parts):
        rows, lanes = run + 2 * HALO, parts * members
        return (
            pltpu.VMEM((rows, channels, lanes), BF16),
            pltpu.VMEM((rows - 2, channels, lanes), BF16),
            pltpu.VMEM((max(run, 8), lanes), F32),
        )

    taps1, taps2, columns, near, near_turned, own, inner = call(
        prepare_kernel,
        (
            shape((channels, 3 * channels), BF16),
            shape((channels + 16, 6 * channels), BF16),
            shape((5, channels, 128)),
            shape((2 * members, 2 * order), jnp.int32),
            shape((2 * order, members), jnp.int32),
            shape((cells, members)),
            shape((cells, members)),
        ),
        (
            log_field, lift_gain, lift_bias, conv_first, bias_first, conv_second, bias_second,
            readout, neighbours,
        ),
        scratch=(
            pltpu.VMEM((channels, 3 * channels), F32),
            pltpu.VMEM((channels + 16, 6 * channels), F32),
        )
        + work(cells // PARTS, PARTS),
        flops=1 << 29,
    )
    sent, ext = call(
        observe_kernel,
        (shape((spaces, slots, 2 * members)), shape((2 * EDGE + cells, members))),
        (
            own, inner, from_left, from_right, taps1, taps2, columns,
            obs_heads, obs_var, obs_noise, obs_index, obs_count,
        ),
        in_specs=[VMEM] * 10 + [SMEM] * 2,
        scratch=work(HALO, 2)
        + (pltpu.VMEM((cells, members), F32), pltpu.VMEM((slots, members), F32)),
    )
    got = lax.all_to_all(sent, "space", 0, 0)
    got, ext = lax.all_gather((got, ext), "members", axis=0, tiled=False)
    return call(
        update_kernel,
        (shape((members, cells)), shape((members, cells))),
        (got, ext, taps1, taps2, columns, near, near_turned),
        scratch=(pltpu.VMEM(((order // 2 + 1) * order, 128), F32),)
        + work(cells // PARTS, PARTS)
        + (pltpu.VMEM((cells, members), F32),),
    )


def solution(mesh):
    in_specs = (
        P("members", "space"),
        P("space"),
        P("space"),
        P("members", "space"),
        P("space", None),
        P("space"),
        P("members", None),
        P(),
        P(),
        P(),
        P(),
        P(),
        P(),
        P(),
    )
    out_specs = (P("members", "space"), P("members", "space"))
    return jax.shard_map(
        on_device, mesh=mesh, in_specs=in_specs, out_specs=out_specs, check_vma=False
    )
```

time: 59.6 us -> 44.8 us (0.75)
  blocking collectives: 20.3 us -> 4.07 us
  Pallas kernels: 27.5 us -> 14 us
  starting transfers between devices: 6.03 us -> 14.1 us
  waiting for transfers between devices: 2.6 us -> 7.37 us
  local copies, waits for them, and re-layouts: 1.36 us -> 3.26 us
    all_to_all x1 -> x0, blocking collectives: 16 us -> none  [on_device(): got = lax.all_to_all(sent, 'space', 0, 0)]
    pallas_call x4, Pallas kernels: 27.5 us -> 14 us  [call(): pl.pallas_call(kernel, out_shape=outs, in_specs=in_specs or [VMEM] * len(...]
    all_to_all x0 -> x1, starting transfers between devices: none -> 7.88 us  [on_device(): got = lax.all_to_all(sent, 'space', 0, 0)]
    all_to_all x0 -> x1, waiting for transfers between devices: none -> 7.22 us  [on_device(): got = lax.all_to_all(sent, 'space', 0, 0)]
    ppermute x1, waiting for transfers between devices: 2.6 us -> 0.15 us  [on_device(): from_right = lax.ppermute(low, 'space', backward)]
    unnamed x27 -> x28, local copies, waits for them, and re-layouts: 1.36 us -> 3.16 us
  transfers between devices with their start and end apart: 2 -> 3, of which waited for: 1 -> 2; matrix products, arithmetic and copies ran while one was open for 0% -> 1% of each run, Pallas kernels for 0% -> 4%
where the time goes in v2:
time: 44.8 us; the launch traced here: 44.3 us
  starting transfers between devices  14.1 us (31%)
  Pallas kernels  14 us (31%)
  waiting for transfers between devices  7.37 us (16%)
  blocking collectives  4.07 us (9%)
  local copies, waits for them, and re-layouts  3.26 us (7%)
  between operations  1.46 us (3%)
    pallas_call x4, Pallas kernels, call(): pl.pallas_call(kernel, out_shape=outs, in_specs=in_specs or [VMEM] * len(...  14 us
    all_to_all x1, starting transfers between devices, on_device(): got = lax.all_to_all(sent, 'space', 0, 0)  7.88 us
    all_to_all x1, waiting for transfers between devices, on_device(): got = lax.all_to_all(sent, 'space', 0, 0)  7.22 us
    ppermute x1, starting transfers between devices, on_device(): from_left = lax.ppermute(high, 'space', forward)  4.97 us
    all_gather x2, blocking collectives, on_device(): got, ext = lax.all_gather((got, ext), 'members', axis=0, tiled=False)  4.07 us
    unnamed x28, local copies, waits for them, and re-layouts  3.16 us
    ppermute x1, starting transfers between devices, on_device(): from_right = lax.ppermute(low, 'space', backward)  1.29 us
  transfers between devices with their start and end apart: 3, of which 2 were waited for; matrix products, arithmetic and copies ran while one was open for 1% of the time, Pallas kernels for 4%

profile of v2, /device:TPU:0, one launch (start us, length us, event | category | flops | bytes accessed | tf_op | source)
XLA Modules:
  0.0 44.3 jit_solution(12748822854894013479)
XLA Ops:
  0.6 0.7 %copy-done = f32[64,128]{1,0:T(8,128)S(1)} copy-done((f32[64,128]{1,0:T(8,128)S(1)}, f32[64,128]{1,0:T(8,128)}, u32[]{:S(2)}) %copy-start) | copy-done | bytes 32792
  1.4 0.1 shard_map.150
  1.5 0.0 copy-start.10
  1.5 0.0 copy-start.11
  1.5 0.0 copy-start.8
  1.5 0.0 copy-start.9
  1.5 5.0 %collective-permute-start = (f32[8,64]{1,0:T(8,128)S(1)}, f32[8,64]{1,0:T(8,128)S(1)}, u32[]{:S(2)}, u32[]{:S(2)}) collective-permute-start(f32[8,64]{1,0:T(8,128)S(1)} %get-tuple-element.15), channel_id=1, source_target_pairs={{0,2},{2,4},{4,6},{6,8},{8,10},{10,12},{12,14},{14,16},{16,18},{18... | collective-permute-start | bytes 6152 | tf_op jit(solution)/shard_map/ppermute | solution.py:325
  6.5 1.3 %collective-permute-start.1 = (f32[8,64]{1,0:T(8,128)S(1)}, f32[8,64]{1,0:T(8,128)S(1)}, u32[]{:S(2)}, u32[]{:S(2)}) collective-permute-start(f32[8,64]{1,0:T(8,128)S(1)} %get-tuple-element.16), channel_id=1, source_target_pairs={{2,0},{4,2},{6,4},{8,6},{10,8},{12,10},{14,12},{16,14},{18,16},{20... | collective-permute-start | bytes 6152 | tf_op jit(solution)/shard_map/ppermute | solution.py:326
  7.9 0.8 %copy-done.4 = bf16[3,48,48]{2,1,0:T(8,128)(2,1)S(1)} copy-done((bf16[3,48,48]{2,1,0:T(8,128)(2,1)S(1)}, bf16[3,48,48]{2,1,0:T(8,128)(2,1)}, u32[]{:S(2)}) %copy-start.4) | copy-done | bytes 13848
  8.6 0.8 %copy-done.5 = bf16[3,48,96]{2,1,0:T(8,128)(2,1)S(1)} copy-done((bf16[3,48,96]{2,1,0:T(8,128)(2,1)S(1)}, bf16[3,48,96]{2,1,0:T(8,128)(2,1)}, u32[]{:S(2)}) %copy-start.5) | copy-done | bytes 27672
  9.4 1.7 %shard_map.149 = (bf16[48,144]{1,0:T(8,128)(2,1)S(1)}, bf16[64,288]{1,0:T(8,128)(2,1)S(1)}, f32[5,48,128]{2,1,0:T(8,128)S(1)}, s32[128,128]{1,0:T(8,128)S(1)}, s...) custom-call(f32[64,128]{1,0:T(8,128)S(1)} %copy-done, f32[48]{0:T(128)S(1)} %copy-done.7, ...), custom_call_target="tpu_custom_call" | custom-call | flops 536870912 | bytes 262144 | tf_op jit(solution)/shard_map/pallas_call | solution.py:22
  11.1 0.1 copy.17.obs_noise
  11.9 0.1 collective-permute-done.1.from_right
  12.0 0.6 %copy-done.1 = f32[32]{0:T(128)S(1)} copy-done((f32[32]{0:T(128)S(1)}, f32[32]{0:T(128)}, u32[]{:S(2)}) %copy-start.1) | copy-done | bytes 152
  12.7 0.0 copy-done.2
  12.7 0.0 copy-done.3
  12.7 2.0 %shard_map.151 = (f32[16,32,128]{2,1,0:T(8,128)}, f32[144,64]{1,0:T(8,128)S(1)}) custom-call(f32[128,64]{1,0:T(8,128)S(1)} %get-tuple-element.13.own, f32[128,64]{1,0:T(8,128)S(1)} %get-tuple-element.14.inner, f32[8,64]{1,0:T(8,128)S(1)} %collective-permute-done.from_left, f32[8,64]{1,0:T(8,128)S(1)} %collective-permute-done.1.from_right, ...), custom_call_target="tpu_custom_call" | custom-call | bytes 262144 | tf_op jit(solution)/shard_map/pallas_call | solution.py:22
  14.7 7.9 %all-to-all-start = ((f32[16,32,128]{2,1,0:T(8,128)}), f32[16,32,128]{2,1,0:T(8,128)S(1)}, u32[]{:S(2)}, u32[]{:S(2)}) async-start(f32[16,32,128]{2,1,0:T(8,128)} %get-tuple-element.20), calls=%async_computation | async-start | bytes 524288 | tf_op jit(solution)/shard_map/all_to_all | solution.py:369
  22.5 0.1 copy.18
  22.6 1.9 %all-gather.2 = f32[2,144,64]{1,2,0:T(8,128)S(1)} all-gather(f32[1,144,64]{1,2,0:T(8,128)S(1)} %copy.18), channel_id=3, replica_groups=mesh['space'=16,'members'=2] {'members'}, dimensions={0}, use_global_device_ids=true | all-gather | bytes 110592 | tf_op jit(solution)/shard_map/all_gather | solution.py:370
  24.5 0.1 copy.19.ext
  24.6 7.2 %all-to-all-done = f32[16,32,128]{2,1,0:T(8,128)S(1)} async-done(((f32[16,32,128]{2,1,0:T(8,128)}), f32[16,32,128]{2,1,0:T(8,128)S(1)}, u32[]{:S(2)}, u32[]{:S(2)}) %all-to-all-start) | async-done | bytes 262176 | tf_op jit(solution)/shard_map/all_to_all | solution.py:369
  31.9 2.2 %all-gather = f32[32,32,128]{2,1,0:T(8,128)S(1)} all-gather(f32[16,32,128]{2,1,0:T(8,128)S(1)} %all-to-all-done), channel_id=2, replica_groups=mesh['space'=16,'members'=2] {'members'}, dimensions={0}, use_global_device_ids=true | all-gather | bytes 786432 | tf_op jit(solution)/shard_map/all_gather | solution.py:370
  34.0 10.3 %shard_map.152 = (f32[64,128]{1,0:T(8,128)}, f32[64,128]{1,0:T(8,128)}) custom-call(f32[2,16,32,128]{3,2,1,0:T(8,128)S(1)} %bitcast.2, f32[2,144,64]{2,1,0:T(8,128)S(1)} %copy.19.ext, bf16[48,144]{1,0:T(8,128)(2,1)S(1)} %get-tuple-element.17.taps1, bf16[64,288]{1,0:T(8,128)(2,1)S(1)} %get-tuple-element.18.taps2, ...), custom_call_target="tpu_custom_call" | custom-call | bytes 262144 | tf_op jit(solution)/shard_map/pallas_call | solution.py:22
  (17 shorter events, 0.0 us)
Async XLA Ops:
  0.6 0.8 %copy-start = (f32[64,128]{1,0:T(8,128)S(1)}, f32[64,128]{1,0:T(8,128)}, u32[]{:S(2)}) copy-start(f32[64,128]{1,0:T(8,128)} %field.3) | copy-start | bytes 98308
  1.4 6.4 %copy-start.6 = (s32[64,64]{1,0:T(8,128)S(1)}, s32[64,64]{1,0:T(8,128)}, u32[]{:S(2)}) copy-start(s32[64,64]{1,0:T(8,128)} %neighbours.1) | copy-start | bytes 49156
  1.5 6.4 %copy-start.10 = (f32[48]{0:T(128)S(1)}, f32[48]{0:T(128)}, u32[]{:S(2)}) copy-start(f32[48]{0:T(128)} %bias2.1) | copy-start | bytes 580
  1.5 6.4 %copy-start.11 = (bf16[144]{0:T(256)(128)(2,1)S(1)}, bf16[144]{0:T(256)(128)(2,1)}, u32[]{:S(2)}) copy-start(bf16[144]{0:T(256)(128)(2,1)} %readout.1) | copy-start | bytes 868
  1.5 6.4 %copy-start.7 = (f32[48]{0:T(128)S(1)}, f32[48]{0:T(128)}, u32[]{:S(2)}) copy-start(f32[48]{0:T(128)} %gain.1) | copy-start | bytes 580
  1.5 6.3 %copy-start.8 = (f32[48]{0:T(128)S(1)}, f32[48]{0:T(128)}, u32[]{:S(2)}) copy-start(f32[48]{0:T(128)} %bias.1) | copy-start | bytes 580
  1.5 6.3 %copy-start.9 = (f32[48]{0:T(128)S(1)}, f32[48]{0:T(128)}, u32[]{:S(2)}) copy-start(f32[48]{0:T(128)} %bias1.1) | copy-start | bytes 580
  1.5 10.3 %collective-permute-start = (f32[8,64]{1,0:T(8,128)S(1)}, f32[8,64]{1,0:T(8,128)S(1)}, u32[]{:S(2)}, u32[]{:S(2)}) collective-permute-start(f32[8,64]{1,0:T(8,128)S(1)} %get-tuple-element.15), channel_id=1, source_target_pairs={{0,2},{2,4},{4,6},{6,8},{8,10},{10,12},{12,14},{14,16},{16,18},{18... | collective-permute-start | bytes 6152 | tf_op jit(solution)/shard_map/ppermute | solution.py:325
  6.5 5.5 %collective-permute-start.1 = (f32[8,64]{1,0:T(8,128)S(1)}, f32[8,64]{1,0:T(8,128)S(1)}, u32[]{:S(2)}, u32[]{:S(2)}) collective-permute-start(f32[8,64]{1,0:T(8,128)S(1)} %get-tuple-element.16), channel_id=1, source_target_pairs={{2,0},{4,2},{6,4},{8,6},{10,8},{12,10},{14,12},{16,14},{18,16},{20... | collective-permute-start | bytes 6152 | tf_op jit(solution)/shard_map/ppermute | solution.py:326
  7.9 0.8 %copy-start.4 = (bf16[3,48,48]{2,1,0:T(8,128)(2,1)S(1)}, bf16[3,48,48]{2,1,0:T(8,128)(2,1)}, u32[]{:S(2)}) copy-start(bf16[3,48,48]{2,1,0:T(8,128)(2,1)} %conv1.1) | copy-start | bytes 41476
  8.6 0.8 %copy-start.5 = (bf16[3,48,96]{2,1,0:T(8,128)(2,1)S(1)}, bf16[3,48,96]{2,1,0:T(8,128)(2,1)}, u32[]{:S(2)}) copy-start(bf16[3,48,96]{2,1,0:T(8,128)(2,1)} %conv2.1) | copy-start | bytes 82948
  9.4 1.7 %copy-start.12 = (f32[64,32]{0,1:T(8,128)S(1)}, f32[64,32]{0,1:T(8,128)}, u32[]{:S(2)}) copy-start(f32[64,32]{0,1:T(8,128)} %param.17) | copy-start | bytes 24580
  12.0 0.7 %copy-start.1 = (f32[32]{0:T(128)S(1)}, f32[32]{0:T(128)}, u32[]{:S(2)}) copy-start(f32[32]{0:T(128)} %obs_heads.1) | copy-start | bytes 388
  12.0 0.7 %copy-start.2 = (f32[32]{0:T(128)S(1)}, f32[32]{0:T(128)}, u32[]{:S(2)}) copy-start(f32[32]{0:T(128)} %obs_var.1) | copy-start | bytes 388
  12.0 0.7 %copy-start.3 = (s32[1,32]{1,0:T(1,128)S(1)}, s32[1,32]{1,0:T(1,128)}, u32[]{:S(2)}) copy-start(s32[1,32]{1,0:T(1,128)} %obs_index.1) | copy-start | bytes 388
  14.7 17.2 %all-to-all-start = ((f32[16,32,128]{2,1,0:T(8,128)}), f32[16,32,128]{2,1,0:T(8,128)S(1)}, u32[]{:S(2)}, u32[]{:S(2)}) async-start(f32[16,32,128]{2,1,0:T(8,128)} %get-tuple-element.20), calls=%async_computation | async-start | bytes 524288 | tf_op jit(solution)/shard_map/all_to_all | solution.py:369

commit v3 on v2

--- a/solution.py
+++ b/solution.py
@@ -1,3 +1,5 @@
+import functools
+
 import jax
 import jax.numpy as jnp
 from jax import lax
@@ -11,18 +13,17 @@
 EDGE = 8
 PARTS = 4
 VMEM = pl.BlockSpec(memory_space=pltpu.VMEM)
-SMEM = pl.BlockSpec(memory_space=pltpu.SMEM)
 
 
 def shape(dims, dtype=F32):
     return jax.ShapeDtypeStruct(dims, dtype)
 
 
-def call(kernel, outs, args, in_specs=None, scratch=(), flops=0, limit=40):
+def call(kernel, outs, args, scratch=(), flops=0, limit=40):
     return pl.pallas_call(
         kernel,
         out_shape=outs,
-        in_specs=in_specs or [VMEM] * len(args),
+        in_specs=[VMEM] * len(args),
         out_specs=jax.tree.map(lambda _: VMEM, outs),
         scratch_shapes=list(scratch),
         cost_estimate=pl.CostEstimate(flops=flops, bytes_accessed=1 << 18, transcendentals=0),
@@ -36,12 +37,6 @@
         jnp.int32, (size, size), 1
     )
     return jnp.sum(jnp.where(same, row, 0.0), axis=1, keepdims=True)
-
-
-def edges_kernel(field, low, high):
-    value = field[...].T
-    low[...] = value[:EDGE]
-    high[...] = value[value.shape[0] - EDGE :]
 
 
 def layers(wide, run, left, right, taps1, taps2, columns, first, second, heads):
@@ -85,11 +80,30 @@
     return jnp.concatenate([ext[q * run : (q + 1) * run + 2 * HALO] for q in range(PARTS)], axis=1)
 
 
+def split3(value):
+    one = value.astype(BF16)
+    rest = value - one.astype(F32)
+    two = rest.astype(BF16)
+    three = (rest - two.astype(F32)).astype(BF16)
+    return jnp.concatenate([one, two, three], axis=1)
+
+
+def edges_kernel(field, low, high, own):
+    turned = field[...].T
+    cells = turned.shape[0]
+    own[...] = turned
+    low[...] = turned[:EDGE]
+    high[...] = turned[cells - EDGE :]
+
+
 def prepare_kernel(
-    field, gain, bias, conv1, bias1, conv2, bias2, readout, neighbours,
-    taps1, taps2, columns, near, near_turned, own, inner,
+    own, gain, bias, conv1, bias1, conv2, bias2, readout, neighbours,
+    obs_heads, obs_var, noise_turned, obs_index, obs_count,
+    taps1, taps2, columns, near, near_turned, chosen, goal, inner,
     wide1, wide2, first, second, heads,
 ):
+    turned = own[...]
+    cells, members = turned.shape
     channels = gain.shape[0]
     split = 3 * channels
     row = readout[...].astype(F32).reshape(1, split)
@@ -115,25 +129,34 @@
     ]
     for spot, value in enumerate(rows):
         columns[spot] = jnp.broadcast_to(column(value), (channels, columns.shape[2]))
-    ids = neighbours[...]
+    everyone = members * lax.axis_size("members")
+    ids = neighbours[...] - members * lax.axis_index("members")
+    ids = jnp.where(ids < 0, ids + everyone, ids)
     pair = jnp.concatenate([ids, ids], axis=1)
     near[...] = jnp.concatenate([pair, pair], axis=0)
     near_turned[...] = pair.T
-    turned = field[...].T
-    own[...] = turned
-    members = turned.shape[1]
+    slots = obs_var.shape[0]
+    cell = column(obs_index[...].astype(F32)).astype(jnp.int32)
+    chosen[...] = jnp.where(
+        lax.broadcasted_iota(jnp.int32, (slots, cells), 1) == cell, 1.0, 0.0
+    ).astype(BF16)
+    target = column(obs_heads[...].reshape(1, slots))
+    variance = column(obs_var[...].reshape(1, slots))
+    live = lax.broadcasted_iota(jnp.int32, (slots, 1), 0) < obs_count[...].reshape(1, 1)
+    root = jnp.where(live, lax.rsqrt(variance), 0.0)
+    wanted = root * (target + jnp.sqrt(variance) * noise_turned[...])
+    goal[...] = jnp.concatenate([jnp.broadcast_to(root, (slots, members)), wanted], axis=1)
     zeros = jnp.zeros((HALO, members), F32)
     wide = in_runs(jnp.concatenate([zeros, turned, zeros], axis=0))
-    run = turned.shape[0] // PARTS
+    run = cells // PARTS
     layers(wide, run, None, None, taps1, taps2, columns, first, second, heads)
     for q in range(PARTS):
         inner[q * run : (q + 1) * run, :] = heads[:, q * members : (q + 1) * members]
 
 
 def observe_kernel(
-    own, inner, from_left, from_right, taps1, taps2, columns,
-    obs_heads, obs_var, obs_noise, obs_index, obs_count,
-    sent, ext, first, second, heads, turned, chosen,
+    own, inner, from_left, from_right, taps1, taps2, columns, chosen, goal,
+    sent, ext, first, second, heads,
 ):
     space = lax.axis_index("space")
     spaces = lax.axis_size("space")
@@ -142,36 +165,25 @@
     ext[EDGE : EDGE + cells, :] = own[...]
     ext[EDGE + cells :, :] = from_right[...]
     ends = jnp.concatenate(
-        [ext[EDGE - HALO : EDGE + 2 * HALO, :], ext[EDGE + cells - 2 * HALO : EDGE + cells + HALO, :]],
+        [
+            jnp.concatenate([from_left[EDGE - HALO :, :], own[0 : 2 * HALO, :]], axis=0),
+            jnp.concatenate([own[cells - 2 * HALO :, :], from_right[0:HALO, :]], axis=0),
+        ],
         axis=1,
     )
     lane = lax.broadcasted_iota(jnp.int32, (1, 2 * members), 1)
     left = jnp.where((lane < members) & (space == 0), 0.0, 1.0)
     right = jnp.where((lane >= members) & (space == spaces - 1), 0.0, 1.0)
     layers(ends, HALO, left, right, taps1, taps2, columns, first, second, heads)
-    turned[...] = inner[...]
-    turned[0:HALO, :] = heads[0:HALO, :members]
-    turned[cells - HALO :, :] = heads[0:HALO, members:]
-    slots = obs_var.shape[0]
-    for k in range(slots):
-        chosen[k : k + 1, :] = turned[pl.ds(obs_index[0, k], 1), :]
-    own_obs = chosen[...]
-    target = column(obs_heads[...].reshape(1, slots))
-    variance = column(obs_var[...].reshape(1, slots))
-    live = lax.broadcasted_iota(jnp.int32, (slots, 1), 0) < obs_count[0]
-    root = jnp.where(live, lax.rsqrt(variance), 0.0)
-    innovation = target + jnp.sqrt(variance) * obs_noise[...].T - own_obs
-    payload = jnp.concatenate([root * own_obs, root * innovation], axis=1)
+    every = jnp.concatenate(
+        [heads[0:HALO, :members], inner[HALO : cells - HALO, :], heads[0:HALO, members:]], axis=0
+    )
+    parts = jnp.dot(chosen[...], split3(every), preferred_element_type=F32)
+    seen = parts[:, :members] + parts[:, members : 2 * members] + parts[:, 2 * members :]
+    weighted = goal[:, :members] * seen
+    payload = jnp.concatenate([weighted, goal[:, members:] - weighted], axis=1)
     for copy in range(sent.shape[0]):
         sent[copy] = payload
-
-
-def split3(value):
-    one = value.astype(BF16)
-    rest = value - one.astype(F32)
-    two = rest.astype(BF16)
-    three = (rest - two.astype(F32)).astype(BF16)
-    return jnp.concatenate([one, two, three], axis=1)
 
 
 def lane_gather(table, index):
@@ -186,25 +198,25 @@
     return found
 
 
-def update_kernel(
-    got, ext, taps1, taps2, columns, near, near_turned,
-    updated, new_heads,
-    system, first, second, heads, turned,
-):
+def update_kernel(groups, *refs):
+    gots, exts = refs[:groups], refs[groups : 2 * groups]
+    (
+        taps1, taps2, columns, near, near_turned,
+        updated, new_heads,
+        system, first, second, heads, turned,
+    ) = refs[2 * groups :]
     space = lax.axis_index("space")
     spaces = lax.axis_size("space")
-    group = lax.axis_index("members")
-    groups, slots = got.shape[0], got.shape[1] * got.shape[2]
-    members = got.shape[3] // 2
+    slots = gots[0].shape[0] * gots[0].shape[1]
+    members = gots[0].shape[2] // 2
     everyone = groups * members
     order = near.shape[0] // 2
     half_lane = lax.broadcasted_iota(jnp.int32, (1, 128), 1) < 64
 
-    panel = jnp.concatenate(
-        [got[g].reshape(slots, 2 * members)[:, :members] for g in range(groups)], axis=1
-    )
+    whole = [got[...].reshape(slots, 2 * members) for got in gots]
+    panel = jnp.concatenate([rows[:, :members] for rows in whole], axis=1)
     panel = panel - jnp.mean(panel, axis=1, keepdims=True)
-    innovation = got[group].reshape(slots, 2 * members)[:, members:]
+    innovation = whole[0][:, members:]
     stacked = jnp.concatenate([panel, innovation], axis=1)
     product = lax.dot_general(
         stacked, panel, (((0,), (0,)), ((), ())),
@@ -245,43 +257,51 @@
     system[order // 2 * order : (order // 2 + 1) * order, :] = side
 
     blocks = order // 2
-    level = lax.broadcasted_iota(jnp.int32, (order, 128), 0)
-
     def both(value):
         turn = pltpu.roll(value, 64, 1)
         return jnp.where(half_lane, value, turn), jnp.where(half_lane, turn, value)
 
-    def factors(current, pair):
+    def without(value, pair):
+        at = 2 * pair // 8 * 8
+        row = lax.broadcasted_iota(jnp.int32, (8, 128), 0) + at
+        tile = jnp.where((row >= 2 * pair) & (row < 2 * pair + 2), 0.0, value[at : at + 8])
+        parts = [value[:at], tile, value[at + 8 :]]
+        return jnp.concatenate([part for part in parts if part.shape[0]], axis=0)
+
+    def factors(col0, col1, pair):
         one, two = 2 * pair, 2 * pair + 1
-        col0, col1 = both(current)
-        d0, e0 = col0[one:two], col1[one:two]
-        inv0 = 1.0 / d0
-        ratio = e0 * inv0
-        inv1 = 1.0 / (col1[two : two + 1] - ratio * e0)
-        fac0 = jnp.where(level == one, 0.0, col0 * inv0)
-        fac1 = jnp.where(level == two, 0.0, (col1 - fac0 * e0) * inv1)
-        return fac0, fac1, ratio, inv0, inv1
-
-    def eliminated(block, pair, fac0, fac1, ratio):
-        at = block * order
-        row0 = system[at + 2 * pair : at + 2 * pair + 1, :]
-        row1 = system[at + 2 * pair + 1 : at + 2 * pair + 2, :] - ratio * row0
-        return system[at : at + order, :] - fac0 * row0 - fac1 * row1
-
-    inverses = []
-    fac0, fac1, ratio, inv0, inv1 = factors(system[0:order, :], 0)
+        d, e, f = col0[one:two], col1[one:two], col1[two : two + 1]
+        inv = 1.0 / (d * f - e * e)
+        fac0 = without((col0 * f - col1 * e) * inv, pair)
+        fac1 = without((col1 * d - col0 * e) * inv, pair)
+        return fac0, fac1, (f * inv, d * inv, e * inv)
+
+    own_share, cross_share = [], []
+    fac0, fac1, shares = factors(*both(system[0:order, :]), 0)
     for pair in range(blocks):
-        inverses += [inv0, inv1]
-        ahead = eliminated(pair + 1, pair, fac0, fac1, ratio)
+        own_share += [shares[0], shares[1]]
+        cross_share += [shares[2], shares[2]]
+        one, two = 2 * pair, 2 * pair + 1
         if pair + 1 < blocks:
-            later = factors(ahead, pair + 1)
-        for block in range(pair + 2, blocks + 1):
-            system[block * order : (block + 1) * order, :] = eliminated(
-                block, pair, fac0, fac1, ratio
+            col0, col1 = both(system[(pair + 1) * order : (pair + 2) * order, :])
+            later = factors(
+                col0 - fac0 * col0[one:two] - fac1 * col0[two : two + 1],
+                col1 - fac0 * col1[one:two] - fac1 * col1[two : two + 1],
+                pair + 1,
             )
+        for block in range(min(pair + 2, blocks), blocks + 1):
+            at = block * order
+            row0 = system[at + one : at + two, :]
+            row1 = system[at + two : at + two + 1, :]
+            system[at : at + order, :] = system[at : at + order, :] - fac0 * row0 - fac1 * row1
         if pair + 1 < blocks:
-            fac0, fac1, ratio, inv0, inv1 = later
-    solved = ahead * jnp.concatenate(inverses, axis=0)
+            fac0, fac1, shares = later
+    sides = system[blocks * order :, :]
+    even = lax.broadcasted_iota(jnp.int32, (order, 128), 0) % 2 == 0
+    partner = jnp.where(even, pltpu.roll(sides, order - 1, 0), pltpu.roll(sides, 1, 0))
+    solved = sides * jnp.concatenate(own_share, axis=0) - partner * jnp.concatenate(
+        cross_share, axis=0
+    )
     sums = jnp.sum(solved, axis=0, keepdims=True)
     share = sums / pltpu.roll(sums, 64, 1)
     coef = (solved - pltpu.roll(solved, 64, 1) * share)[:, :members]
@@ -293,8 +313,8 @@
 
     cells = updated.shape[1]
     inside = slice(EDGE - HALO, EDGE + cells + HALO)
-    sources = jnp.concatenate([ext[g][inside] for g in range(groups)], axis=1)
-    field = ext[group][inside] + jnp.dot(
+    sources = jnp.concatenate([ext[inside, :] for ext in exts], axis=1)
+    field = exts[0][inside, :] + jnp.dot(
         sources, mixing, precision=lax.Precision.HIGHEST, preferred_element_type=F32
     )
     updated[...] = field[HALO : HALO + cells].T
@@ -308,22 +328,25 @@
     new_heads[...] = turned[...].T
 
 
+def from_groups(value):
+    groups = lax.axis_size("members")
+    found = [value]
+    for step in range(1, groups):
+        pairs = [((i + step) % groups, i) for i in range(groups)]
+        found.append(lax.ppermute(value, "members", pairs))
+    return found
+
+
 def on_device(
     log_field, obs_heads, obs_var, obs_noise, obs_index, obs_count, neighbours,
     lift_gain, lift_bias, conv_first, bias_first, conv_second, bias_second, readout,
 ):
     members, cells = log_field.shape
     spaces = lax.axis_size("space")
+    groups = lax.axis_size("members")
     channels = lift_gain.shape[0]
     slots = obs_var.shape[0]
     order = neighbours.shape[1]
-    low, high = call(
-        edges_kernel, (shape((EDGE, members)), shape((EDGE, members))), (log_field,)
-    )
-    forward = [(i, i + 1) for i in range(spaces - 1)]
-    backward = [(i + 1, i) for i in range(spaces - 1)]
-    from_left = lax.ppermute(high, "space", forward)
-    from_right = lax.ppermute(low, "space", backward)
 
     def work(run, parts):
         rows, lanes = run + 2 * HALO, parts * members
@@ -333,7 +356,17 @@
             pltpu.VMEM((max(run, 8), lanes), F32),
         )
 
-    taps1, taps2, columns, near, near_turned, own, inner = call(
+    low, high, own = call(
+        edges_kernel,
+        (shape((EDGE, members)), shape((EDGE, members)), shape((cells, members))),
+        (log_field,),
+        flops=1 << 34,
+    )
+    forward = [(i, i + 1) for i in range(spaces - 1)]
+    backward = [(i + 1, i) for i in range(spaces - 1)]
+    from_left = lax.ppermute(high, "space", forward)
+    from_right = lax.ppermute(low, "space", backward)
+    taps1, taps2, columns, near, near_turned, chosen, goal, inner = call(
         prepare_kernel,
         (
             shape((channels, 3 * channels), BF16),
@@ -341,12 +374,13 @@
             shape((5, channels, 128)),
             shape((2 * members, 2 * order), jnp.int32),
             shape((2 * order, members), jnp.int32),
-            shape((cells, members)),
+            shape((slots, cells), BF16),
+            shape((slots, 2 * members)),
             shape((cells, members)),
         ),
         (
-            log_field, lift_gain, lift_bias, conv_first, bias_first, conv_second, bias_second,
-            readout, neighbours,
+            own, lift_gain, lift_bias, conv_first, bias_first, conv_second, bias_second,
+            readout, neighbours, obs_heads, obs_var, obs_noise.T, obs_index, obs_count,
         ),
         scratch=(
             pltpu.VMEM((channels, 3 * channels), F32),
@@ -358,20 +392,14 @@
     sent, ext = call(
         observe_kernel,
         (shape((spaces, slots, 2 * members)), shape((2 * EDGE + cells, members))),
-        (
-            own, inner, from_left, from_right, taps1, taps2, columns,
-            obs_heads, obs_var, obs_noise, obs_index, obs_count,
-        ),
-        in_specs=[VMEM] * 10 + [SMEM] * 2,
-        scratch=work(HALO, 2)
-        + (pltpu.VMEM((cells, members), F32), pltpu.VMEM((slots, members), F32)),
+        (own, inner, from_left, from_right, taps1, taps2, columns, chosen, goal),
+        scratch=work(HALO, 2),
     )
     got = lax.all_to_all(sent, "space", 0, 0)
-    got, ext = lax.all_gather((got, ext), "members", axis=0, tiled=False)
     return call(
-        update_kernel,
+        functools.partial(update_kernel, groups),
         (shape((members, cells)), shape((members, cells))),
-        (got, ext, taps1, taps2, columns, near, near_turned),
+        (*from_groups(got), *from_groups(ext), taps1, taps2, columns, near, near_turned),
         scratch=(pltpu.VMEM(((order // 2 + 1) * order, 128), F32),)
         + work(cells // PARTS, PARTS)
         + (pltpu.VMEM((cells, members), F32),),

time: 44.8 us -> 40.1 us (0.90)
  blocking collectives: 4.07 us -> 16 us
  starting transfers between devices: 14.1 us -> 6.64 us
  waiting for transfers between devices: 7.37 us -> 2.37 us
  Pallas kernels: 14 us -> 11.9 us
  local copies, waits for them, and re-layouts: 3.26 us -> 1.38 us
    all_to_all x0 -> x1, blocking collectives: none -> 16 us  [on_device(): got = lax.all_to_all(sent, 'space', 0, 0)]
    all_to_all x1 -> x0, starting transfers between devices: 7.88 us -> none  [on_device(): got = lax.all_to_all(sent, 'space', 0, 0)]
    all_to_all x1 -> x0, waiting for transfers between devices: 7.22 us -> none  [on_device(): got = lax.all_to_all(sent, 'space', 0, 0)]
    all_gather x2 -> x0, blocking collectives: 4.07 us -> none  [on_device(): got, ext = lax.all_gather((got, ext), 'members', axis=0, tiled=False)]
    pallas_call x4, Pallas kernels: 14 us -> 11.9 us  [call(): pl.pallas_call(kernel, out_shape=outs, in_specs=[VMEM] * len(args), out_s...]
    unnamed x28 -> x26, local copies, waits for them, and re-layouts: 3.16 us -> 1.38 us
    ppermute x0 -> x2, waiting for transfers between devices: none -> 1.13 us  [from_groups(): found.append(lax.ppermute(value, 'members', pairs))]
    ppermute x1, waiting for transfers between devices: 0.15 us -> 1.23 us  [on_device(): from_right = lax.ppermute(low, 'space', backward)]
  transfers between devices with their start and end apart: 3 -> 4, of which waited for: 2 -> 2; matrix products, arithmetic and copies ran while one was open for 1% -> 0% of each run, Pallas kernels for 4% -> 4%
where the time goes in v3:
time: 40.1 us; the launch traced here: 39.7 us
  blocking collectives  16 us (40%)
  Pallas kernels  11.9 us (30%)
  starting transfers between devices  6.64 us (17%)
  waiting for transfers between devices  2.37 us (6%)
  between operations  1.46 us (4%)
  local copies, waits for them, and re-layouts  1.38 us (3%)
    all_to_all x1, blocking collectives, on_device(): got = lax.all_to_all(sent, 'space', 0, 0)  16 us
    pallas_call x4, Pallas kernels, call(): pl.pallas_call(kernel, out_shape=outs, in_specs=[VMEM] * len(args), out_s...  11.9 us
    ppermute x1, starting transfers between devices, on_device(): from_left = lax.ppermute(high, 'space', forward)  4.84 us
    unnamed x26, local copies, waits for them, and re-layouts  1.38 us
    ppermute x1, starting transfers between devices, on_device(): from_right = lax.ppermute(low, 'space', backward)  1.29 us
    ppermute x1, waiting for transfers between devices, on_device(): from_right = lax.ppermute(low, 'space', backward)  1.23 us
    ppermute x2, waiting for transfers between devices, from_groups(): found.append(lax.ppermute(value, 'members', pairs))  1.13 us
  transfers between devices with their start and end apart: 4, of which 2 were waited for; matrix products, arithmetic and copies ran while one was open for 0% of the time, Pallas kernels for 4%

profile of v3, /device:TPU:0, one launch (start us, length us, event | category | flops | bytes accessed | tf_op | source)
XLA Modules:
  0.0 39.7 jit_solution(5245976644719690511)
XLA Ops:
  0.6 0.0 copy-start.1
  0.6 0.0 copy-start
  0.7 0.0 copy-start.2
  0.7 0.8 %copy-done.2 = f32[64,128]{1,0:T(8,128)S(1)} copy-done((f32[64,128]{1,0:T(8,128)S(1)}, f32[64,128]{1,0:T(8,128)}, u32[]{:S(2)}) %copy-start.2) | copy-done | bytes 32792
  1.4 0.0 copy-start.10
  1.5 0.1 shard_map.149
  1.6 4.8 %collective-permute-start = (f32[8,64]{1,0:T(8,128)S(1)}, f32[8,64]{1,0:T(8,128)S(1)}, u32[]{:S(2)}, u32[]{:S(2)}) collective-permute-start(f32[8,64]{1,0:T(8,128)S(1)} %get-tuple-element.17), channel_id=1, source_target_pairs={{0,2},{2,4},{4,6},{6,8},{8,10},{10,12},{12,14},{14,16},{16,18},{18... | collective-permute-start | bytes 6152 | tf_op jit(solution)/shard_map/ppermute | solution.py:367
  6.4 1.3 %collective-permute-start.1 = (f32[8,64]{1,0:T(8,128)S(1)}, f32[8,64]{1,0:T(8,128)S(1)}, u32[]{:S(2)}, u32[]{:S(2)}) collective-permute-start(f32[8,64]{1,0:T(8,128)S(1)} %get-tuple-element.18), channel_id=1, source_target_pairs={{2,0},{4,2},{6,4},{8,6},{10,8},{12,10},{14,12},{16,14},{18,16},{20... | collective-permute-start | bytes 6152 | tf_op jit(solution)/shard_map/ppermute | solution.py:368
  8.4 0.0 copy-start.5
  8.4 0.0 copy-start.6
  8.4 0.0 copy-start.7
  8.5 0.5 %copy-done.5 = f32[48]{0:T(128)S(1)} copy-done((f32[48]{0:T(128)S(1)}, f32[48]{0:T(128)}, u32[]{:S(2)}) %copy-start.5) | copy-done | bytes 216
  9.0 0.0 copy-done.6
  9.0 0.0 copy-done.7
  9.1 1.6 %shard_map.150 = (bf16[48,144]{1,0:T(8,128)(2,1)S(1)}, bf16[64,288]{1,0:T(8,128)(2,1)S(1)}, f32[5,48,128]{2,1,0:T(8,128)S(1)}, s32[128,128]{1,0:T(8,128)S(1)}, s...) custom-call(f32[128,64]{1,0:T(8,128)S(1)} %get-tuple-element.15.own, ...), custom_call_target="tpu_custom_call" | custom-call | flops 536870912 | bytes 262144 | tf_op jit(solution)/shard_map/pallas_call | solution.py:23
  10.7 0.0 collective-permute-done.from_left
  10.7 1.2 %collective-permute-done.1.from_right = f32[8,64]{1,0:T(8,128)S(1)} collective-permute-done((f32[8,64]{1,0:T(8,128)S(1)}, f32[8,64]{1,0:T(8,128)S(1)}, u32[]{:S(2)}, u32[]{:S(2)}) %collective-permute-start.1) | collective-permute-done | bytes 2080 | tf_op jit(solution)/shard_map/ppermute | solution.py:368
  11.9 0.9 %shard_map.151 = (f32[16,32,128]{2,1,0:T(8,128)S(1)}, f32[144,64]{1,0:T(8,128)S(1)}) custom-call(f32[128,64]{1,0:T(8,128)S(1)} %get-tuple-element.15.own, f32[128,64]{1,0:T(8,128)S(1)} %get-tuple-element.16.inner, f32[8,64]{1,0:T(8,128)S(1)} %collective-permute-done.from_left, f32[8,64]{1,0:T(8,128)S(1)} %collective-permute-done.1.from_right, ...), custom_call_target="tpu_custom_call" | custom-call | bytes 262144 | tf_op jit(solution)/shard_map/pallas_call | solution.py:23
  12.9 16.0 %all_to_all.5.refs_0_ = f32[16,32,128]{2,1,0:T(8,128)S(1)} all-to-all(f32[16,32,128]{2,1,0:T(8,128)S(1)} %get-tuple-element.24), channel_id=1, replica_groups=mesh['space'=16,'members'=2] {'space'}, dimensions={0} | all-to-all | bytes 524288 | tf_op jit(solution)/shard_map/all_to_all | solution.py:398
  28.8 0.0 collective-permute-start.2
  28.8 0.5 %collective-permute-start.3 = (f32[144,64]{1,0:T(8,128)S(1)}, f32[144,64]{1,0:T(8,128)S(1)}, u32[]{:S(2)}, u32[]{:S(2)}) collective-permute-start(f32[144,64]{1,0:T(8,128)S(1)} %get-tuple-element.25.refs_2_), channel_id=1, source_target_pairs={{1,0},{0,1},{3,2},{2,3},{5,4},{4,5},{7,6},{6,7},{9,8},{8,9},{11,10... | collective-permute-start | bytes 110600 | tf_op jit(solution)/shard_map/ppermute | solution.py:336
  29.3 1.1 %collective-permute-done.3.refs_3_ = f32[144,64]{1,0:T(8,128)S(1)} collective-permute-done((f32[144,64]{1,0:T(8,128)S(1)}, f32[144,64]{1,0:T(8,128)S(1)}, u32[]{:S(2)}, u32[]{:S(2)}) %collective-permute-start.3) | collective-permute-done | bytes 36896 | tf_op jit(solution)/shard_map/ppermute | solution.py:336
  30.5 0.0 collective-permute-done.2.refs_1_
  30.5 9.3 %shard_map.152 = (f32[64,128]{1,0:T(8,128)}, f32[64,128]{1,0:T(8,128)}) custom-call(f32[16,32,128]{2,1,0:T(8,128)S(1)} %all_to_all.5.refs_0_, f32[16,32,128]{2,1,0:T(8,128)S(1)} %collective-permute-done.2.refs_1_, f32[144,64]{1,0:T(8,128)S(1)} %get-tuple-element.25.refs_2_, f32[144,64]{1,0:T(8,128)S(1)} %collective-permute-done.3.refs_3_, ...), custom_call_target="tpu_custom_call" | custom-call | bytes 262144 | tf_op jit(solution)/shard_map/pallas_call | solution.py:23
  (15 shorter events, 0.0 us)
Async XLA Ops:
  0.6 7.8 %copy-start.1 = (bf16[3,48,96]{2,1,0:T(8,128)(2,1)S(1)}, bf16[3,48,96]{2,1,0:T(8,128)(2,1)}, u32[]{:S(2)}) copy-start(bf16[3,48,96]{2,1,0:T(8,128)(2,1)} %conv2.1) | copy-start | bytes 82948
  0.6 7.8 %copy-start = (bf16[3,48,48]{2,1,0:T(8,128)(2,1)S(1)}, bf16[3,48,48]{2,1,0:T(8,128)(2,1)}, u32[]{:S(2)}) copy-start(bf16[3,48,48]{2,1,0:T(8,128)(2,1)} %conv1.1) | copy-start | bytes 41476
  0.7 0.8 %copy-start.2 = (f32[64,128]{1,0:T(8,128)S(1)}, f32[64,128]{1,0:T(8,128)}, u32[]{:S(2)}) copy-start(f32[64,128]{1,0:T(8,128)} %field.1) | copy-start | bytes 98308
  1.4 7.0 %copy-start.3 = (s32[64,64]{1,0:T(8,128)S(1)}, s32[64,64]{1,0:T(8,128)}, u32[]{:S(2)}) copy-start(s32[64,64]{1,0:T(8,128)} %neighbours.1) | copy-start | bytes 49156
  1.4 7.0 %copy-start.4 = (f32[64,32]{0,1:T(8,128)S(1)}, f32[64,32]{0,1:T(8,128)}, u32[]{:S(2)}) copy-start(f32[64,32]{0,1:T(8,128)} %param.17) | copy-start | bytes 24580
  1.4 7.0 %copy-start.8 = (f32[48]{0:T(128)S(1)}, f32[48]{0:T(128)}, u32[]{:S(2)}) copy-start(f32[48]{0:T(128)} %bias2.1) | copy-start | bytes 580
  1.4 7.0 %copy-start.9 = (bf16[144]{0:T(256)(128)(2,1)S(1)}, bf16[144]{0:T(256)(128)(2,1)}, u32[]{:S(2)}) copy-start(bf16[144]{0:T(256)(128)(2,1)} %readout.1) | copy-start | bytes 868
  1.4 7.0 %copy-start.10 = (f32[32]{0:T(128)S(1)}, f32[32]{0:T(128)}, u32[]{:S(2)}) copy-start(f32[32]{0:T(128)} %obs_heads.1) | copy-start | bytes 388
  1.4 7.0 %copy-start.11 = (f32[32]{0:T(128)S(1)}, f32[32]{0:T(128)}, u32[]{:S(2)}) copy-start(f32[32]{0:T(128)} %obs_var.1) | copy-start | bytes 388
  1.5 7.0 %copy-start.12 = (s32[1,32]{1,0:T(1,128)S(1)}, s32[1,32]{1,0:T(1,128)}, u32[]{:S(2)}) copy-start(s32[1,32]{1,0:T(1,128)} %obs_index.1) | copy-start | bytes 388
  1.6 9.1 %collective-permute-start = (f32[8,64]{1,0:T(8,128)S(1)}, f32[8,64]{1,0:T(8,128)S(1)}, u32[]{:S(2)}, u32[]{:S(2)}) collective-permute-start(f32[8,64]{1,0:T(8,128)S(1)} %get-tuple-element.17), channel_id=1, source_target_pairs={{0,2},{2,4},{4,6},{6,8},{8,10},{10,12},{12,14},{14,16},{16,18},{18... | collective-permute-start | bytes 6152 | tf_op jit(solution)/shard_map/ppermute | solution.py:367
  6.4 5.5 %collective-permute-start.1 = (f32[8,64]{1,0:T(8,128)S(1)}, f32[8,64]{1,0:T(8,128)S(1)}, u32[]{:S(2)}, u32[]{:S(2)}) collective-permute-start(f32[8,64]{1,0:T(8,128)S(1)} %get-tuple-element.18), channel_id=1, source_target_pairs={{2,0},{4,2},{6,4},{8,6},{10,8},{12,10},{14,12},{16,14},{18,16},{20... | collective-permute-start | bytes 6152 | tf_op jit(solution)/shard_map/ppermute | solution.py:368
  8.4 0.7 %copy-start.5 = (f32[48]{0:T(128)S(1)}, f32[48]{0:T(128)}, u32[]{:S(2)}) copy-start(f32[48]{0:T(128)} %gain.1) | copy-start | bytes 580
  8.4 0.7 %copy-start.6 = (f32[48]{0:T(128)S(1)}, f32[48]{0:T(128)}, u32[]{:S(2)}) copy-start(f32[48]{0:T(128)} %bias.1) | copy-start | bytes 580
  8.4 0.7 %copy-start.7 = (f32[48]{0:T(128)S(1)}, f32[48]{0:T(128)}, u32[]{:S(2)}) copy-start(f32[48]{0:T(128)} %bias1.1) | copy-start | bytes 580
  28.8 1.6 %collective-permute-start.2 = (f32[16,32,128]{2,1,0:T(8,128)S(1)}, f32[16,32,128]{2,1,0:T(8,128)S(1)}, u32[]{:S(2)}, u32[]{:S(2)}) collective-permute-start(f32[16,32,128]{2,1,0:T(8,128)S(1)} %all_to_all.5.refs_0_), channel_id=1, source_target_pairs={{1,0},{0,1},{3,2},{2,3},{5,4},{4,5},{7,6},{6,7},{9,8},{8,9},{11,10... | collective-permute-start | bytes 786440 | tf_op jit(solution)/shard_map/ppermute | solution.py:336
  28.8 1.6 %collective-permute-start.3 = (f32[144,64]{1,0:T(8,128)S(1)}, f32[144,64]{1,0:T(8,128)S(1)}, u32[]{:S(2)}, u32[]{:S(2)}) collective-permute-start(f32[144,64]{1,0:T(8,128)S(1)} %get-tuple-element.25.refs_2_), channel_id=1, source_target_pairs={{1,0},{0,1},{3,2},{2,3},{5,4},{4,5},{7,6},{6,7},{9,8},{8,9},{11,10... | collective-permute-start | bytes 110600 | tf_op jit(solution)/shard_map/ppermute | solution.py:336

commit v4 on v3

--- a/solution.py
+++ b/solution.py
@@ -88,20 +88,26 @@
     return jnp.concatenate([one, two, three], axis=1)
 
 
-def edges_kernel(field, low, high, own):
-    turned = field[...].T
-    cells = turned.shape[0]
-    own[...] = turned
-    low[...] = turned[:EDGE]
-    high[...] = turned[cells - EDGE :]
+def turn_kernel(field, own):
+    own[...] = field[...].T
+
+
+def end_masks(parts, members):
+    space = lax.axis_index("space")
+    lane = lax.broadcasted_iota(jnp.int32, (1, parts * members), 1)
+    left = (lane < members) & (space == 0)
+    right = (lane >= (parts - 1) * members) & (space == lax.axis_size("space") - 1)
+    return jnp.where(left, 0.0, 1.0), jnp.where(right, 0.0, 1.0)
 
 
 def prepare_kernel(
     own, gain, bias, conv1, bias1, conv2, bias2, readout, neighbours,
     obs_heads, obs_var, noise_turned, obs_index, obs_count,
-    taps1, taps2, columns, near, near_turned, chosen, goal, inner,
+    taps1, taps2, columns, near, near_turned, sent,
     wide1, wide2, first, second, heads,
 ):
+    space = lax.axis_index("space")
+    spaces = lax.axis_size("space")
     turned = own[...]
     cells, members = turned.shape
     channels = gain.shape[0]
@@ -136,54 +142,85 @@
     near[...] = jnp.concatenate([pair, pair], axis=0)
     near_turned[...] = pair.T
     slots = obs_var.shape[0]
-    cell = column(obs_index[...].astype(F32)).astype(jnp.int32)
-    chosen[...] = jnp.where(
-        lax.broadcasted_iota(jnp.int32, (slots, cells), 1) == cell, 1.0, 0.0
+    cell = obs_index[...]
+    low_end = (cell < HALO) & (space > 0)
+    high_end = (cell >= cells - HALO) & (space < spaces - 1)
+    end_row = jnp.where(
+        low_end,
+        (space - 1) * EDGE + HALO + cell,
+        jnp.where(high_end, space * EDGE + cell - (cells - HALO), -1),
+    )
+    inside = column(jnp.where(end_row < 0, cell, -1).astype(F32)).astype(jnp.int32)
+    chosen = jnp.where(
+        lax.broadcasted_iota(jnp.int32, (slots, cells), 1) == inside, 1.0, 0.0
     ).astype(BF16)
+    variance = obs_var[...].reshape(1, slots)
+    live = lax.broadcasted_iota(jnp.int32, (1, slots), 1) < obs_count[...].reshape(1, 1)
+    root_row = jnp.where(live, lax.rsqrt(variance), 0.0)
+    root = column(root_row)
     target = column(obs_heads[...].reshape(1, slots))
-    variance = column(obs_var[...].reshape(1, slots))
-    live = lax.broadcasted_iota(jnp.int32, (slots, 1), 0) < obs_count[...].reshape(1, 1)
-    root = jnp.where(live, lax.rsqrt(variance), 0.0)
-    wanted = root * (target + jnp.sqrt(variance) * noise_turned[...])
-    goal[...] = jnp.concatenate([jnp.broadcast_to(root, (slots, members)), wanted], axis=1)
+    wanted = root * (target + jnp.sqrt(column(variance)) * noise_turned[...])
+
     zeros = jnp.zeros((HALO, members), F32)
     wide = in_runs(jnp.concatenate([zeros, turned, zeros], axis=0))
-    run = cells // PARTS
-    layers(wide, run, None, None, taps1, taps2, columns, first, second, heads)
-    for q in range(PARTS):
-        inner[q * run : (q + 1) * run, :] = heads[:, q * members : (q + 1) * members]
-
-
-def observe_kernel(
-    own, inner, from_left, from_right, taps1, taps2, columns, chosen, goal,
-    sent, ext, first, second, heads,
-):
-    space = lax.axis_index("space")
-    spaces = lax.axis_size("space")
-    cells, members = own.shape
-    ext[0:EDGE, :] = from_left[...]
-    ext[EDGE : EDGE + cells, :] = own[...]
-    ext[EDGE + cells :, :] = from_right[...]
-    ends = jnp.concatenate(
+    left, right = end_masks(PARTS, members)
+    layers(wide, cells // PARTS, left, right, taps1, taps2, columns, first, second, heads)
+    every = jnp.concatenate(
+        [heads[:, q * members : (q + 1) * members] for q in range(PARTS)], axis=0
+    )
+    parts = jnp.dot(chosen, split3(every), preferred_element_type=F32)
+    seen = parts[:, :members] + parts[:, members : 2 * members] + parts[:, 2 * members :]
+    weighted = root * seen
+    blank = jnp.zeros((1, 2 * members - slots), F32)
+    payload = jnp.concatenate(
         [
-            jnp.concatenate([from_left[EDGE - HALO :, :], own[0 : 2 * HALO, :]], axis=0),
-            jnp.concatenate([own[cells - 2 * HALO :, :], from_right[0:HALO, :]], axis=0),
+            jnp.concatenate([weighted, wanted - weighted], axis=1),
+            jnp.concatenate([turned[: 2 * HALO], turned[cells - 2 * HALO :]], axis=1),
+            jnp.concatenate([end_row.astype(F32), blank], axis=1),
+            jnp.concatenate([root_row, blank], axis=1),
         ],
-        axis=1,
-    )
-    lane = lax.broadcasted_iota(jnp.int32, (1, 2 * members), 1)
-    left = jnp.where((lane < members) & (space == 0), 0.0, 1.0)
-    right = jnp.where((lane >= members) & (space == spaces - 1), 0.0, 1.0)
-    layers(ends, HALO, left, right, taps1, taps2, columns, first, second, heads)
-    every = jnp.concatenate(
-        [heads[0:HALO, :members], inner[HALO : cells - HALO, :], heads[0:HALO, members:]], axis=0
-    )
-    parts = jnp.dot(chosen[...], split3(every), preferred_element_type=F32)
-    seen = parts[:, :members] + parts[:, members : 2 * members] + parts[:, 2 * members :]
-    weighted = goal[:, :members] * seen
-    payload = jnp.concatenate([weighted, goal[:, members:] - weighted], axis=1)
+        axis=0,
+    )
     for copy in range(sent.shape[0]):
         sent[copy] = payload
+
+
+def ends_kernel(got, taps1, taps2, columns, full, first, second, heads, ends, marks):
+    space = lax.axis_index("space")
+    spaces = got.shape[0]
+    slots = got.shape[1] - EDGE
+    members = got.shape[2] // 2
+    inner = 2 * HALO
+    for start in range(0, spaces, PARTS):
+        sides = []
+        for here in range(start, start + PARTS):
+            there = (here + 1) % spaces
+            near_end = got[here, slots : slots + inner, members:]
+            far_end = got[there, slots : slots + inner, :members]
+            sides.append(jnp.concatenate([near_end, far_end], axis=0))
+        wide = jnp.concatenate(sides, axis=1)
+        layers(wide, inner, None, None, taps1, taps2, columns, first, second, heads)
+        for q in range(PARTS):
+            at = (start + q) * EDGE
+            ends[at : at + EDGE, :] = heads[:, q * members : (q + 1) * members]
+    for tile in range(spaces):
+        at = tile * slots
+        marks[0:2, at : at + slots] = got[tile, slots + inner : slots + EDGE, :slots]
+    row = lax.broadcasted_iota(jnp.int32, (spaces * EDGE, spaces * slots), 0).astype(F32)
+    picks = jnp.where(row == marks[0:1, :], marks[1:2, :], 0.0)
+    added = lax.dot_general(
+        picks, ends[...], (((0,), (0,)), ((), ())),
+        precision=lax.Precision.HIGHEST, preferred_element_type=F32,
+    )
+    signed = jnp.concatenate([added, -added], axis=1)
+    for tile in range(spaces):
+        at = tile * slots
+        full[at : at + slots, :] = got[tile, :slots, :] + signed[at : at + slots]
+    before = jnp.where(space == 0, spaces - 1, space - 1)
+    after = jnp.where(space == spaces - 1, 0, space + 1)
+    at = spaces * slots
+    full[at : at + EDGE, :] = got[before, slots:, :]
+    full[at + EDGE : at + 2 * EDGE, :] = got[after, slots:, :]
 
 
 def lane_gather(table, index):
@@ -199,24 +236,21 @@
 
 
 def update_kernel(groups, *refs):
-    gots, exts = refs[:groups], refs[groups : 2 * groups]
+    fulls, owns = refs[:groups], refs[groups : 2 * groups]
     (
         taps1, taps2, columns, near, near_turned,
         updated, new_heads,
         system, first, second, heads, turned,
     ) = refs[2 * groups :]
-    space = lax.axis_index("space")
-    spaces = lax.axis_size("space")
-    slots = gots[0].shape[0] * gots[0].shape[1]
-    members = gots[0].shape[2] // 2
+    slots = fulls[0].shape[0] - 2 * EDGE
+    members = fulls[0].shape[1] // 2
     everyone = groups * members
     order = near.shape[0] // 2
     half_lane = lax.broadcasted_iota(jnp.int32, (1, 128), 1) < 64
 
-    whole = [got[...].reshape(slots, 2 * members) for got in gots]
-    panel = jnp.concatenate([rows[:, :members] for rows in whole], axis=1)
+    panel = jnp.concatenate([full[0:slots, :members] for full in fulls], axis=1)
     panel = panel - jnp.mean(panel, axis=1, keepdims=True)
-    innovation = whole[0][:, members:]
+    innovation = fulls[0][0:slots, members:]
     stacked = jnp.concatenate([panel, innovation], axis=1)
     product = lax.dot_general(
         stacked, panel, (((0,), (0,)), ((), ())),
@@ -312,16 +346,20 @@
         mixing = jnp.where(names == near_turned[i : i + 1, :members], coef[i : i + 1], mixing)
 
     cells = updated.shape[1]
-    inside = slice(EDGE - HALO, EDGE + cells + HALO)
-    sources = jnp.concatenate([ext[inside, :] for ext in exts], axis=1)
-    field = exts[0][inside, :] + jnp.dot(
+    sources = jnp.concatenate(
+        [
+            jnp.concatenate([full[slots + HALO : slots + 2 * HALO, members:] for full in fulls], axis=1),
+            jnp.concatenate([own[...] for own in owns], axis=1),
+            jnp.concatenate([full[slots + EDGE : slots + EDGE + HALO, :members] for full in fulls], axis=1),
+        ],
+        axis=0,
+    )
+    field = sources[:, :members] + jnp.dot(
         sources, mixing, precision=lax.Precision.HIGHEST, preferred_element_type=F32
     )
     updated[...] = field[HALO : HALO + cells].T
     run = cells // PARTS
-    lane = lax.broadcasted_iota(jnp.int32, (1, PARTS * members), 1)
-    left = jnp.where((lane < members) & (space == 0), 0.0, 1.0)
-    right = jnp.where((lane >= (PARTS - 1) * members) & (space == spaces - 1), 0.0, 1.0)
+    left, right = end_masks(PARTS, members)
     layers(in_runs(field), run, left, right, taps1, taps2, columns, first, second, heads)
     for q in range(PARTS):
         turned[q * run : (q + 1) * run, :] = heads[:, q * members : (q + 1) * members]
@@ -356,17 +394,8 @@
             pltpu.VMEM((max(run, 8), lanes), F32),
         )
 
-    low, high, own = call(
-        edges_kernel,
-        (shape((EDGE, members)), shape((EDGE, members)), shape((cells, members))),
-        (log_field,),
-        flops=1 << 34,
-    )
-    forward = [(i, i + 1) for i in range(spaces - 1)]
-    backward = [(i + 1, i) for i in range(spaces - 1)]
-    from_left = lax.ppermute(high, "space", forward)
-    from_right = lax.ppermute(low, "space", backward)
-    taps1, taps2, columns, near, near_turned, chosen, goal, inner = call(
+    own = call(turn_kernel, shape((cells, members)), (log_field,), flops=1 << 34)
+    taps1, taps2, columns, near, near_turned, sent = call(
         prepare_kernel,
         (
             shape((channels, 3 * channels), BF16),
@@ -374,9 +403,7 @@
             shape((5, channels, 128)),
             shape((2 * members, 2 * order), jnp.int32),
             shape((2 * order, members), jnp.int32),
-            shape((slots, cells), BF16),
-            shape((slots, 2 * members)),
-            shape((cells, members)),
+            shape((spaces, slots + EDGE, 2 * members)),
         ),
         (
             own, lift_gain, lift_bias, conv_first, bias_first, conv_second, bias_second,
@@ -387,19 +414,22 @@
             pltpu.VMEM((channels + 16, 6 * channels), F32),
         )
         + work(cells // PARTS, PARTS),
-        flops=1 << 29,
-    )
-    sent, ext = call(
-        observe_kernel,
-        (shape((spaces, slots, 2 * members)), shape((2 * EDGE + cells, members))),
-        (own, inner, from_left, from_right, taps1, taps2, columns, chosen, goal),
-        scratch=work(HALO, 2),
     )
     got = lax.all_to_all(sent, "space", 0, 0)
+    full = call(
+        ends_kernel,
+        shape((spaces * slots + 2 * EDGE, 2 * members)),
+        (got, taps1, taps2, columns),
+        scratch=work(2 * HALO, PARTS)
+        + (
+            pltpu.VMEM((spaces * EDGE, members), F32),
+            pltpu.VMEM((8, spaces * slots), F32),
+        ),
+    )
     return call(
         functools.partial(update_kernel, groups),
         (shape((members, cells)), shape((members, cells))),
-        (*from_groups(got), *from_groups(ext), taps1, taps2, columns, near, near_turned),
+        (*from_groups(full), *from_groups(own), taps1, taps2, columns, near, near_turned),
         scratch=(pltpu.VMEM(((order // 2 + 1) * order, 128), F32),)
         + work(cells // PARTS, PARTS)
         + (pltpu.VMEM((cells, members), F32),),

time: 40.1 us -> 37.9 us (0.945)
  starting transfers between devices: 6.64 us -> 0.57 us
  blocking collectives: 16 us -> 19.4 us
  Pallas kernels: 11.9 us -> 13.6 us
  waiting for transfers between devices: 2.37 us -> 1.13 us
    ppermute x2 -> x0, starting transfers between devices: 6.13 us -> none  [the longest x1 4.84 us: on_device(): from_left = lax.ppermute(high, 'space', forward)]
    all_to_all x1, blocking collectives: 16 us -> 19.4 us  [on_device(): got = lax.all_to_all(sent, 'space', 0, 0)]
    pallas_call x4, Pallas kernels: 11.9 us -> 13.6 us  [call(): pl.pallas_call(kernel, out_shape=outs, in_specs=[VMEM] * len(args), out_s...]
    ppermute x2 -> x0, waiting for transfers between devices: 1.24 us -> none  [the longest x1 1.23 us: on_device(): from_right = lax.ppermute(low, 'space', backward)]
  transfers between devices with their start and end apart: 4 -> 2, of which waited for: 2 -> 1; matrix products, arithmetic and copies ran while one was open for 0% -> 0% of each run, Pallas kernels for 4% -> 0%
where the time goes in v4:
time: 37.9 us; the launch traced here: 37.6 us
  blocking collectives  19.4 us (51%)
  Pallas kernels  13.6 us (36%)
  between operations  1.46 us (4%)
  local copies, waits for them, and re-layouts  1.39 us (4%)
  waiting for transfers between devices  1.13 us (3%)
  starting transfers between devices  0.57 us (2%)
    all_to_all x1, blocking collectives, on_device(): got = lax.all_to_all(sent, 'space', 0, 0)  19.4 us
    pallas_call x4, Pallas kernels, call(): pl.pallas_call(kernel, out_shape=outs, in_specs=[VMEM] * len(args), out_s...  13.6 us
    unnamed x26, local copies, waits for them, and re-layouts  1.39 us
    ppermute x2, waiting for transfers between devices, from_groups(): found.append(lax.ppermute(value, 'members', pairs))  1.13 us
  transfers between devices with their start and end apart: 2, of which 1 were waited for; matrix products, arithmetic and copies ran while one was open for 0% of the time, Pallas kernels for 0%

profile of v4, /device:TPU:0, one launch (start us, length us, event | category | flops | bytes accessed | tf_op | source)
XLA Modules:
  0.0 37.6 jit_solution(1165249774166989505)
XLA Ops:
  0.6 0.0 copy-start.3
  0.6 0.0 copy-start.2
  0.7 0.0 copy-start
  0.7 0.0 copy-start.1
  0.7 0.0 copy-start.12
  0.7 0.8 %copy-done.12 = f32[64,128]{1,0:T(8,128)S(1)} copy-done((f32[64,128]{1,0:T(8,128)S(1)}, f32[64,128]{1,0:T(8,128)}, u32[]{:S(2)}) %copy-start.12) | copy-done | bytes 32792
  1.5 0.0 copy-start.11
  1.5 0.1 shard_map.149.own.refs_2_
  2.2 0.0 copy-start.4
  2.2 0.0 copy-start.5
  2.3 0.0 copy-start.6
  2.3 0.0 copy-done.3
  2.3 0.0 copy-done.2
  2.4 0.5 %copy-done.4 = f32[48]{0:T(128)S(1)} copy-done((f32[48]{0:T(128)S(1)}, f32[48]{0:T(128)}, u32[]{:S(2)}) %copy-start.4) | copy-done | bytes 216
  2.9 0.0 copy-done.5
  2.9 0.0 copy-done.6
  2.9 2.0 %shard_map.150 = (bf16[48,144]{1,0:T(8,128)(2,1)S(1)}, bf16[64,288]{1,0:T(8,128)(2,1)S(1)}, f32[5,48,128]{2,1,0:T(8,128)S(1)}, s32[128,128]{1,0:T(8,128)S(1)}, s...) custom-call(f32[128,64]{1,0:T(8,128)S(1)} %shard_map.149.own.refs_2_, f32[48]{0:T(128)S(1)} %copy-done.4, ...), custom_call_target="tpu_custom_call" | custom-call | bytes 262144 | tf_op jit(solution)/shard_map/pallas_call | solution.py:23
  5.0 19.4 %all_to_all.5.got = f32[16,40,128]{2,1,0:T(8,128)S(1)} all-to-all(f32[16,40,128]{2,1,0:T(8,128)S(1)} %get-tuple-element.8), channel_id=1, replica_groups=mesh['space'=16,'members'=2] {'space'}, dimensions={0} | all-to-all | bytes 655360 | tf_op jit(solution)/shard_map/all_to_all | solution.py:418
  24.4 2.2 %shard_map.151.refs_0_ = f32[528,128]{1,0:T(8,128)S(1)} custom-call(f32[16,40,128]{2,1,0:T(8,128)S(1)} %all_to_all.5.got, bf16[48,144]{1,0:T(8,128)(2,1)S(1)} %get-tuple-element.9.taps1.refs_4_, bf16[64,288]{1,0:T(8,128)(2,1)S(1)} %get-tuple-element.10.taps2.refs_5_, f32[5,48,128]{2,1,0:T(8,128)S(1)} %get-tuple-element.11.columns.refs_6_), custom_call_target="tpu_custom_call" | custom-call | bytes 262144 | tf_op jit(solution)/shard_map/pallas_call | solution.py:23
  26.6 0.1 collective-permute-start
  26.7 0.5 %collective-permute-start.1 = (f32[128,64]{1,0:T(8,128)S(1)}, f32[128,64]{1,0:T(8,128)S(1)}, u32[]{:S(2)}, u32[]{:S(2)}) collective-permute-start(f32[128,64]{1,0:T(8,128)S(1)} %shard_map.149.own.refs_2_), channel_id=1, source_target_pairs={{1,0},{0,1},{3,2},{2,3},{5,4},{4,5},{7,6},{6,7},{9,8},{8,9},{11,10... | collective-permute-start | bytes 98312 | tf_op jit(solution)/shard_map/ppermute | solution.py:374
  27.2 1.1 %collective-permute-done.1.refs_3_ = f32[128,64]{1,0:T(8,128)S(1)} collective-permute-done((f32[128,64]{1,0:T(8,128)S(1)}, f32[128,64]{1,0:T(8,128)S(1)}, u32[]{:S(2)}, u32[]{:S(2)}) %collective-permute-start.1) | collective-permute-done | bytes 32800 | tf_op jit(solution)/shard_map/ppermute | solution.py:374
  28.3 0.0 collective-permute-done.refs_1_
  28.3 9.3 %shard_map.152 = (f32[64,128]{1,0:T(8,128)}, f32[64,128]{1,0:T(8,128)}) custom-call(f32[528,128]{1,0:T(8,128)S(1)} %shard_map.151.refs_0_, f32[528,128]{1,0:T(8,128)S(1)} %collective-permute-done.refs_1_, f32[128,64]{1,0:T(8,128)S(1)} %shard_map.149.own.refs_2_, f32[128,64]{1,0:T(8,128)S(1)} %collective-permute-done.1.refs_3_, ...), custom_call_target="tpu_custom_call" | custom-call | bytes 262144 | tf_op jit(solution)/shard_map/pallas_call | solution.py:23
  (11 shorter events, 0.0 us)
Async XLA Ops:
  0.6 1.6 %copy-start.3 = (f32[64,32]{0,1:T(8,128)S(1)}, f32[64,32]{0,1:T(8,128)}, u32[]{:S(2)}) copy-start(f32[64,32]{0,1:T(8,128)} %param.17) | copy-start | bytes 24580
  0.6 1.6 %copy-start.2 = (s32[64,64]{1,0:T(8,128)S(1)}, s32[64,64]{1,0:T(8,128)}, u32[]{:S(2)}) copy-start(s32[64,64]{1,0:T(8,128)} %neighbours.1) | copy-start | bytes 49156
  0.7 1.6 %copy-start = (bf16[3,48,48]{2,1,0:T(8,128)(2,1)S(1)}, bf16[3,48,48]{2,1,0:T(8,128)(2,1)}, u32[]{:S(2)}) copy-start(bf16[3,48,48]{2,1,0:T(8,128)(2,1)} %conv1.1) | copy-start | bytes 41476
  0.7 1.6 %copy-start.1 = (bf16[3,48,96]{2,1,0:T(8,128)(2,1)S(1)}, bf16[3,48,96]{2,1,0:T(8,128)(2,1)}, u32[]{:S(2)}) copy-start(bf16[3,48,96]{2,1,0:T(8,128)(2,1)} %conv2.1) | copy-start | bytes 82948
  0.7 0.8 %copy-start.12 = (f32[64,128]{1,0:T(8,128)S(1)}, f32[64,128]{1,0:T(8,128)}, u32[]{:S(2)}) copy-start(f32[64,128]{1,0:T(8,128)} %field.1) | copy-start | bytes 98308
  1.5 0.9 %copy-start.7 = (f32[48]{0:T(128)S(1)}, f32[48]{0:T(128)}, u32[]{:S(2)}) copy-start(f32[48]{0:T(128)} %bias2.1) | copy-start | bytes 580
  1.5 0.9 %copy-start.8 = (bf16[144]{0:T(256)(128)(2,1)S(1)}, bf16[144]{0:T(256)(128)(2,1)}, u32[]{:S(2)}) copy-start(bf16[144]{0:T(256)(128)(2,1)} %readout.1) | copy-start | bytes 868
  1.5 0.9 %copy-start.9 = (f32[32]{0:T(128)S(1)}, f32[32]{0:T(128)}, u32[]{:S(2)}) copy-start(f32[32]{0:T(128)} %obs_heads.1) | copy-start | bytes 388
  1.5 0.9 %copy-start.10 = (f32[32]{0:T(128)S(1)}, f32[32]{0:T(128)}, u32[]{:S(2)}) copy-start(f32[32]{0:T(128)} %obs_var.1) | copy-start | bytes 388
  1.5 0.9 %copy-start.11 = (s32[1,32]{1,0:T(1,128)S(1)}, s32[1,32]{1,0:T(1,128)}, u32[]{:S(2)}) copy-start(s32[1,32]{1,0:T(1,128)} %obs_index.1) | copy-start | bytes 388
  2.2 0.7 %copy-start.4 = (f32[48]{0:T(128)S(1)}, f32[48]{0:T(128)}, u32[]{:S(2)}) copy-start(f32[48]{0:T(128)} %gain.1) | copy-start | bytes 580
  2.2 0.7 %copy-start.5 = (f32[48]{0:T(128)S(1)}, f32[48]{0:T(128)}, u32[]{:S(2)}) copy-start(f32[48]{0:T(128)} %bias.1) | copy-start | bytes 580
  2.3 0.7 %copy-start.6 = (f32[48]{0:T(128)S(1)}, f32[48]{0:T(128)}, u32[]{:S(2)}) copy-start(f32[48]{0:T(128)} %bias1.1) | copy-start | bytes 580
  26.6 1.7 %collective-permute-start = (f32[528,128]{1,0:T(8,128)S(1)}, f32[528,128]{1,0:T(8,128)S(1)}, u32[]{:S(2)}, u32[]{:S(2)}) collective-permute-start(f32[528,128]{1,0:T(8,128)S(1)} %shard_map.151.refs_0_), channel_id=1, source_target_pairs={{1,0},{0,1},{3,2},{2,3},{5,4},{4,5},{7,6},{6,7},{9,8},{8,9},{11,10... | collective-permute-start | bytes 811016 | tf_op jit(solution)/shard_map/ppermute | solution.py:374
  26.7 1.6 %collective-permute-start.1 = (f32[128,64]{1,0:T(8,128)S(1)}, f32[128,64]{1,0:T(8,128)S(1)}, u32[]{:S(2)}, u32[]{:S(2)}) collective-permute-start(f32[128,64]{1,0:T(8,128)S(1)} %shard_map.149.own.refs_2_), channel_id=1, source_target_pairs={{1,0},{0,1},{3,2},{2,3},{5,4},{4,5},{7,6},{6,7},{9,8},{8,9},{11,10... | collective-permute-start | bytes 98312 | tf_op jit(solution)/shard_map/ppermute | solution.py:374

commit v5 on v4

--- a/solution.py
+++ b/solution.py
@@ -101,9 +101,9 @@
 
 
 def prepare_kernel(
-    own, gain, bias, conv1, bias1, conv2, bias2, readout, neighbours,
+    own, gain, bias, conv1, bias1, conv2, bias2, readout,
     obs_heads, obs_var, noise_turned, obs_index, obs_count,
-    taps1, taps2, columns, near, near_turned, sent,
+    taps1, taps2, columns, sent,
     wide1, wide2, first, second, heads,
 ):
     space = lax.axis_index("space")
@@ -135,12 +135,6 @@
     ]
     for spot, value in enumerate(rows):
         columns[spot] = jnp.broadcast_to(column(value), (channels, columns.shape[2]))
-    everyone = members * lax.axis_size("members")
-    ids = neighbours[...] - members * lax.axis_index("members")
-    ids = jnp.where(ids < 0, ids + everyone, ids)
-    pair = jnp.concatenate([ids, ids], axis=1)
-    near[...] = jnp.concatenate([pair, pair], axis=0)
-    near_turned[...] = pair.T
     slots = obs_var.shape[0]
     cell = obs_index[...]
     low_end = (cell < HALO) & (space > 0)
@@ -171,13 +165,14 @@
     parts = jnp.dot(chosen, split3(every), preferred_element_type=F32)
     seen = parts[:, :members] + parts[:, members : 2 * members] + parts[:, 2 * members :]
     weighted = root * seen
+    shown = jnp.where(column(jnp.where(end_row < 0, 0.0, 1.0)) > 0.0, root, weighted)
     blank = jnp.zeros((1, 2 * members - slots), F32)
     payload = jnp.concatenate(
         [
-            jnp.concatenate([weighted, wanted - weighted], axis=1),
+            jnp.concatenate([shown, wanted - weighted], axis=1),
             jnp.concatenate([turned[: 2 * HALO], turned[cells - 2 * HALO :]], axis=1),
             jnp.concatenate([end_row.astype(F32), blank], axis=1),
-            jnp.concatenate([root_row, blank], axis=1),
+            jnp.zeros((1, 2 * members), F32),
         ],
         axis=0,
     )
@@ -185,7 +180,27 @@
         sent[copy] = payload
 
 
-def ends_kernel(got, taps1, taps2, columns, full, first, second, heads, ends, marks):
+def tables_kernel(neighbours, near, near_turned, choice):
+    members, order = neighbours.shape
+    everyone = choice.shape[2]
+    ids = neighbours[...] - members * lax.axis_index("members")
+    ids = jnp.where(ids < 0, ids + everyone, ids)
+    pair = jnp.concatenate([ids, ids], axis=1)
+    table = jnp.concatenate([pair, pair], axis=0)
+    near[...] = table
+    turned = pair.T[:order]
+    near_turned[...] = jnp.concatenate([turned, turned], axis=1)
+    second_half = (lax.broadcasted_iota(jnp.int32, (128, 128), 0) >= 64).astype(jnp.int32)
+    everyone_id = lax.broadcasted_iota(jnp.int32, (128, everyone), 1)
+    for two in range(order // 2):
+        member = jnp.take_along_axis(
+            table, 2 * two + second_half, axis=1, mode="promise_in_bounds"
+        )
+        member = jnp.concatenate([member] * (everyone // 128), axis=1)
+        choice[two] = jnp.where(member == everyone_id, 1.0, 0.0).astype(BF16)
+
+
+def ends_kernel(got, own, taps1, taps2, columns, full, first, second, heads, ends, marks):
     space = lax.axis_index("space")
     spaces = got.shape[0]
     slots = got.shape[1] - EDGE
@@ -199,28 +214,50 @@
             far_end = got[there, slots : slots + inner, :members]
             sides.append(jnp.concatenate([near_end, far_end], axis=0))
         wide = jnp.concatenate(sides, axis=1)
-        layers(wide, inner, None, None, taps1, taps2, columns, first, second, heads)
+        turn = start // PARTS
+        layers(
+            wide, inner, None, None, taps1, taps2, columns,
+            first.at[turn], second.at[turn], heads.at[turn],
+        )
         for q in range(PARTS):
             at = (start + q) * EDGE
-            ends[at : at + EDGE, :] = heads[:, q * members : (q + 1) * members]
+            ends[at : at + EDGE, :] = heads[turn, :, q * members : (q + 1) * members]
     for tile in range(spaces):
         at = tile * slots
-        marks[0:2, at : at + slots] = got[tile, slots + inner : slots + EDGE, :slots]
+        marks[0:1, at : at + slots] = got[tile, slots + inner : slots + inner + 1, :slots]
     row = lax.broadcasted_iota(jnp.int32, (spaces * EDGE, spaces * slots), 0).astype(F32)
-    picks = jnp.where(row == marks[0:1, :], marks[1:2, :], 0.0)
-    added = lax.dot_general(
-        picks, ends[...], (((0,), (0,)), ((), ())),
-        precision=lax.Precision.HIGHEST, preferred_element_type=F32,
-    )
-    signed = jnp.concatenate([added, -added], axis=1)
+    picks = jnp.where(row == marks[0:1, :], 1.0, 0.0).astype(BF16)
+    exact = split3(ends[...])
+    exact = [exact[:, i * members : (i + 1) * members] for i in range(3)]
+    flag = jnp.ones((spaces * EDGE, 2 * members), BF16)
+    none = jnp.zeros((spaces * EDGE, 2 * members), BF16)
+    table = jnp.concatenate(
+        [
+            jnp.concatenate([part, part, flag if i == 0 else none], axis=1)
+            for i, part in enumerate(exact)
+        ],
+        axis=0,
+    )
+    parts = lax.dot_general(
+        jnp.concatenate([picks] * 3, axis=0), table, (((0,), (0,)), ((), ())),
+        preferred_element_type=F32,
+    )
+    heads_lane = lax.broadcasted_iota(jnp.int32, (1, 2 * members), 1) < members
     for tile in range(spaces):
-        at = tile * slots
-        full[at : at + slots, :] = got[tile, :slots, :] + signed[at : at + slots]
+        at = slice(tile * slots, (tile + 1) * slots)
+        there = got[tile, :slots, :]
+        shown = jnp.where(heads_lane, there, pltpu.roll(there, members, 1))
+        seen, marked = parts[at, : 2 * members], parts[at, 2 * members :]
+        full[at, :] = jnp.where(
+            heads_lane, shown * (1.0 - marked + seen), there - shown * seen
+        )
     before = jnp.where(space == 0, spaces - 1, space - 1)
     after = jnp.where(space == spaces - 1, 0, space + 1)
     at = spaces * slots
     full[at : at + EDGE, :] = got[before, slots:, :]
     full[at + EDGE : at + 2 * EDGE, :] = got[after, slots:, :]
+    half = own.shape[0] // 2
+    full[at + 2 * EDGE :, :] = jnp.concatenate([own[:half, :], own[half:, :]], axis=1)
 
 
 def lane_gather(table, index):
@@ -236,13 +273,14 @@
 
 
 def update_kernel(groups, *refs):
-    fulls, owns = refs[:groups], refs[groups : 2 * groups]
+    fulls = refs[:groups]
     (
-        taps1, taps2, columns, near, near_turned,
+        taps1, taps2, columns, near, near_turned, choice,
         updated, new_heads,
         system, first, second, heads, turned,
-    ) = refs[2 * groups :]
-    slots = fulls[0].shape[0] - 2 * EDGE
+    ) = refs[groups:]
+    cells = updated.shape[1]
+    slots = fulls[0].shape[0] - 2 * EDGE - cells // 2
     members = fulls[0].shape[1] // 2
     everyone = groups * members
     order = near.shape[0] // 2
@@ -260,19 +298,13 @@
     sides = product[everyone:]
 
     ids = near[...]
-    second_half = (lax.broadcasted_iota(jnp.int32, (128, 128), 0) >= 64).astype(jnp.int32)
     lane_id = lax.broadcasted_iota(jnp.int32, (128, 128), 1)
     row_id = lax.broadcasted_iota(jnp.int32, (128, 128), 0)
-    everyone_id = lax.broadcasted_iota(jnp.int32, (128, everyone), 1)
 
     def extract(quad, carry):
         found = []
         for b in range(2):
-            column_id = 4 * quad + 2 * b + second_half
-            member = jnp.take_along_axis(ids, column_id, axis=1, mode="promise_in_bounds")
-            member = jnp.concatenate([member] * (everyone // 128), axis=1)
-            chosen = jnp.where(member == everyone_id, 1.0, 0.0).astype(BF16)
-            parts = jnp.dot(chosen, gram, preferred_element_type=F32)
+            parts = jnp.dot(choice[2 * quad + b], gram, preferred_element_type=F32)
             rows = (
                 parts[:, :everyone]
                 + parts[:, everyone : 2 * everyone]
@@ -340,17 +372,22 @@
     share = sums / pltpu.roll(sums, 64, 1)
     coef = (solved - pltpu.roll(solved, 64, 1) * share)[:, :members]
     coef = coef - jnp.mean(coef, axis=0, keepdims=True)
-    names = lax.broadcasted_iota(jnp.int32, (everyone, members), 0)
-    mixing = jnp.zeros((everyone, members), F32)
+    coef = jnp.concatenate([coef, coef], axis=1)
+    name = lax.broadcasted_iota(jnp.int32, (everyone // 2, 128), 0) + jnp.where(
+        half_lane, 0, everyone // 2
+    )
+    mixing = jnp.zeros((everyone // 2, 128), F32)
     for i in range(order):
-        mixing = jnp.where(names == near_turned[i : i + 1, :members], coef[i : i + 1], mixing)
-
-    cells = updated.shape[1]
+        mixing = jnp.where(name == near_turned[i : i + 1, :], coef[i : i + 1], mixing)
+    mixing = jnp.concatenate([mixing[:, :members], mixing[:, members:]], axis=0)
+
+    before, after, body = slots, slots + EDGE, slots + 2 * EDGE
     sources = jnp.concatenate(
         [
-            jnp.concatenate([full[slots + HALO : slots + 2 * HALO, members:] for full in fulls], axis=1),
-            jnp.concatenate([own[...] for own in owns], axis=1),
-            jnp.concatenate([full[slots + EDGE : slots + EDGE + HALO, :members] for full in fulls], axis=1),
+            jnp.concatenate([full[before + HALO : before + 2 * HALO, members:] for full in fulls], axis=1),
+            jnp.concatenate([full[body:, :members] for full in fulls], axis=1),
+            jnp.concatenate([full[body:, members:] for full in fulls], axis=1),
+            jnp.concatenate([full[after : after + HALO, :members] for full in fulls], axis=1),
         ],
         axis=0,
     )
@@ -395,19 +432,17 @@
         )
 
     own = call(turn_kernel, shape((cells, members)), (log_field,), flops=1 << 34)
-    taps1, taps2, columns, near, near_turned, sent = call(
+    taps1, taps2, columns, sent = call(
         prepare_kernel,
         (
             shape((channels, 3 * channels), BF16),
             shape((channels + 16, 6 * channels), BF16),
             shape((5, channels, 128)),
-            shape((2 * members, 2 * order), jnp.int32),
-            shape((2 * order, members), jnp.int32),
             shape((spaces, slots + EDGE, 2 * members)),
         ),
         (
             own, lift_gain, lift_bias, conv_first, bias_first, conv_second, bias_second,
-            readout, neighbours, obs_heads, obs_var, obs_noise.T, obs_index, obs_count,
+            readout, obs_heads, obs_var, obs_noise.T, obs_index, obs_count,
         ),
         scratch=(
             pltpu.VMEM((channels, 3 * channels), F32),
@@ -416,11 +451,24 @@
         + work(cells // PARTS, PARTS),
     )
     got = lax.all_to_all(sent, "space", 0, 0)
+    near, near_turned, choice = call(
+        tables_kernel,
+        (
+            shape((2 * members, 2 * order), jnp.int32),
+            shape((order, 2 * members), jnp.int32),
+            shape((order // 2, 2 * members, groups * members), BF16),
+        ),
+        (neighbours,),
+        flops=1 << 30,
+    )
+    turns = spaces // PARTS
     full = call(
         ends_kernel,
-        shape((spaces * slots + 2 * EDGE, 2 * members)),
-        (got, taps1, taps2, columns),
-        scratch=work(2 * HALO, PARTS)
+        shape((spaces * slots + 2 * EDGE + cells // 2, 2 * members)),
+        (got, own, taps1, taps2, columns),
+        scratch=tuple(
+            pltpu.VMEM((turns, *value.shape), value.dtype) for value in work(2 * HALO, PARTS)
+        )
         + (
             pltpu.VMEM((spaces * EDGE, members), F32),
             pltpu.VMEM((8, spaces * slots), F32),
@@ -429,7 +477,7 @@
     return call(
         functools.partial(update_kernel, groups),
         (shape((members, cells)), shape((members, cells))),
-        (*from_groups(full), *from_groups(own), taps1, taps2, columns, near, near_turned),
+        (*from_groups(full), taps1, taps2, columns, near, near_turned, choice),
         scratch=(pltpu.VMEM(((order // 2 + 1) * order, 128), F32),)
         + work(cells // PARTS, PARTS)
         + (pltpu.VMEM((cells, members), F32),),

time: 37.9 us -> 37.2 us (0.982)
  starting transfers between devices: 0.57 us -> 0.07 us
  waiting for transfers between devices: 1.13 us -> 0.65 us
    ppermute x2 -> x1, starting transfers between devices: 0.57 us -> 0.07 us  [from_groups(): found.append(lax.ppermute(value, 'members', pairs))]
    ppermute x2 -> x1, waiting for transfers between devices: 1.13 us -> 0.65 us  [from_groups(): found.append(lax.ppermute(value, 'members', pairs))]
    pallas_call x4 -> x5, Pallas kernels: 13.6 us -> 13.9 us  [call(): pl.pallas_call(kernel, out_shape=outs, in_specs=[VMEM] * len(args), out_s...]
  transfers between devices with their start and end apart: 2 -> 1, of which waited for: 1 -> 1; matrix products, arithmetic and copies ran while one was open for 0% -> 0% of each run, Pallas kernels for 0% -> 2%
where the time goes in v5:
time: 37.2 us; the launch traced here: 36.9 us
  blocking collectives  19.4 us (52%)
  Pallas kernels  13.9 us (37%)
  between operations  1.43 us (4%)
  local copies, waits for them, and re-layouts  1.41 us (4%)
  waiting for transfers between devices  0.65 us (2%)
    all_to_all x1, blocking collectives, on_device(): got = lax.all_to_all(sent, 'space', 0, 0)  19.4 us
    pallas_call x5, Pallas kernels, call(): pl.pallas_call(kernel, out_shape=outs, in_specs=[VMEM] * len(args), out_s...  13.9 us
    unnamed x26, local copies, waits for them, and re-layouts  1.41 us
  transfers between devices with their start and end apart: 1, of which 1 were waited for; matrix products, arithmetic and copies ran while one was open for 0% of the time, Pallas kernels for 2%

profile of v5, /device:TPU:0, one launch (start us, length us, event | category | flops | bytes accessed | tf_op | source)
XLA Modules:
  0.0 36.9 jit_solution(885779296398513933)
XLA Ops:
  1.3 0.0 copy-start.11
  1.3 0.7 %copy-done.11 = f32[64,128]{1,0:T(8,128)S(1)} copy-done((f32[64,128]{1,0:T(8,128)S(1)}, f32[64,128]{1,0:T(8,128)}, u32[]{:S(2)}) %copy-start.11) | copy-done | bytes 32792
  2.0 0.0 copy-start.7
  2.1 0.0 copy-start.8
  2.1 0.0 copy-start.9
  2.1 0.0 copy-start.10
  2.1 0.1 shard_map.149.own
  2.2 0.0 copy-start.3
  2.2 0.0 copy-start.4
  2.2 0.0 copy-start.5
  2.2 0.6 %copy-done = bf16[3,48,48]{2,1,0:T(8,128)(2,1)S(1)} copy-done((bf16[3,48,48]{2,1,0:T(8,128)(2,1)S(1)}, bf16[3,48,48]{2,1,0:T(8,128)(2,1)}, u32[]{:S(2)}) %copy-start) | copy-done | bytes 13848
  2.8 0.0 copy-done.1
  2.8 0.0 copy-done.2
  2.8 0.0 copy-done.6
  2.8 0.0 copy-done.8
  2.9 0.0 copy-done.4
  2.9 0.0 copy-done.5
  2.9 2.0 %shard_map.150 = (bf16[48,144]{1,0:T(8,128)(2,1)S(1)}, bf16[64,288]{1,0:T(8,128)(2,1)S(1)}, f32[5,48,128]{2,1,0:T(8,128)S(1)}, f32[16,40,128]{2,1,0:T(8,128)S(1)}) custom-call(f32[128,64]{1,0:T(8,128)S(1)} %shard_map.149.own, f32[48]{0:T(128)S(1)} %copy-done.3, f32[48]{0:T(128)S(1)} %copy-done.4, bf16[3,48,48]{2,1,0:T(8,128)(2,1)S(1)} %copy-done, ...), custom_call_target="tpu_custom_call" | custom-call | bytes 262144 | tf_op jit(solution)/shard_map/pallas_call | solution.py:23
  4.9 19.4 %all_to_all.5.got = f32[16,40,128]{2,1,0:T(8,128)S(1)} all-to-all(f32[16,40,128]{2,1,0:T(8,128)S(1)} %get-tuple-element.9), channel_id=1, replica_groups=mesh['space'=16,'members'=2] {'space'}, dimensions={0} | all-to-all | bytes 655360 | tf_op jit(solution)/shard_map/all_to_all | solution.py:453
  24.3 2.2 %shard_map.151.refs_0_ = f32[592,128]{1,0:T(8,128)S(1)} custom-call(f32[16,40,128]{2,1,0:T(8,128)S(1)} %all_to_all.5.got, f32[128,64]{1,0:T(8,128)S(1)} %shard_map.149.own, bf16[48,144]{1,0:T(8,128)(2,1)S(1)} %get-tuple-element.10.taps1.refs_2_, bf16[64,288]{1,0:T(8,128)(2,1)S(1)} %get-tuple-element.11.taps2.refs_3_, ...), custom_call_target="tpu_custom_call" | custom-call | bytes 262144 | tf_op jit(solution)/shard_map/pallas_call | solution.py:23
  26.5 0.1 collective-permute-start
  26.6 0.9 %shard_map.152 = (s32[128,128]{1,0:T(8,128)S(1)}, s32[64,128]{1,0:T(8,128)S(1)}, bf16[32,128,128]{2,1,0:T(8,128)(2,1)S(1)}) custom-call(s32[64,64]{1,0:T(8,128)S(1)} %copy-done.12), custom_call_target="tpu_custom_call" | custom-call | flops 1073741824 | bytes 262144 | tf_op jit(solution)/shard_map/pallas_call | solution.py:23
  27.5 0.6 %collective-permute-done.refs_1_ = f32[592,128]{1,0:T(8,128)S(1)} collective-permute-done((f32[592,128]{1,0:T(8,128)S(1)}, f32[592,128]{1,0:T(8,128)S(1)}, u32[]{:S(2)}, u32[]{:S(2)}) %collective-permute-start) | collective-permute-done | bytes 303136 | tf_op jit(solution)/shard_map/ppermute | solution.py:411
  28.2 8.7 %shard_map.153 = (f32[64,128]{1,0:T(8,128)}, f32[64,128]{1,0:T(8,128)}) custom-call(f32[592,128]{1,0:T(8,128)S(1)} %shard_map.151.refs_0_, f32[592,128]{1,0:T(8,128)S(1)} %collective-permute-done.refs_1_, bf16[48,144]{1,0:T(8,128)(2,1)S(1)} %get-tuple-element.10.taps1.refs_2_, bf16[64,288]{1,0:T(8,128)(2,1)S(1)} %get-tuple-element.11.taps2.refs_3_, ...), custom_call_target="tpu_custom_call" | custom-call | bytes 262144 | tf_op jit(solution)/shard_map/pallas_call | solution.py:23
  (10 shorter events, 0.0 us)
Async XLA Ops:
  1.3 0.8 %copy-start.11 = (f32[64,128]{1,0:T(8,128)S(1)}, f32[64,128]{1,0:T(8,128)}, u32[]{:S(2)}) copy-start(f32[64,128]{1,0:T(8,128)} %field.1) | copy-start | bytes 98308
  2.0 0.8 %copy-start = (bf16[3,48,48]{2,1,0:T(8,128)(2,1)S(1)}, bf16[3,48,48]{2,1,0:T(8,128)(2,1)}, u32[]{:S(2)}) copy-start(bf16[3,48,48]{2,1,0:T(8,128)(2,1)} %conv1.1) | copy-start | bytes 41476
  2.0 0.8 %copy-start.1 = (bf16[3,48,96]{2,1,0:T(8,128)(2,1)S(1)}, bf16[3,48,96]{2,1,0:T(8,128)(2,1)}, u32[]{:S(2)}) copy-start(bf16[3,48,96]{2,1,0:T(8,128)(2,1)} %conv2.1) | copy-start | bytes 82948
  2.0 0.8 %copy-start.2 = (f32[64,32]{0,1:T(8,128)S(1)}, f32[64,32]{0,1:T(8,128)}, u32[]{:S(2)}) copy-start(f32[64,32]{0,1:T(8,128)} %param.17) | copy-start | bytes 24580
  2.0 0.8 %copy-start.6 = (f32[48]{0:T(128)S(1)}, f32[48]{0:T(128)}, u32[]{:S(2)}) copy-start(f32[48]{0:T(128)} %bias2.1) | copy-start | bytes 580
  2.0 0.8 %copy-start.7 = (bf16[144]{0:T(256)(128)(2,1)S(1)}, bf16[144]{0:T(256)(128)(2,1)}, u32[]{:S(2)}) copy-start(bf16[144]{0:T(256)(128)(2,1)} %readout.1) | copy-start | bytes 868
  2.1 0.8 %copy-start.8 = (f32[32]{0:T(128)S(1)}, f32[32]{0:T(128)}, u32[]{:S(2)}) copy-start(f32[32]{0:T(128)} %obs_heads.1) | copy-start | bytes 388
  2.1 0.8 %copy-start.9 = (f32[32]{0:T(128)S(1)}, f32[32]{0:T(128)}, u32[]{:S(2)}) copy-start(f32[32]{0:T(128)} %obs_var.1) | copy-start | bytes 388
  2.1 0.8 %copy-start.10 = (s32[1,32]{1,0:T(1,128)S(1)}, s32[1,32]{1,0:T(1,128)}, u32[]{:S(2)}) copy-start(s32[1,32]{1,0:T(1,128)} %obs_index.1) | copy-start | bytes 388
  2.2 0.7 %copy-start.3 = (f32[48]{0:T(128)S(1)}, f32[48]{0:T(128)}, u32[]{:S(2)}) copy-start(f32[48]{0:T(128)} %gain.1) | copy-start | bytes 580
  2.2 0.7 %copy-start.4 = (f32[48]{0:T(128)S(1)}, f32[48]{0:T(128)}, u32[]{:S(2)}) copy-start(f32[48]{0:T(128)} %bias.1) | copy-start | bytes 580
  2.2 0.7 %copy-start.5 = (f32[48]{0:T(128)S(1)}, f32[48]{0:T(128)}, u32[]{:S(2)}) copy-start(f32[48]{0:T(128)} %bias1.1) | copy-start | bytes 580
  24.3 2.3 %copy-start.12 = (s32[64,64]{1,0:T(8,128)S(1)}, s32[64,64]{1,0:T(8,128)}, u32[]{:S(2)}) copy-start(s32[64,64]{1,0:T(8,128)} %neighbours.1) | copy-start | bytes 49156
  26.5 1.7 %collective-permute-start = (f32[592,128]{1,0:T(8,128)S(1)}, f32[592,128]{1,0:T(8,128)S(1)}, u32[]{:S(2)}, u32[]{:S(2)}) collective-permute-start(f32[592,128]{1,0:T(8,128)S(1)} %shard_map.151.refs_0_), channel_id=1, source_target_pairs={{1,0},{0,1},{3,2},{2,3},{5,4},{4,5},{7,6},{6,7},{9,8},{8,9},{11,10... | collective-permute-start | bytes 909320 | tf_op jit(solution)/shard_map/ppermute | solution.py:411

commit v6 on v5

--- a/solution.py
+++ b/solution.py
@@ -12,6 +12,7 @@
 HALO = 3
 EDGE = 8
 PARTS = 4
+BAND = 3
 VMEM = pl.BlockSpec(memory_space=pltpu.VMEM)
 
 
@@ -37,6 +38,10 @@
         jnp.int32, (size, size), 1
     )
     return jnp.sum(jnp.where(same, row, 0.0), axis=1, keepdims=True)
+
+
+def groups_of(count):
+    return [min(at, count - BAND) for at in range(0, count, BAND)]
 
 
 def layers(wide, run, left, right, taps1, taps2, columns, first, second, heads):
@@ -53,26 +58,35 @@
         if right is not None and r >= rows - HALO:
             value = value * right
         first[r] = value.astype(BF16)
-    for i in range(rows - 2):
-        window = first[i : i + 3].reshape(3 * channels, lanes)
-        half = jnp.dot(taps1[...], window, preferred_element_type=F32) + bias1
-        value = half + half * jnp.tanh(half)
-        if left is not None and i < HALO - 1:
-            value = value * left
-        if right is not None and i >= rows - 2 - (HALO - 1):
-            value = value * right
-        second[i] = value.astype(BF16)
-    split = 3 * channels
-    for n in range(run):
-        window1 = jnp.concatenate([first[n + 1], first[n + 3], first[n + 5]], axis=0)
-        window2 = jnp.concatenate([second[n], second[n + 2], second[n + 4]], axis=0)
-        total = jnp.dot(taps2[:, :split], window1, preferred_element_type=F32) + jnp.dot(
-            taps2[:, split:], window2, preferred_element_type=F32
-        )
-        half = total[:channels] + bias2
-        third = (half + half * jnp.tanh(half)).astype(BF16).astype(F32)
-        rest = jnp.sum(third * last, axis=0, keepdims=True)
-        heads[n : n + 1, :] = total[channels : channels + 1] + rest
+    reach = BAND + 2
+    for start in groups_of(rows - 2):
+        window = first[start : start + reach].reshape(reach * channels, lanes)
+        total = jnp.dot(taps1[...], window, preferred_element_type=F32)
+        for r in range(BAND):
+            i = start + r
+            half = total[r * channels : (r + 1) * channels] + bias1
+            value = half + half * jnp.tanh(half)
+            if left is not None and i < HALO - 1:
+                value = value * left
+            if right is not None and i >= rows - 2 - (HALO - 1):
+                value = value * right
+            second[i] = value.astype(BF16)
+    split = reach * channels
+    for parity in range(2):
+        for group in groups_of(run // 2):
+            start = 2 * group + parity
+            near = [first[start + 1 + 2 * i] for i in range(reach)]
+            far = [second[start + 2 * i] for i in range(reach)]
+            total = jnp.dot(
+                taps2[:, :split], jnp.concatenate(near, axis=0), preferred_element_type=F32
+            ) + jnp.dot(taps2[:, split:], jnp.concatenate(far, axis=0), preferred_element_type=F32)
+            for r in range(BAND):
+                n = start + 2 * r
+                half = total[r * channels : (r + 1) * channels] + bias2
+                third = (half + half * jnp.tanh(half)).astype(BF16).astype(F32)
+                rest = jnp.sum(third * last, axis=0, keepdims=True)
+                at = BAND * channels + r
+                heads[n : n + 1, :] = total[at : at + 1] + rest
 
 
 def in_runs(ext):
@@ -88,8 +102,8 @@
     return jnp.concatenate([one, two, three], axis=1)
 
 
-def turn_kernel(field, own):
-    own[...] = field[...].T
+def blank_kernel(blank):
+    blank[...] = jnp.zeros_like(blank)
 
 
 def end_masks(parts, members):
@@ -101,29 +115,34 @@
 
 
 def prepare_kernel(
-    own, gain, bias, conv1, bias1, conv2, bias2, readout,
+    empty, field, gain, bias, conv1, bias1, conv2, bias2, readout,
     obs_heads, obs_var, noise_turned, obs_index, obs_count,
-    taps1, taps2, columns, sent,
+    own, taps1, taps2, columns, sent,
     wide1, wide2, first, second, heads,
 ):
     space = lax.axis_index("space")
     spaces = lax.axis_size("space")
-    turned = own[...]
+    turned = field[...].T
+    own[...] = turned
     cells, members = turned.shape
     channels = gain.shape[0]
-    split = 3 * channels
-    row = readout[...].astype(F32).reshape(1, split)
+    row = readout[...].astype(F32).reshape(1, 3 * channels)
+    split = (BAND + 2) * channels
+    wide1[...] = jnp.zeros_like(wide1)
     wide2[...] = jnp.zeros_like(wide2)
     for tap in range(3):
-        at = slice(tap * channels, (tap + 1) * channels)
-        wide1[:, at] = 0.5 * conv1[tap].astype(F32)
+        one = 0.5 * conv1[tap].astype(F32)
         both = 0.5 * conv2[tap].astype(F32)
-        wide2[0:channels, at] = both[:, :channels]
-        wide2[0:channels, split + tap * channels : split + (tap + 1) * channels] = both[:, channels:]
-    wide2[channels : channels + 1, channels : 2 * channels] = row[:, :channels]
-    wide2[channels : channels + 1, split + channels : split + 2 * channels] = row[
-        :, channels : 2 * channels
-    ]
+        for r in range(BAND):
+            out = slice(r * channels, (r + 1) * channels)
+            at = (r + tap) * channels
+            wide1[out, at : at + channels] = one
+            wide2[out, at : at + channels] = both[:, :channels]
+            wide2[out, split + at : split + at + channels] = both[:, channels:]
+    for r in range(BAND):
+        out, at = BAND * channels + r, (r + 1) * channels
+        wide2[out : out + 1, at : at + channels] = row[:, :channels]
+        wide2[out : out + 1, split + at : split + at + channels] = row[:, channels : 2 * channels]
     taps1[...] = wide1[...].astype(BF16)
     taps2[...] = wide2[...].astype(BF16)
     rows = [
@@ -166,7 +185,7 @@
     seen = parts[:, :members] + parts[:, members : 2 * members] + parts[:, 2 * members :]
     weighted = root * seen
     shown = jnp.where(column(jnp.where(end_row < 0, 0.0, 1.0)) > 0.0, root, weighted)
-    blank = jnp.zeros((1, 2 * members - slots), F32)
+    blank = empty[0:1, slots : 2 * members]
     payload = jnp.concatenate(
         [
             jnp.concatenate([shown, wanted - weighted], axis=1),
@@ -200,7 +219,10 @@
         choice[two] = jnp.where(member == everyone_id, 1.0, 0.0).astype(BF16)
 
 
-def ends_kernel(got, own, taps1, taps2, columns, full, first, second, heads, ends, marks):
+def ends_kernel(
+    got, own, taps1, taps2, columns,
+    kept, swapped, first, second, heads, ends, marks,
+):
     space = lax.axis_index("space")
     spaces = got.shape[0]
     slots = got.shape[1] - EDGE
@@ -243,21 +265,27 @@
         preferred_element_type=F32,
     )
     heads_lane = lax.broadcasted_iota(jnp.int32, (1, 2 * members), 1) < members
-    for tile in range(spaces):
+    half = spaces * slots // 2
+
+    def finished(tile):
         at = slice(tile * slots, (tile + 1) * slots)
         there = got[tile, :slots, :]
         shown = jnp.where(heads_lane, there, pltpu.roll(there, members, 1))
         seen, marked = parts[at, : 2 * members], parts[at, 2 * members :]
-        full[at, :] = jnp.where(
-            heads_lane, shown * (1.0 - marked + seen), there - shown * seen
-        )
+        return jnp.where(heads_lane, shown * (1.0 - marked + seen), there - shown * seen)
+
+    for tile in range(spaces // 2):
+        at = slice(tile * slots, (tile + 1) * slots)
+        one, two = finished(tile), finished(tile + spaces // 2)
+        kept[at, :] = one
+        kept[half + tile * slots : half + (tile + 1) * slots, :] = two
+        swapped[at, :] = jnp.where(heads_lane, one, pltpu.roll(two, members, 1))
     before = jnp.where(space == 0, spaces - 1, space - 1)
     after = jnp.where(space == spaces - 1, 0, space + 1)
-    at = spaces * slots
-    full[at : at + EDGE, :] = got[before, slots:, :]
-    full[at + EDGE : at + 2 * EDGE, :] = got[after, slots:, :]
-    half = own.shape[0] // 2
-    full[at + 2 * EDGE :, :] = jnp.concatenate([own[:half, :], own[half:, :]], axis=1)
+    swapped[half : half + EDGE, :] = got[before, slots:, :]
+    swapped[half + EDGE : half + 2 * EDGE, :] = got[after, slots:, :]
+    middle = own.shape[0] // 2
+    swapped[half + 2 * EDGE :, :] = jnp.concatenate([own[:middle, :], own[middle:, :]], axis=1)
 
 
 def lane_gather(table, index):
@@ -273,22 +301,31 @@
 
 
 def update_kernel(groups, *refs):
-    fulls = refs[:groups]
+    kept, parcels = refs[0], refs[1 : 1 + groups]
     (
         taps1, taps2, columns, near, near_turned, choice,
         updated, new_heads,
         system, first, second, heads, turned,
-    ) = refs[groups:]
+    ) = refs[1 + groups :]
     cells = updated.shape[1]
-    slots = fulls[0].shape[0] - 2 * EDGE - cells // 2
-    members = fulls[0].shape[1] // 2
+    slots, members = kept.shape[0], kept.shape[1] // 2
     everyone = groups * members
     order = near.shape[0] // 2
     half_lane = lax.broadcasted_iota(jnp.int32, (1, 128), 1) < 64
 
-    panel = jnp.concatenate([full[0:slots, :members] for full in fulls], axis=1)
+    panel = []
+    for g in range(0, groups, 2):
+        right = parcels[g + 1][0 : slots // 2, :]
+        right = jnp.concatenate([pltpu.roll(right, members, 1), right], axis=0)
+        if g:
+            left = parcels[g][0 : slots // 2, :]
+            left = jnp.concatenate([left, pltpu.roll(left, members, 1)], axis=0)
+        else:
+            left = kept[...]
+        panel.append(jnp.where(half_lane, left, right))
+    panel = jnp.concatenate(panel, axis=1)
     panel = panel - jnp.mean(panel, axis=1, keepdims=True)
-    innovation = fulls[0][0:slots, members:]
+    innovation = kept[:, members:]
     stacked = jnp.concatenate([panel, innovation], axis=1)
     product = lax.dot_general(
         stacked, panel, (((0,), (0,)), ((), ())),
@@ -381,13 +418,14 @@
         mixing = jnp.where(name == near_turned[i : i + 1, :], coef[i : i + 1], mixing)
     mixing = jnp.concatenate([mixing[:, :members], mixing[:, members:]], axis=0)
 
-    before, after, body = slots, slots + EDGE, slots + 2 * EDGE
+    before = slots // 2
+    after, body = before + EDGE, before + 2 * EDGE
     sources = jnp.concatenate(
         [
-            jnp.concatenate([full[before + HALO : before + 2 * HALO, members:] for full in fulls], axis=1),
-            jnp.concatenate([full[body:, :members] for full in fulls], axis=1),
-            jnp.concatenate([full[body:, members:] for full in fulls], axis=1),
-            jnp.concatenate([full[after : after + HALO, :members] for full in fulls], axis=1),
+            jnp.concatenate([full[before + HALO : before + 2 * HALO, members:] for full in parcels], axis=1),
+            jnp.concatenate([full[body:, :members] for full in parcels], axis=1),
+            jnp.concatenate([full[body:, members:] for full in parcels], axis=1),
+            jnp.concatenate([full[after : after + HALO, :members] for full in parcels], axis=1),
         ],
         axis=0,
     )
@@ -431,22 +469,24 @@
             pltpu.VMEM((max(run, 8), lanes), F32),
         )
 
-    own = call(turn_kernel, shape((cells, members)), (log_field,), flops=1 << 34)
-    taps1, taps2, columns, sent = call(
+    reach = (BAND + 2) * channels
+    empty = call(blank_kernel, shape((8, 2 * members)), (), flops=1 << 34)
+    own, taps1, taps2, columns, sent = call(
         prepare_kernel,
         (
-            shape((channels, 3 * channels), BF16),
-            shape((channels + 16, 6 * channels), BF16),
+            shape((cells, members)),
+            shape((BAND * channels, reach), BF16),
+            shape((BAND * channels + 16, 2 * reach), BF16),
             shape((5, channels, 128)),
             shape((spaces, slots + EDGE, 2 * members)),
         ),
         (
-            own, lift_gain, lift_bias, conv_first, bias_first, conv_second, bias_second,
+            empty, log_field, lift_gain, lift_bias, conv_first, bias_first, conv_second, bias_second,
             readout, obs_heads, obs_var, obs_noise.T, obs_index, obs_count,
         ),
         scratch=(
-            pltpu.VMEM((channels, 3 * channels), F32),
-            pltpu.VMEM((channels + 16, 6 * channels), F32),
+            pltpu.VMEM((BAND * channels, reach), F32),
+            pltpu.VMEM((BAND * channels + 16, 2 * reach), F32),
         )
         + work(cells // PARTS, PARTS),
     )
@@ -462,9 +502,12 @@
         flops=1 << 30,
     )
     turns = spaces // PARTS
-    full = call(
+    kept, swapped = call(
         ends_kernel,
-        shape((spaces * slots + 2 * EDGE + cells // 2, 2 * members)),
+        (
+            shape((spaces * slots, 2 * members)),
+            shape((spaces * slots // 2 + 2 * EDGE + cells // 2, 2 * members)),
+        ),
         (got, own, taps1, taps2, columns),
         scratch=tuple(
             pltpu.VMEM((turns, *value.shape), value.dtype) for value in work(2 * HALO, PARTS)
@@ -477,7 +520,7 @@
     return call(
         functools.partial(update_kernel, groups),
         (shape((members, cells)), shape((members, cells))),
-        (*from_groups(full), taps1, taps2, columns, near, near_turned, choice),
+        (kept, *from_groups(swapped), taps1, taps2, columns, near, near_turned, choice),
         scratch=(pltpu.VMEM(((order // 2 + 1) * order, 128), F32),)
         + work(cells // PARTS, PARTS)
         + (pltpu.VMEM((cells, members), F32),),

time: 37.2 us -> 36.3 us (0.976)
  local copies, waits for them, and re-layouts: 1.41 us -> 0.62 us
    unnamed x26, local copies, waits for them, and re-layouts: 1.41 us -> 0.62 us
  transfers between devices with their start and end apart: 1 -> 1, of which waited for: 1 -> 1; matrix products, arithmetic and copies ran while one was open for 0% -> 0% of each run, Pallas kernels for 2% -> 3%
where the time goes in v6:
time: 36.3 us; the launch traced here: 36.1 us
  blocking collectives  19.4 us (53%)
  Pallas kernels  14 us (39%)
  between operations  1.55 us (4%)
  local copies, waits for them, and re-layouts  0.62 us (2%)
  waiting for transfers between devices  0.46 us (1%)
    all_to_all x1, blocking collectives, on_device(): got = lax.all_to_all(sent, 'space', 0, 0)  19.4 us
    pallas_call x5, Pallas kernels, call(): pl.pallas_call(kernel, out_shape=outs, in_specs=[VMEM] * len(args), out_s...  14 us
  transfers between devices with their start and end apart: 1, of which 1 were waited for; matrix products, arithmetic and copies ran while one was open for 0% of the time, Pallas kernels for 3%

profile of v6, /device:TPU:0, one launch (start us, length us, event | category | flops | bytes accessed | tf_op | source)
XLA Modules:
  0.0 36.1 jit_solution(8019576006147024074)
XLA Ops:
  0.6 0.0 copy-start.1
  1.4 0.0 copy-start.4
  1.4 0.0 copy-start.5
  1.5 0.0 copy-start.6
  1.5 0.0 copy-done.1
  1.5 0.0 copy-done
  1.5 0.0 copy-done.3
  1.5 0.0 copy-done.2
  1.5 0.0 copy-done.7
  1.5 0.0 copy-done.8
  1.5 0.0 copy-done.9
  1.5 0.0 copy-done.10
  1.5 0.0 copy-done.11
  1.6 0.5 %copy-done.4 = f32[48]{0:T(128)S(1)} copy-done((f32[48]{0:T(128)S(1)}, f32[48]{0:T(128)}, u32[]{:S(2)}) %copy-start.4) | copy-done | bytes 216
  2.1 0.0 copy-done.5
  2.1 0.0 copy-done.6
  2.1 2.1 %shard_map.150 = (f32[128,64]{1,0:T(8,128)S(1)}, bf16[144,240]{1,0:T(8,128)(2,1)S(1)}, bf16[160,480]{1,0:T(8,128)(2,1)S(1)}, f32[5,48,128]{2,1,0:T(8,128)S(1)}, f32[16,40,128]{2,1,0:T(8,128)S(1)}) custom-call(f32[8,128]{1,0:T(8,128)S(1)} %shard_map.149.empty, f32[64,128]{1,0:T(8,128)S(1)} %copy-done.2, f32[48]{0:T(128)S(1)} %copy-done.4, f32[48]{0:T(128)S(1)} %copy-done.5, ...), custom_call_target="tpu_custom_call" | custom-call | bytes 262144 | tf_op jit(solution)/shard_map/pallas_call | solution.py:24
  4.3 19.4 %all_to_all.5.got = f32[16,40,128]{2,1,0:T(8,128)S(1)} all-to-all(f32[16,40,128]{2,1,0:T(8,128)S(1)} %get-tuple-element.12), channel_id=1, replica_groups=mesh['space'=16,'members'=2] {'space'}, dimensions={0} | all-to-all | bytes 655360 | tf_op jit(solution)/shard_map/all_to_all | solution.py:493
  23.7 2.3 %shard_map.151 = (f32[512,128]{1,0:T(8,128)S(1)}, f32[336,128]{1,0:T(8,128)S(1)}) custom-call(f32[16,40,128]{2,1,0:T(8,128)S(1)} %all_to_all.5.got, f32[128,64]{1,0:T(8,128)S(1)} %get-tuple-element.13.own, bf16[144,240]{1,0:T(8,128)(2,1)S(1)} %get-tuple-element.14.taps1.refs_3_, bf16[160,480]{1,0:T(8,128)(2,1)S(1)} %get-tuple-element.15.taps2.refs_4_, ...), custom_call_target="tpu_custom_call" | custom-call | bytes 262144 | tf_op jit(solution)/shard_map/pallas_call | solution.py:24
  26.0 0.1 collective-permute-start
  26.1 0.0 copy-done.12
  26.1 0.9 %shard_map.152 = (s32[128,128]{1,0:T(8,128)S(1)}, s32[64,128]{1,0:T(8,128)S(1)}, bf16[32,128,128]{2,1,0:T(8,128)(2,1)S(1)}) custom-call(s32[64,64]{1,0:T(8,128)S(1)} %copy-done.12), custom_call_target="tpu_custom_call" | custom-call | flops 1073741824 | bytes 262144 | tf_op jit(solution)/shard_map/pallas_call | solution.py:24
  27.0 0.5 %collective-permute-done.refs_2_ = f32[336,128]{1,0:T(8,128)S(1)} collective-permute-done((f32[336,128]{1,0:T(8,128)S(1)}, f32[336,128]{1,0:T(8,128)S(1)}, u32[]{:S(2)}, u32[]{:S(2)}) %collective-permute-start) | collective-permute-done | bytes 172064 | tf_op jit(solution)/shard_map/ppermute | solution.py:449
  27.5 8.6 %shard_map.153 = (f32[64,128]{1,0:T(8,128)}, f32[64,128]{1,0:T(8,128)}) custom-call(f32[512,128]{1,0:T(8,128)S(1)} %get-tuple-element.17.refs_0_, f32[336,128]{1,0:T(8,128)S(1)} %get-tuple-element.18.refs_1_, f32[336,128]{1,0:T(8,128)S(1)} %collective-permute-done.refs_2_, bf16[144,240]{1,0:T(8,128)(2,1)S(1)} %get-tuple-element.14.taps1.refs_3_, ...), custom_call_target="tpu_custom_call" | custom-call | bytes 262144 | tf_op jit(solution)/shard_map/pallas_call | solution.py:24
  (10 shorter events, 0.0 us)
Async XLA Ops:
  0.6 0.8 %copy-start.1 = (bf16[3,48,96]{2,1,0:T(8,128)(2,1)S(1)}, bf16[3,48,96]{2,1,0:T(8,128)(2,1)}, u32[]{:S(2)}) copy-start(bf16[3,48,96]{2,1,0:T(8,128)(2,1)} %conv2.1) | copy-start | bytes 82948
  0.6 0.8 %copy-start = (bf16[3,48,48]{2,1,0:T(8,128)(2,1)S(1)}, bf16[3,48,48]{2,1,0:T(8,128)(2,1)}, u32[]{:S(2)}) copy-start(bf16[3,48,48]{2,1,0:T(8,128)(2,1)} %conv1.1) | copy-start | bytes 41476
  0.7 0.8 %copy-start.3 = (f32[64,32]{0,1:T(8,128)S(1)}, f32[64,32]{0,1:T(8,128)}, u32[]{:S(2)}) copy-start(f32[64,32]{0,1:T(8,128)} %param.17) | copy-start | bytes 24580
  0.7 0.8 %copy-start.2 = (f32[64,128]{1,0:T(8,128)S(1)}, f32[64,128]{1,0:T(8,128)}, u32[]{:S(2)}) copy-start(f32[64,128]{1,0:T(8,128)} %field.1) | copy-start | bytes 98308
  0.7 0.8 %copy-start.7 = (f32[48]{0:T(128)S(1)}, f32[48]{0:T(128)}, u32[]{:S(2)}) copy-start(f32[48]{0:T(128)} %bias2.1) | copy-start | bytes 580
  0.7 0.8 %copy-start.8 = (bf16[144]{0:T(256)(128)(2,1)S(1)}, bf16[144]{0:T(256)(128)(2,1)}, u32[]{:S(2)}) copy-start(bf16[144]{0:T(256)(128)(2,1)} %readout.1) | copy-start | bytes 868
  0.7 0.8 %copy-start.9 = (f32[32]{0:T(128)S(1)}, f32[32]{0:T(128)}, u32[]{:S(2)}) copy-start(f32[32]{0:T(128)} %obs_heads.1) | copy-start | bytes 388
  0.7 0.8 %copy-start.10 = (f32[32]{0:T(128)S(1)}, f32[32]{0:T(128)}, u32[]{:S(2)}) copy-start(f32[32]{0:T(128)} %obs_var.1) | copy-start | bytes 388
  0.7 0.8 %copy-start.11 = (s32[1,32]{1,0:T(1,128)S(1)}, s32[1,32]{1,0:T(1,128)}, u32[]{:S(2)}) copy-start(s32[1,32]{1,0:T(1,128)} %obs_index.1) | copy-start | bytes 388
  1.4 0.7 %copy-start.4 = (f32[48]{0:T(128)S(1)}, f32[48]{0:T(128)}, u32[]{:S(2)}) copy-start(f32[48]{0:T(128)} %gain.1) | copy-start | bytes 580
  1.4 0.7 %copy-start.5 = (f32[48]{0:T(128)S(1)}, f32[48]{0:T(128)}, u32[]{:S(2)}) copy-start(f32[48]{0:T(128)} %bias.1) | copy-start | bytes 580
  1.5 0.7 %copy-start.6 = (f32[48]{0:T(128)S(1)}, f32[48]{0:T(128)}, u32[]{:S(2)}) copy-start(f32[48]{0:T(128)} %bias1.1) | copy-start | bytes 580
  23.7 2.4 %copy-start.12 = (s32[64,64]{1,0:T(8,128)S(1)}, s32[64,64]{1,0:T(8,128)}, u32[]{:S(2)}) copy-start(s32[64,64]{1,0:T(8,128)} %neighbours.1) | copy-start | bytes 49156
  26.0 1.5 %collective-permute-start = (f32[336,128]{1,0:T(8,128)S(1)}, f32[336,128]{1,0:T(8,128)S(1)}, u32[]{:S(2)}, u32[]{:S(2)}) collective-permute-start(f32[336,128]{1,0:T(8,128)S(1)} %get-tuple-element.18.refs_1_), channel_id=1, source_target_pairs={{1,0},{0,1},{3,2},{2,3},{5,4},{4,5},{7,6},{6,7},{9,8},{8,9},{11,10... | collective-permute-start | bytes 516104 | tf_op jit(solution)/shard_map/ppermute | solution.py:449

commit v7 on v6

--- a/solution.py
+++ b/solution.py
@@ -172,7 +172,8 @@
     root_row = jnp.where(live, lax.rsqrt(variance), 0.0)
     root = column(root_row)
     target = column(obs_heads[...].reshape(1, slots))
-    wanted = root * (target + jnp.sqrt(column(variance)) * noise_turned[...])
+    goal = root * target
+    noise = jnp.where(column(jnp.where(live, 1.0, 0.0)) > 0.0, noise_turned[...], 0.0)
 
     zeros = jnp.zeros((HALO, members), F32)
     wide = in_runs(jnp.concatenate([zeros, turned, zeros], axis=0))
@@ -183,18 +184,26 @@
     )
     parts = jnp.dot(chosen, split3(every), preferred_element_type=F32)
     seen = parts[:, :members] + parts[:, members : 2 * members] + parts[:, 2 * members :]
-    weighted = root * seen
-    shown = jnp.where(column(jnp.where(end_row < 0, 0.0, 1.0)) > 0.0, root, weighted)
+    gap = goal - root * seen
+    gap_high = gap.astype(BF16).astype(F32)
+    root_high = root_row.astype(BF16).astype(F32)
+    ends = jnp.concatenate([turned[: 2 * HALO], turned[cells - 2 * HALO :]], axis=1)
+    ends_high = ends.astype(BF16).astype(F32)
+    row_high = (end_row >> 6) << 6
     blank = empty[0:1, slots : 2 * members]
     payload = jnp.concatenate(
         [
-            jnp.concatenate([shown, wanted - weighted], axis=1),
-            jnp.concatenate([turned[: 2 * HALO], turned[cells - 2 * HALO :]], axis=1),
-            jnp.concatenate([end_row.astype(F32), blank], axis=1),
-            jnp.zeros((1, 2 * members), F32),
+            jnp.concatenate([gap_high, gap - gap_high], axis=1),
+            jnp.concatenate([noise[: slots // 2], noise[slots // 2 :]], axis=1),
+            ends_high,
+            jnp.concatenate([row_high.astype(F32), blank], axis=1),
+            jnp.concatenate([root_high, blank], axis=1),
+            ends - ends_high,
+            jnp.concatenate([(end_row - row_high).astype(F32), blank], axis=1),
+            jnp.concatenate([root_row - root_high, blank], axis=1),
         ],
         axis=0,
-    )
+    ).astype(BF16)
     for copy in range(sent.shape[0]):
         sent[copy] = payload
 
@@ -221,19 +230,23 @@
 
 def ends_kernel(
     got, own, taps1, taps2, columns,
-    kept, swapped, first, second, heads, ends, marks,
+    kept, swapped, first, second, heads, ends, marks, tails,
 ):
     space = lax.axis_index("space")
     spaces = got.shape[0]
-    slots = got.shape[1] - EDGE
+    slots = (got.shape[1] - 2 * EDGE) * 2 // 3
     members = got.shape[2] // 2
     inner = 2 * HALO
+    edge = slots + slots // 2
+    for tile in range(spaces):
+        pair = got[tile].astype(F32)[edge:]
+        tails[tile] = pair[:EDGE] + pair[EDGE:]
     for start in range(0, spaces, PARTS):
         sides = []
         for here in range(start, start + PARTS):
             there = (here + 1) % spaces
-            near_end = got[here, slots : slots + inner, members:]
-            far_end = got[there, slots : slots + inner, :members]
+            near_end = tails[here, :inner, members:]
+            far_end = tails[there, :inner, :members]
             sides.append(jnp.concatenate([near_end, far_end], axis=0))
         wide = jnp.concatenate(sides, axis=1)
         turn = start // PARTS
@@ -246,33 +259,23 @@
             ends[at : at + EDGE, :] = heads[turn, :, q * members : (q + 1) * members]
     for tile in range(spaces):
         at = tile * slots
-        marks[0:1, at : at + slots] = got[tile, slots + inner : slots + inner + 1, :slots]
+        marks[0:2, at : at + slots] = tails[tile, inner : inner + 2, :slots]
     row = lax.broadcasted_iota(jnp.int32, (spaces * EDGE, spaces * slots), 0).astype(F32)
-    picks = jnp.where(row == marks[0:1, :], 1.0, 0.0).astype(BF16)
-    exact = split3(ends[...])
-    exact = [exact[:, i * members : (i + 1) * members] for i in range(3)]
-    flag = jnp.ones((spaces * EDGE, 2 * members), BF16)
-    none = jnp.zeros((spaces * EDGE, 2 * members), BF16)
-    table = jnp.concatenate(
-        [
-            jnp.concatenate([part, part, flag if i == 0 else none], axis=1)
-            for i, part in enumerate(exact)
-        ],
-        axis=0,
-    )
-    parts = lax.dot_general(
-        jnp.concatenate([picks] * 3, axis=0), table, (((0,), (0,)), ((), ())),
-        preferred_element_type=F32,
+    picks = jnp.where(row == marks[0:1, :], marks[1:2, :], 0.0)
+    added = lax.dot_general(
+        picks, jnp.concatenate([ends[...]] * 2, axis=1), (((0,), (0,)), ((), ())),
+        precision=lax.Precision.HIGHEST, preferred_element_type=F32,
     )
     heads_lane = lax.broadcasted_iota(jnp.int32, (1, 2 * members), 1) < members
     half = spaces * slots // 2
 
     def finished(tile):
         at = slice(tile * slots, (tile + 1) * slots)
-        there = got[tile, :slots, :]
-        shown = jnp.where(heads_lane, there, pltpu.roll(there, members, 1))
-        seen, marked = parts[at, : 2 * members], parts[at, 2 * members :]
-        return jnp.where(heads_lane, shown * (1.0 - marked + seen), there - shown * seen)
+        there = got[tile].astype(F32)
+        gap = there[:slots] + pltpu.roll(there[:slots], members, 1) - added[at]
+        noise = there[slots:edge]
+        noise = jnp.concatenate([pltpu.roll(noise, members, 1), noise], axis=0)
+        return jnp.where(heads_lane, gap, gap + noise)
 
     for tile in range(spaces // 2):
         at = slice(tile * slots, (tile + 1) * slots)
@@ -282,8 +285,8 @@
         swapped[at, :] = jnp.where(heads_lane, one, pltpu.roll(two, members, 1))
     before = jnp.where(space == 0, spaces - 1, space - 1)
     after = jnp.where(space == spaces - 1, 0, space + 1)
-    swapped[half : half + EDGE, :] = got[before, slots:, :]
-    swapped[half + EDGE : half + 2 * EDGE, :] = got[after, slots:, :]
+    swapped[half : half + EDGE, :] = tails[before]
+    swapped[half + EDGE : half + 2 * EDGE, :] = tails[after]
     middle = own.shape[0] // 2
     swapped[half + 2 * EDGE :, :] = jnp.concatenate([own[:middle, :], own[middle:, :]], axis=1)
 
@@ -332,7 +335,7 @@
         precision=lax.Precision.HIGHEST, preferred_element_type=F32,
     )
     gram = split3(product[:everyone])
-    sides = product[everyone:]
+    sides = -product[everyone:]
 
     ids = near[...]
     lane_id = lax.broadcasted_iota(jnp.int32, (128, 128), 1)
@@ -478,7 +481,7 @@
             shape((BAND * channels, reach), BF16),
             shape((BAND * channels + 16, 2 * reach), BF16),
             shape((5, channels, 128)),
-            shape((spaces, slots + EDGE, 2 * members)),
+            shape((spaces, slots + slots // 2 + 2 * EDGE, 2 * members), BF16),
         ),
         (
             empty, log_field, lift_gain, lift_bias, conv_first, bias_first, conv_second, bias_second,
@@ -515,6 +518,7 @@
         + (
             pltpu.VMEM((spaces * EDGE, members), F32),
             pltpu.VMEM((8, spaces * slots), F32),
+            pltpu.VMEM((spaces, EDGE, 2 * members), F32),
         ),
     )
     return call(

time: 36.3 us -> 34.9 us (0.961)
  blocking collectives: 19.4 us -> 18 us
    all_to_all x1, blocking collectives: 19.4 us -> 18 us  [on_device(): got = lax.all_to_all(sent, 'space', 0, 0)]
where the time goes in v7:
time: 34.9 us; the launch traced here: 34.6 us
  blocking collectives  18 us (52%)
  Pallas kernels  14 us (40%)
  between operations  1.54 us (4%)
  local copies, waits for them, and re-layouts  0.62 us (2%)
  waiting for transfers between devices  0.46 us (1%)
    all_to_all x1, blocking collectives, on_device(): got = lax.all_to_all(sent, 'space', 0, 0)  18 us
    pallas_call x5, Pallas kernels, call(): pl.pallas_call(kernel, out_shape=outs, in_specs=[VMEM] * len(args), out_s...  14 us
  transfers between devices with their start and end apart: 1, of which 1 were waited for; matrix products, arithmetic and copies ran while one was open for 0% of the time, Pallas kernels for 3%

profile of v7, /device:TPU:0, one launch (start us, length us, event | category | flops | bytes accessed | tf_op | source)
XLA Modules:
  0.0 34.6 jit_solution(2285955566659421227)
XLA Ops:
  0.6 0.0 copy-start.1
  1.4 0.0 copy-start.4
  1.4 0.0 copy-start.5
  1.5 0.0 copy-start.6
  1.5 0.0 copy-done.1
  1.5 0.0 copy-done
  1.5 0.0 copy-done.3
  1.5 0.0 copy-done.2
  1.5 0.0 copy-done.7
  1.5 0.0 copy-done.8
  1.5 0.0 copy-done.9
  1.5 0.0 copy-done.10
  1.5 0.0 copy-done.11
  1.6 0.5 %copy-done.4 = f32[48]{0:T(128)S(1)} copy-done((f32[48]{0:T(128)S(1)}, f32[48]{0:T(128)}, u32[]{:S(2)}) %copy-start.4) | copy-done | bytes 216
  2.1 0.0 copy-done.5
  2.1 0.0 copy-done.6
  2.1 2.1 %shard_map.150 = (f32[128,64]{1,0:T(8,128)S(1)}, bf16[144,240]{1,0:T(8,128)(2,1)S(1)}, bf16[160,480]{1,0:T(8,128)(2,1)S(1)}, f32[5,48,128]{2,1,0:T(8,128)S(1)}, bf16[16,64,128]{2,1,0:T(8,128)(2,1)S(1)}) custom-call(f32[8,128]{1,0:T(8,128)S(1)} %shard_map.149.empty, f32[64,128]{1,0:T(8,128)S(1)} %copy-done.2, f32[48]{0:T(128)S(1)} %copy-done.4, ...), custom_call_target="tpu_custom_call" | custom-call | bytes 262144 | tf_op jit(solution)/shard_map/pallas_call | solution.py:24
  4.3 18.0 %all_to_all.5.got = bf16[16,64,128]{2,1,0:T(8,128)(2,1)S(1)} all-to-all(bf16[16,64,128]{2,1,0:T(8,128)(2,1)S(1)} %get-tuple-element.12), channel_id=1, replica_groups=mesh['space'=16,'members'=2] {'space'}, dimensions={0} | all-to-all | bytes 524288 | tf_op jit(solution)/shard_map/all_to_all | solution.py:496
  22.3 2.3 %shard_map.151 = (f32[512,128]{1,0:T(8,128)S(1)}, f32[336,128]{1,0:T(8,128)S(1)}) custom-call(bf16[16,64,128]{2,1,0:T(8,128)(2,1)S(1)} %all_to_all.5.got, f32[128,64]{1,0:T(8,128)S(1)} %get-tuple-element.13.own, bf16[144,240]{1,0:T(8,128)(2,1)S(1)} %get-tuple-element.14.taps1.refs_3_, bf16[160,480]{1,0:T(8,128)(2,1)S(1)} %get-tuple-element.15.taps2.refs_4_, ...), custom_call_target="tpu_custom_call" | custom-call | bytes 262144 | tf_op jit(solution)/shard_map/pallas_call | solution.py:24
  24.6 0.1 collective-permute-start
  24.7 0.0 copy-done.12
  24.7 0.9 %shard_map.152 = (s32[128,128]{1,0:T(8,128)S(1)}, s32[64,128]{1,0:T(8,128)S(1)}, bf16[32,128,128]{2,1,0:T(8,128)(2,1)S(1)}) custom-call(s32[64,64]{1,0:T(8,128)S(1)} %copy-done.12), custom_call_target="tpu_custom_call" | custom-call | flops 1073741824 | bytes 262144 | tf_op jit(solution)/shard_map/pallas_call | solution.py:24
  25.6 0.5 %collective-permute-done.refs_2_ = f32[336,128]{1,0:T(8,128)S(1)} collective-permute-done((f32[336,128]{1,0:T(8,128)S(1)}, f32[336,128]{1,0:T(8,128)S(1)}, u32[]{:S(2)}, u32[]{:S(2)}) %collective-permute-start) | collective-permute-done | bytes 172064 | tf_op jit(solution)/shard_map/ppermute | solution.py:452
  26.0 8.6 %shard_map.153 = (f32[64,128]{1,0:T(8,128)}, f32[64,128]{1,0:T(8,128)}) custom-call(f32[512,128]{1,0:T(8,128)S(1)} %get-tuple-element.17.refs_0_, f32[336,128]{1,0:T(8,128)S(1)} %get-tuple-element.18.refs_1_, f32[336,128]{1,0:T(8,128)S(1)} %collective-permute-done.refs_2_, bf16[144,240]{1,0:T(8,128)(2,1)S(1)} %get-tuple-element.14.taps1.refs_3_, ...), custom_call_target="tpu_custom_call" | custom-call | bytes 262144 | tf_op jit(solution)/shard_map/pallas_call | solution.py:24
  (10 shorter events, 0.0 us)
Async XLA Ops:
  0.6 0.8 %copy-start.1 = (bf16[3,48,96]{2,1,0:T(8,128)(2,1)S(1)}, bf16[3,48,96]{2,1,0:T(8,128)(2,1)}, u32[]{:S(2)}) copy-start(bf16[3,48,96]{2,1,0:T(8,128)(2,1)} %conv2.1) | copy-start | bytes 82948
  0.6 0.8 %copy-start = (bf16[3,48,48]{2,1,0:T(8,128)(2,1)S(1)}, bf16[3,48,48]{2,1,0:T(8,128)(2,1)}, u32[]{:S(2)}) copy-start(bf16[3,48,48]{2,1,0:T(8,128)(2,1)} %conv1.1) | copy-start | bytes 41476
  0.7 0.8 %copy-start.3 = (f32[64,32]{0,1:T(8,128)S(1)}, f32[64,32]{0,1:T(8,128)}, u32[]{:S(2)}) copy-start(f32[64,32]{0,1:T(8,128)} %param.17) | copy-start | bytes 24580
  0.7 0.8 %copy-start.2 = (f32[64,128]{1,0:T(8,128)S(1)}, f32[64,128]{1,0:T(8,128)}, u32[]{:S(2)}) copy-start(f32[64,128]{1,0:T(8,128)} %field.1) | copy-start | bytes 98308
  0.7 0.8 %copy-start.7 = (f32[48]{0:T(128)S(1)}, f32[48]{0:T(128)}, u32[]{:S(2)}) copy-start(f32[48]{0:T(128)} %bias2.1) | copy-start | bytes 580
  0.7 0.8 %copy-start.8 = (bf16[144]{0:T(256)(128)(2,1)S(1)}, bf16[144]{0:T(256)(128)(2,1)}, u32[]{:S(2)}) copy-start(bf16[144]{0:T(256)(128)(2,1)} %readout.1) | copy-start | bytes 868
  0.7 0.8 %copy-start.9 = (f32[32]{0:T(128)S(1)}, f32[32]{0:T(128)}, u32[]{:S(2)}) copy-start(f32[32]{0:T(128)} %obs_heads.1) | copy-start | bytes 388
  0.7 0.8 %copy-start.10 = (f32[32]{0:T(128)S(1)}, f32[32]{0:T(128)}, u32[]{:S(2)}) copy-start(f32[32]{0:T(128)} %obs_var.1) | copy-start | bytes 388
  0.7 0.8 %copy-start.11 = (s32[1,32]{1,0:T(1,128)S(1)}, s32[1,32]{1,0:T(1,128)}, u32[]{:S(2)}) copy-start(s32[1,32]{1,0:T(1,128)} %obs_index.1) | copy-start | bytes 388
  1.4 0.7 %copy-start.4 = (f32[48]{0:T(128)S(1)}, f32[48]{0:T(128)}, u32[]{:S(2)}) copy-start(f32[48]{0:T(128)} %gain.1) | copy-start | bytes 580
  1.4 0.7 %copy-start.5 = (f32[48]{0:T(128)S(1)}, f32[48]{0:T(128)}, u32[]{:S(2)}) copy-start(f32[48]{0:T(128)} %bias.1) | copy-start | bytes 580
  1.5 0.7 %copy-start.6 = (f32[48]{0:T(128)S(1)}, f32[48]{0:T(128)}, u32[]{:S(2)}) copy-start(f32[48]{0:T(128)} %bias1.1) | copy-start | bytes 580
  22.3 2.4 %copy-start.12 = (s32[64,64]{1,0:T(8,128)S(1)}, s32[64,64]{1,0:T(8,128)}, u32[]{:S(2)}) copy-start(s32[64,64]{1,0:T(8,128)} %neighbours.1) | copy-start | bytes 49156
  24.6 1.5 %collective-permute-start = (f32[336,128]{1,0:T(8,128)S(1)}, f32[336,128]{1,0:T(8,128)S(1)}, u32[]{:S(2)}, u32[]{:S(2)}) collective-permute-start(f32[336,128]{1,0:T(8,128)S(1)} %get-tuple-element.18.refs_1_), channel_id=1, source_target_pairs={{1,0},{0,1},{3,2},{2,3},{5,4},{4,5},{7,6},{6,7},{9,8},{8,9},{11,10... | collective-permute-start | bytes 516104 | tf_op jit(solution)/shard_map/ppermute | solution.py:452

commit v8 on v7

--- a/solution.py
+++ b/solution.py
@@ -241,6 +241,7 @@
     for tile in range(spaces):
         pair = got[tile].astype(F32)[edge:]
         tails[tile] = pair[:EDGE] + pair[EDGE:]
+    ends[...] = jnp.zeros_like(ends)
     for start in range(0, spaces, PARTS):
         sides = []
         for here in range(start, start + PARTS):
@@ -256,7 +257,7 @@
         )
         for q in range(PARTS):
             at = (start + q) * EDGE
-            ends[at : at + EDGE, :] = heads[turn, :, q * members : (q + 1) * members]
+            ends[at : at + inner, :] = heads[turn, :inner, q * members : (q + 1) * members]
     for tile in range(spaces):
         at = tile * slots
         marks[0:2, at : at + slots] = tails[tile, inner : inner + 2, :slots]

time: 34.9 us -> 34.9 us (level)
  no operation moved by 1% of the time
where the time goes in v8:
time: 34.9 us; the launch traced here: 34.6 us
  blocking collectives  18 us (52%)
  Pallas kernels  14 us (40%)
  between operations  1.54 us (4%)
  local copies, waits for them, and re-layouts  0.62 us (2%)
  waiting for transfers between devices  0.46 us (1%)
    all_to_all x1, blocking collectives, on_device(): got = lax.all_to_all(sent, 'space', 0, 0)  18 us
    pallas_call x5, Pallas kernels, call(): pl.pallas_call(kernel, out_shape=outs, in_specs=[VMEM] * len(args), out_s...  14 us
  transfers between devices with their start and end apart: 1, of which 1 were waited for; matrix products, arithmetic and copies ran while one was open for 0% of the time, Pallas kernels for 3%

profile of v8, /device:TPU:0, one launch (start us, length us, event | category | flops | bytes accessed | tf_op | source)
XLA Modules:
  0.0 34.6 jit_solution(3503107567330905575)
XLA Ops:
  0.6 0.0 copy-start.1
  1.4 0.0 copy-start.4
  1.4 0.0 copy-start.5
  1.5 0.0 copy-start.6
  1.5 0.0 copy-done.1
  1.5 0.0 copy-done
  1.5 0.0 copy-done.3
  1.5 0.0 copy-done.2
  1.5 0.0 copy-done.7
  1.5 0.0 copy-done.8
  1.5 0.0 copy-done.9
  1.5 0.0 copy-done.10
  1.5 0.0 copy-done.11
  1.6 0.5 %copy-done.4 = f32[48]{0:T(128)S(1)} copy-done((f32[48]{0:T(128)S(1)}, f32[48]{0:T(128)}, u32[]{:S(2)}) %copy-start.4) | copy-done | bytes 216
  2.1 0.0 copy-done.5
  2.1 0.0 copy-done.6
  2.1 2.1 %shard_map.150 = (f32[128,64]{1,0:T(8,128)S(1)}, bf16[144,240]{1,0:T(8,128)(2,1)S(1)}, bf16[160,480]{1,0:T(8,128)(2,1)S(1)}, f32[5,48,128]{2,1,0:T(8,128)S(1)}, bf16[16,64,128]{2,1,0:T(8,128)(2,1)S(1)}) custom-call(f32[8,128]{1,0:T(8,128)S(1)} %shard_map.149.empty, f32[64,128]{1,0:T(8,128)S(1)} %copy-done.2, f32[48]{0:T(128)S(1)} %copy-done.4, ...), custom_call_target="tpu_custom_call" | custom-call | bytes 262144 | tf_op jit(solution)/shard_map/pallas_call | solution.py:24
  4.3 18.0 %all_to_all.5.got = bf16[16,64,128]{2,1,0:T(8,128)(2,1)S(1)} all-to-all(bf16[16,64,128]{2,1,0:T(8,128)(2,1)S(1)} %get-tuple-element.12), channel_id=1, replica_groups=mesh['space'=16,'members'=2] {'space'}, dimensions={0} | all-to-all | bytes 524288 | tf_op jit(solution)/shard_map/all_to_all | solution.py:497
  22.3 2.3 %shard_map.151 = (f32[512,128]{1,0:T(8,128)S(1)}, f32[336,128]{1,0:T(8,128)S(1)}) custom-call(bf16[16,64,128]{2,1,0:T(8,128)(2,1)S(1)} %all_to_all.5.got, f32[128,64]{1,0:T(8,128)S(1)} %get-tuple-element.13.own, bf16[144,240]{1,0:T(8,128)(2,1)S(1)} %get-tuple-element.14.taps1.refs_3_, bf16[160,480]{1,0:T(8,128)(2,1)S(1)} %get-tuple-element.15.taps2.refs_4_, ...), custom_call_target="tpu_custom_call" | custom-call | bytes 262144 | tf_op jit(solution)/shard_map/pallas_call | solution.py:24
  24.6 0.1 collective-permute-start
  24.6 0.0 copy-done.12
  24.7 0.9 %shard_map.152 = (s32[128,128]{1,0:T(8,128)S(1)}, s32[64,128]{1,0:T(8,128)S(1)}, bf16[32,128,128]{2,1,0:T(8,128)(2,1)S(1)}) custom-call(s32[64,64]{1,0:T(8,128)S(1)} %copy-done.12), custom_call_target="tpu_custom_call" | custom-call | flops 1073741824 | bytes 262144 | tf_op jit(solution)/shard_map/pallas_call | solution.py:24
  25.6 0.5 %collective-permute-done.refs_2_ = f32[336,128]{1,0:T(8,128)S(1)} collective-permute-done((f32[336,128]{1,0:T(8,128)S(1)}, f32[336,128]{1,0:T(8,128)S(1)}, u32[]{:S(2)}, u32[]{:S(2)}) %collective-permute-start) | collective-permute-done | bytes 172064 | tf_op jit(solution)/shard_map/ppermute | solution.py:453
  26.0 8.6 %shard_map.153 = (f32[64,128]{1,0:T(8,128)}, f32[64,128]{1,0:T(8,128)}) custom-call(f32[512,128]{1,0:T(8,128)S(1)} %get-tuple-element.17.refs_0_, f32[336,128]{1,0:T(8,128)S(1)} %get-tuple-element.18.refs_1_, f32[336,128]{1,0:T(8,128)S(1)} %collective-permute-done.refs_2_, bf16[144,240]{1,0:T(8,128)(2,1)S(1)} %get-tuple-element.14.taps1.refs_3_, ...), custom_call_target="tpu_custom_call" | custom-call | bytes 262144 | tf_op jit(solution)/shard_map/pallas_call | solution.py:24
  (10 shorter events, 0.0 us)
Async XLA Ops:
  0.6 0.8 %copy-start.1 = (bf16[3,48,96]{2,1,0:T(8,128)(2,1)S(1)}, bf16[3,48,96]{2,1,0:T(8,128)(2,1)}, u32[]{:S(2)}) copy-start(bf16[3,48,96]{2,1,0:T(8,128)(2,1)} %conv2.1) | copy-start | bytes 82948
  0.6 0.8 %copy-start = (bf16[3,48,48]{2,1,0:T(8,128)(2,1)S(1)}, bf16[3,48,48]{2,1,0:T(8,128)(2,1)}, u32[]{:S(2)}) copy-start(bf16[3,48,48]{2,1,0:T(8,128)(2,1)} %conv1.1) | copy-start | bytes 41476
  0.7 0.8 %copy-start.3 = (f32[64,32]{0,1:T(8,128)S(1)}, f32[64,32]{0,1:T(8,128)}, u32[]{:S(2)}) copy-start(f32[64,32]{0,1:T(8,128)} %param.17) | copy-start | bytes 24580
  0.7 0.8 %copy-start.2 = (f32[64,128]{1,0:T(8,128)S(1)}, f32[64,128]{1,0:T(8,128)}, u32[]{:S(2)}) copy-start(f32[64,128]{1,0:T(8,128)} %field.1) | copy-start | bytes 98308
  0.7 0.8 %copy-start.7 = (f32[48]{0:T(128)S(1)}, f32[48]{0:T(128)}, u32[]{:S(2)}) copy-start(f32[48]{0:T(128)} %bias2.1) | copy-start | bytes 580
  0.7 0.8 %copy-start.8 = (bf16[144]{0:T(256)(128)(2,1)S(1)}, bf16[144]{0:T(256)(128)(2,1)}, u32[]{:S(2)}) copy-start(bf16[144]{0:T(256)(128)(2,1)} %readout.1) | copy-start | bytes 868
  0.7 0.8 %copy-start.9 = (f32[32]{0:T(128)S(1)}, f32[32]{0:T(128)}, u32[]{:S(2)}) copy-start(f32[32]{0:T(128)} %obs_heads.1) | copy-start | bytes 388
  0.7 0.8 %copy-start.10 = (f32[32]{0:T(128)S(1)}, f32[32]{0:T(128)}, u32[]{:S(2)}) copy-start(f32[32]{0:T(128)} %obs_var.1) | copy-start | bytes 388
  0.7 0.8 %copy-start.11 = (s32[1,32]{1,0:T(1,128)S(1)}, s32[1,32]{1,0:T(1,128)}, u32[]{:S(2)}) copy-start(s32[1,32]{1,0:T(1,128)} %obs_index.1) | copy-start | bytes 388
  1.4 0.7 %copy-start.4 = (f32[48]{0:T(128)S(1)}, f32[48]{0:T(128)}, u32[]{:S(2)}) copy-start(f32[48]{0:T(128)} %gain.1) | copy-start | bytes 580
  1.4 0.7 %copy-start.5 = (f32[48]{0:T(128)S(1)}, f32[48]{0:T(128)}, u32[]{:S(2)}) copy-start(f32[48]{0:T(128)} %bias.1) | copy-start | bytes 580
  1.5 0.7 %copy-start.6 = (f32[48]{0:T(128)S(1)}, f32[48]{0:T(128)}, u32[]{:S(2)}) copy-start(f32[48]{0:T(128)} %bias1.1) | copy-start | bytes 580
  22.3 2.4 %copy-start.12 = (s32[64,64]{1,0:T(8,128)S(1)}, s32[64,64]{1,0:T(8,128)}, u32[]{:S(2)}) copy-start(s32[64,64]{1,0:T(8,128)} %neighbours.1) | copy-start | bytes 49156
  24.6 1.5 %collective-permute-start = (f32[336,128]{1,0:T(8,128)S(1)}, f32[336,128]{1,0:T(8,128)S(1)}, u32[]{:S(2)}, u32[]{:S(2)}) collective-permute-start(f32[336,128]{1,0:T(8,128)S(1)} %get-tuple-element.18.refs_1_), channel_id=1, source_target_pairs={{1,0},{0,1},{3,2},{2,3},{5,4},{4,5},{7,6},{6,7},{9,8},{8,9},{11,10... | collective-permute-start | bytes 516104 | tf_op jit(solution)/shard_map/ppermute | solution.py:453

commit v9 on v8

--- a/solution.py
+++ b/solution.py
@@ -336,6 +336,9 @@
         precision=lax.Precision.HIGHEST, preferred_element_type=F32,
     )
     gram = split3(product[:everyone])
+    gram = jnp.concatenate(
+        [gram[:, i * everyone : (i + 1) * everyone] for i in range(3)], axis=0
+    )
     sides = -product[everyone:]
 
     ids = near[...]
@@ -345,11 +348,9 @@
     def extract(quad, carry):
         found = []
         for b in range(2):
-            parts = jnp.dot(choice[2 * quad + b], gram, preferred_element_type=F32)
-            rows = (
-                parts[:, :everyone]
-                + parts[:, everyone : 2 * everyone]
-                + parts[:, 2 * everyone :]
+            one_hot = choice[2 * quad + b]
+            rows = jnp.dot(
+                jnp.concatenate([one_hot] * 3, axis=1), gram, preferred_element_type=F32
             )
             found.append(lane_gather(rows, ids))
         block = jnp.where(half_lane, found[0], found[1]).T

time: 34.9 us -> 34.9 us (level)
  no operation moved by 1% of the time
where the time goes in v9:
time: 34.9 us; the launch traced here: 34.6 us
  blocking collectives  18 us (52%)
  Pallas kernels  14 us (40%)
  between operations  1.54 us (4%)
  local copies, waits for them, and re-layouts  0.62 us (2%)
  waiting for transfers between devices  0.46 us (1%)
    all_to_all x1, blocking collectives, on_device(): got = lax.all_to_all(sent, 'space', 0, 0)  18 us
    pallas_call x5, Pallas kernels, call(): pl.pallas_call(kernel, out_shape=outs, in_specs=[VMEM] * len(args), out_s...  14 us
  transfers between devices with their start and end apart: 1, of which 1 were waited for; matrix products, arithmetic and copies ran while one was open for 0% of the time, Pallas kernels for 3%

profile of v9, /device:TPU:0, one launch (start us, length us, event | category | flops | bytes accessed | tf_op | source)
XLA Modules:
  0.0 34.6 jit_solution(12520266746597857292)
XLA Ops:
  0.6 0.0 copy-start.1
  0.6 0.0 copy-start
  1.4 0.0 copy-start.4
  1.4 0.0 copy-start.5
  1.5 0.0 copy-start.6
  1.5 0.0 copy-done.1
  1.5 0.0 copy-done
  1.5 0.0 copy-done.3
  1.5 0.0 copy-done.2
  1.5 0.0 copy-done.7
  1.5 0.0 copy-done.8
  1.5 0.0 copy-done.9
  1.5 0.0 copy-done.10
  1.5 0.0 copy-done.11
  1.6 0.5 %copy-done.4 = f32[48]{0:T(128)S(1)} copy-done((f32[48]{0:T(128)S(1)}, f32[48]{0:T(128)}, u32[]{:S(2)}) %copy-start.4) | copy-done | bytes 216
  2.1 0.0 copy-done.5
  2.1 0.0 copy-done.6
  2.1 2.1 %shard_map.150 = (f32[128,64]{1,0:T(8,128)S(1)}, bf16[144,240]{1,0:T(8,128)(2,1)S(1)}, bf16[160,480]{1,0:T(8,128)(2,1)S(1)}, f32[5,48,128]{2,1,0:T(8,128)S(1)}, bf16[16,64,128]{2,1,0:T(8,128)(2,1)S(1)}) custom-call(f32[8,128]{1,0:T(8,128)S(1)} %shard_map.149.empty, f32[64,128]{1,0:T(8,128)S(1)} %copy-done.2, f32[48]{0:T(128)S(1)} %copy-done.4, ...), custom_call_target="tpu_custom_call" | custom-call | bytes 262144 | tf_op jit(solution)/shard_map/pallas_call | solution.py:24
  4.3 18.0 %all_to_all.5.got = bf16[16,64,128]{2,1,0:T(8,128)(2,1)S(1)} all-to-all(bf16[16,64,128]{2,1,0:T(8,128)(2,1)S(1)} %get-tuple-element.12), channel_id=1, replica_groups=mesh['space'=16,'members'=2] {'space'}, dimensions={0} | all-to-all | bytes 524288 | tf_op jit(solution)/shard_map/all_to_all | solution.py:498
  22.3 2.3 %shard_map.151 = (f32[512,128]{1,0:T(8,128)S(1)}, f32[336,128]{1,0:T(8,128)S(1)}) custom-call(bf16[16,64,128]{2,1,0:T(8,128)(2,1)S(1)} %all_to_all.5.got, f32[128,64]{1,0:T(8,128)S(1)} %get-tuple-element.13.own, bf16[144,240]{1,0:T(8,128)(2,1)S(1)} %get-tuple-element.14.taps1.refs_3_, bf16[160,480]{1,0:T(8,128)(2,1)S(1)} %get-tuple-element.15.taps2.refs_4_, ...), custom_call_target="tpu_custom_call" | custom-call | bytes 262144 | tf_op jit(solution)/shard_map/pallas_call | solution.py:24
  24.6 0.1 collective-permute-start
  24.7 0.9 %shard_map.152 = (s32[128,128]{1,0:T(8,128)S(1)}, s32[64,128]{1,0:T(8,128)S(1)}, bf16[32,128,128]{2,1,0:T(8,128)(2,1)S(1)}) custom-call(s32[64,64]{1,0:T(8,128)S(1)} %copy-done.12), custom_call_target="tpu_custom_call" | custom-call | flops 1073741824 | bytes 262144 | tf_op jit(solution)/shard_map/pallas_call | solution.py:24
  25.6 0.5 %collective-permute-done.refs_2_ = f32[336,128]{1,0:T(8,128)S(1)} collective-permute-done((f32[336,128]{1,0:T(8,128)S(1)}, f32[336,128]{1,0:T(8,128)S(1)}, u32[]{:S(2)}, u32[]{:S(2)}) %collective-permute-start) | collective-permute-done | bytes 172064 | tf_op jit(solution)/shard_map/ppermute | solution.py:454
  26.0 8.6 %shard_map.153 = (f32[64,128]{1,0:T(8,128)}, f32[64,128]{1,0:T(8,128)}) custom-call(f32[512,128]{1,0:T(8,128)S(1)} %get-tuple-element.17.refs_0_, f32[336,128]{1,0:T(8,128)S(1)} %get-tuple-element.18.refs_1_, f32[336,128]{1,0:T(8,128)S(1)} %collective-permute-done.refs_2_, bf16[144,240]{1,0:T(8,128)(2,1)S(1)} %get-tuple-element.14.taps1.refs_3_, ...), custom_call_target="tpu_custom_call" | custom-call | bytes 262144 | tf_op jit(solution)/shard_map/pallas_call | solution.py:24
  (10 shorter events, 0.0 us)
Async XLA Ops:
  0.6 0.8 %copy-start.1 = (bf16[3,48,96]{2,1,0:T(8,128)(2,1)S(1)}, bf16[3,48,96]{2,1,0:T(8,128)(2,1)}, u32[]{:S(2)}) copy-start(bf16[3,48,96]{2,1,0:T(8,128)(2,1)} %conv2.1) | copy-start | bytes 82948
  0.6 0.8 %copy-start = (bf16[3,48,48]{2,1,0:T(8,128)(2,1)S(1)}, bf16[3,48,48]{2,1,0:T(8,128)(2,1)}, u32[]{:S(2)}) copy-start(bf16[3,48,48]{2,1,0:T(8,128)(2,1)} %conv1.1) | copy-start | bytes 41476
  0.7 0.8 %copy-start.3 = (f32[64,32]{0,1:T(8,128)S(1)}, f32[64,32]{0,1:T(8,128)}, u32[]{:S(2)}) copy-start(f32[64,32]{0,1:T(8,128)} %param.17) | copy-start | bytes 24580
  0.7 0.8 %copy-start.2 = (f32[64,128]{1,0:T(8,128)S(1)}, f32[64,128]{1,0:T(8,128)}, u32[]{:S(2)}) copy-start(f32[64,128]{1,0:T(8,128)} %field.1) | copy-start | bytes 98308
  0.7 0.8 %copy-start.7 = (f32[48]{0:T(128)S(1)}, f32[48]{0:T(128)}, u32[]{:S(2)}) copy-start(f32[48]{0:T(128)} %bias2.1) | copy-start | bytes 580
  0.7 0.8 %copy-start.8 = (bf16[144]{0:T(256)(128)(2,1)S(1)}, bf16[144]{0:T(256)(128)(2,1)}, u32[]{:S(2)}) copy-start(bf16[144]{0:T(256)(128)(2,1)} %readout.1) | copy-start | bytes 868
  0.7 0.8 %copy-start.9 = (f32[32]{0:T(128)S(1)}, f32[32]{0:T(128)}, u32[]{:S(2)}) copy-start(f32[32]{0:T(128)} %obs_heads.1) | copy-start | bytes 388
  0.7 0.8 %copy-start.10 = (f32[32]{0:T(128)S(1)}, f32[32]{0:T(128)}, u32[]{:S(2)}) copy-start(f32[32]{0:T(128)} %obs_var.1) | copy-start | bytes 388
  0.7 0.8 %copy-start.11 = (s32[1,32]{1,0:T(1,128)S(1)}, s32[1,32]{1,0:T(1,128)}, u32[]{:S(2)}) copy-start(s32[1,32]{1,0:T(1,128)} %obs_index.1) | copy-start | bytes 388
  1.4 0.7 %copy-start.4 = (f32[48]{0:T(128)S(1)}, f32[48]{0:T(128)}, u32[]{:S(2)}) copy-start(f32[48]{0:T(128)} %gain.1) | copy-start | bytes 580
  1.4 0.7 %copy-start.5 = (f32[48]{0:T(128)S(1)}, f32[48]{0:T(128)}, u32[]{:S(2)}) copy-start(f32[48]{0:T(128)} %bias.1) | copy-start | bytes 580
  1.5 0.7 %copy-start.6 = (f32[48]{0:T(128)S(1)}, f32[48]{0:T(128)}, u32[]{:S(2)}) copy-start(f32[48]{0:T(128)} %bias1.1) | copy-start | bytes 580
  22.3 2.4 %copy-start.12 = (s32[64,64]{1,0:T(8,128)S(1)}, s32[64,64]{1,0:T(8,128)}, u32[]{:S(2)}) copy-start(s32[64,64]{1,0:T(8,128)} %neighbours.1) | copy-start | bytes 49156
  24.6 1.5 %collective-permute-start = (f32[336,128]{1,0:T(8,128)S(1)}, f32[336,128]{1,0:T(8,128)S(1)}, u32[]{:S(2)}, u32[]{:S(2)}) collective-permute-start(f32[336,128]{1,0:T(8,128)S(1)} %get-tuple-element.18.refs_1_), channel_id=1, source_target_pairs={{1,0},{0,1},{3,2},{2,3},{5,4},{4,5},{7,6},{6,7},{9,8},{8,9},{11,10... | collective-permute-start | bytes 516104 | tf_op jit(solution)/shard_map/ppermute | solution.py:454
